TPU v7x, 256 devices: a whole 4x4x8 slice. The times are simulated.
256 devices in a mesh: shower: 8 (over x, core), seq: 32 (over y, z).
Axes of the slice: x: 4, y: 4, z: 8, core: 2. Of those that a mesh axis runs over, the one named last changes fastest.
Arguments:
- ssm_input: bfloat16 [8, 8192, 2048], P('shower', 'seq'), may hold values from -6 to 6
- gate_input: bfloat16 [8, 8192, 2048], P('shower', 'seq'), may hold values from -6 to 6
- state_input: bfloat16 [8, 8192, 128], P('shower', 'seq'), may hold values from -6 to 6
- state_output: bfloat16 [8, 8192, 128], P('shower', 'seq'), may hold values from -0.52734375 to 0.52734375
- log_decay: float32 [8, 8192, 16], P('shower', 'seq'), may hold values from -1 to 0, as said below
- norm_gain: float32 [2048], replicated, may hold values from 0.1 to 1.9
- out_weight: bfloat16 [1024, 2048], P(None, ('shower', 'seq')), may hold values from -0.125 to 0.125
- grad_output: bfloat16 [8, 8192, 1024], P('shower', 'seq'), may hold values from -6 to 6
Outputs:
- grad_input: bfloat16 [8, 8192, 2048], P('shower', 'seq')
- grad_gate: bfloat16 [8, 8192, 2048], P('shower', 'seq')
- grad_state_in: bfloat16 [8, 8192, 128], P('shower', 'seq')
- grad_state_out: bfloat16 [8, 8192, 128], P('shower', 'seq')
- grad_log_decay: float32 [8, 8192, 16], P('shower', 'seq')
- grad_out_weight: float32 [1024, 2048], P(('shower', 'seq'))
- grad_norm_gain: float32 [2048], P(('shower', 'seq'))
Inputs may be any that keep to these rules, and one draw needn't show every extreme that they name: `log_decay`: negative per-step log decays.
All inputs are finite; a program needn't handle non-finite values.
Results may differ from a plain program's by a relative error of at most 0.022.
Values may be sent and summed in bfloat16 or wider, within the bound.
No kernel may reach another device: no remote copies, remote signals or barrier semaphores. Data moves between devices by JAX's collectives and lax.ppermute only.
A program may use at most 128 MiB of HBM per device.

v0:
```python
import jax
import jax.numpy as jnp
from jax import lax
from jax.sharding import PartitionSpec as P

GROUP = 256


def carried_in(value, axis, combine, identity, reverse):
    peers, position = (lax.axis_size(axis), lax.axis_index(axis))
    everything = jax.tree.map(lambda part: lax.all_gather(part, axis), value)
    start = jax.tree.map(
        lambda part, zero: jnp.broadcast_to(jnp.asarray(zero, part.dtype), part.shape),
        value,
        identity,
    )

    def turn(k, before):
        at = peers - 1 - k if reverse else k
        reached = at > position if reverse else at < position
        new = combine(before, jax.tree.map(lambda part: part[at], everything))
        return jax.tree.map(lambda a, b: jnp.where(reached, a, b), new, before)

    return lax.fori_loop(0, peers, turn, start)


def decay_table(cum_decay):
    along = jnp.swapaxes(cum_decay, 1, 2)
    differ = along[:, :, :, None] - along[:, :, None, :]
    size = cum_decay.shape[1]
    row_index = lax.broadcasted_iota(jnp.int32, (size, size), 0)
    col_index = lax.broadcasted_iota(jnp.int32, (size, size), 1)
    causal = (row_index >= col_index)[None, None]
    return jnp.where(causal, jnp.exp(jnp.where(causal, differ, 0.0)), 0.0)


def chain_combine(earlier, later):
    return (earlier[0] + later[0], jnp.exp(later[0])[:, None, None] * earlier[1] + later[1])


def add_sums(earlier, later):
    return earlier + later


def local_chain(totals, terms, backward):

    def advance(carry, item):
        return (jnp.exp(item[0])[:, None, None] * carry + item[1], carry)

    return lax.scan(advance, jnp.zeros_like(terms[0]), (totals, terms), reverse=backward)


def body(
    ssm_input, gate_input, state_input, state_output, log_decay, norm_gain, out_weight, grad_output
):
    length_dev = ssm_input.shape[1]
    heads = log_decay.shape[2]
    head_size = ssm_input.shape[2] // heads
    width = state_input.shape[2]
    groups = length_dev // GROUP
    x_heads = ssm_input[0].reshape(groups, GROUP, heads, head_size)
    b_rows = state_input[0].reshape(groups, GROUP, width)
    c_rows = state_output[0].reshape(groups, GROUP, width)
    cum_decay = jnp.cumsum(log_decay[0].reshape(groups, GROUP, heads), axis=1)
    group_total = cum_decay[:, -1]
    scores = jnp.einsum("ctn,csn->cts", c_rows, b_rows, preferred_element_type=jnp.float32)
    kernel = (scores[:, None] * decay_table(cum_decay)).astype(jnp.bfloat16)
    keep_start = jnp.exp(cum_decay)
    keep_end = jnp.exp(group_total[:, None, :] - cum_decay)
    x_end = (x_heads * keep_end[..., None]).astype(jnp.bfloat16)
    group_state = jnp.einsum("cshp,csn->chpn", x_end, b_rows, preferred_element_type=jnp.float32)
    inner_part = jnp.einsum("chts,cshp->cthp", kernel, x_heads, preferred_element_type=jnp.float32)
    own_state, local_before = local_chain(group_total, group_state, False)
    own_total = jnp.sum(group_total, axis=0)
    empty_state = (jnp.zeros_like(own_total), jnp.zeros_like(own_state))
    _, state_in = carried_in((own_total, own_state), "seq", chain_combine, empty_state, False)
    before_total = jnp.cumsum(group_total, axis=0) - group_total
    entering = jnp.exp(before_total)[:, :, None, None] * state_in[None] + local_before
    entering_bf = entering.astype(jnp.bfloat16)
    carried = jnp.einsum("chpn,ctn->cthp", entering_bf, c_rows, preferred_element_type=jnp.float32)
    output_y = inner_part + keep_start[..., None] * carried
    output_flat = output_y.reshape(length_dev, heads * head_size)
    grad_rows = grad_output[0]
    grad_normed = jnp.dot(
        grad_rows,
        lax.all_gather(out_weight, ("shower", "seq"), axis=1, tiled=True),
        preferred_element_type=jnp.float32,
    )
    gate_float = gate_input[0].astype(jnp.float32)
    sigmoid_gate = jax.nn.sigmoid(gate_float)
    active = gate_float * sigmoid_gate
    pre_norm = output_flat * active
    inv_rms = lax.rsqrt(jnp.mean(pre_norm * pre_norm, axis=-1, keepdims=True) + 1e-05)
    normed = (pre_norm * inv_rms * norm_gain).astype(jnp.bfloat16)
    scaled = norm_gain * grad_normed
    grad_pre = inv_rms * scaled - pre_norm * (inv_rms * inv_rms * inv_rms) * jnp.mean(
        scaled * pre_norm, axis=-1, keepdims=True
    )
    grad_y = grad_pre * active
    grad_gate = (
        grad_pre * output_flat * sigmoid_gate * (1.0 + gate_float * (1.0 - sigmoid_gate))
    ).astype(jnp.bfloat16)
    gain_term = jnp.sum(grad_normed * pre_norm * inv_rms, axis=0)
    weight_term = jnp.einsum("td,ti->di", grad_rows, normed, preferred_element_type=jnp.float32)
    grad_heads = grad_y.reshape(groups, GROUP, heads, head_size)
    grad_bf = grad_heads.astype(jnp.bfloat16)
    grad_start = (grad_heads * keep_start[..., None]).astype(jnp.bfloat16)
    grad_group = jnp.einsum(
        "cthp,ctn->chpn", grad_start, c_rows, preferred_element_type=jnp.float32
    )
    own_grad, local_after = local_chain(group_total, grad_group, True)
    grad_inner = jnp.einsum("chts,cthp->cshp", kernel, grad_bf, preferred_element_type=jnp.float32)
    pair_scores = jnp.einsum(
        "cthp,cshp->chts", grad_bf, x_heads, preferred_element_type=jnp.float32
    )
    pair_weights = (pair_scores * decay_table(cum_decay)).astype(jnp.bfloat16)
    grad_c_inner = jnp.einsum(
        "chts,csn->ctn", pair_weights, b_rows, preferred_element_type=jnp.float32
    )
    grad_b_inner = jnp.einsum(
        "chts,ctn->csn", pair_weights, c_rows, preferred_element_type=jnp.float32
    )
    _, grad_in = carried_in((own_total, own_grad), "seq", chain_combine, empty_state, True)
    after_total = jnp.flip(jnp.cumsum(jnp.flip(group_total, 0), axis=0), 0) - group_total
    leaving = jnp.exp(after_total)[:, :, None, None] * grad_in[None] + local_after
    leaving_bf = leaving.astype(jnp.bfloat16)
    grad_xf = grad_inner + keep_end[..., None] * jnp.einsum(
        "chpn,csn->cshp", leaving_bf, b_rows, preferred_element_type=jnp.float32
    )
    grad_c = grad_c_inner + jnp.einsum(
        "cthp,chpn->ctn", grad_start, entering_bf, preferred_element_type=jnp.float32
    )
    grad_b = grad_b_inner + jnp.einsum(
        "cshp,chpn->csn", x_end, leaving_bf, preferred_element_type=jnp.float32
    )
    rate_term = jnp.sum(grad_heads * output_y, axis=-1) - jnp.sum(x_heads * grad_xf, axis=-1)
    rate_flat = rate_term.reshape(length_dev, heads)
    suffix = jnp.flip(jnp.cumsum(jnp.flip(rate_flat, 0), axis=0), 0)
    own_rate = jnp.sum(rate_flat, axis=0)
    tail_sum = carried_in(own_rate, "seq", add_sums, jnp.zeros_like(own_rate), True)
    grad_log_decay = suffix + tail_sum[None, :]
    weight_sum, gain_sum = (
        lax.psum_scatter(weight_term, ("shower", "seq"), scatter_dimension=0, tiled=True),
        lax.psum_scatter(gain_term, ("shower", "seq"), scatter_dimension=0, tiled=True),
    )
    grad_input = grad_xf.reshape(length_dev, heads * head_size).astype(jnp.bfloat16)
    grad_state_in = grad_b.reshape(length_dev, width).astype(jnp.bfloat16)
    grad_state_out = grad_c.reshape(length_dev, width).astype(jnp.bfloat16)
    return (
        grad_input[None],
        grad_gate[None],
        grad_state_in[None],
        grad_state_out[None],
        grad_log_decay[None],
        weight_sum,
        gain_sum,
    )


def solution(mesh):
    in_specs = (
        P("shower", "seq", None),
        P("shower", "seq", None),
        P("shower", "seq", None),
        P("shower", "seq", None),
        P("shower", "seq", None),
        P(),
        P(None, ("shower", "seq")),
        P("shower", "seq", None),
    )
    out_specs = (
        P("shower", "seq", None),
        P("shower", "seq", None),
        P("shower", "seq", None),
        P("shower", "seq", None),
        P("shower", "seq", None),
        P(("shower", "seq"), None),
        P(("shower", "seq")),
    )
    return jax.shard_map(body, mesh=mesh, in_specs=in_specs, out_specs=out_specs, check_vma=False)
```

profile of v0, /device:TPU:38, one launch (start us, length us, event | category | flops | bytes accessed | tf_op | source)
XLA Modules:
  0.0 1036.7 jit_solution(12176705346648678810)
XLA Ops:
  10.9 3.0 copy.93
  19.5 40.3 %all-gather = f32[32,1,16]{2,1,0:T(1,128)S(1)} all-gather(f32[1,1,16]{2,1,0:T(1,128)S(1)} %copy.91), channel_id=2, replica_groups=mesh['shower'=8,'seq'=32] {'seq'}, dimensions={0}, use_global_device_ids=true | all-gather | bytes 2112 | tf_op jit(solution)/shard_map/all_gather | solution.py:11
  61.2 2.6 copy.96
  65.3 3.0 copy.99
  68.3 3.0 fusion.9
  71.3 181.5 %all-gather.10.cloned.1.call-done = f32[512,128,128]{2,1,0:T(8,128)} async-done(((f32[16,128,128]{2,1,0:T(8,128)}), f32[512,128,128]{2,1,0:T(8,128)}) %all-gather.10.cloned.1.call-update) | async-done | bytes 33554448 | tf_op jit(solution)/shard_map/all_gather | solution.py:11
  252.8 48.0 %while.56 = (s32[]{:T(128)}, f32[16,128,128]{2,1,0:T(8,128)S(1)}, s32[]{:T(128)}, f32[32,16]{1,0:T(8,128)S(1)}, f32[32,16,128,128]{3,2,1,0:T(8,128)}, /*index=5*/s32[]{:T(128)}, s32[]{:T(128)}) while((s32[]{:T(128)}, f32[16,128,128]{2,1,0:T(8,128)S(1)}, s32[]{:T(128)}, f32[32,16]{1,0:T(8,128)S(1)}, f32[32,16,128,128]{3,2,1,0:T(8,128)}, ...), condition=%wide.region_3.4_spmd.clone, body=%wide.region_2.3_spmd.clone.sunk | while | flops 1048580 | bytes 3146025 | solution.py:24
  300.8 5.1 multiply_reduce_fusion.4
  305.8 3.0 copy.97
  308.9 60.6 %all-gather.8.cloned.1.call-done = bf16[1024,2048]{0,1:T(8,128)(2,1)} async-done(((bf16[1024,8]{0,1:T(8,128)(2,1)}), bf16[1024,2048]{0,1:T(8,128)(2,1)}) %all-gather.8.cloned.1.call-update) | async-done | bytes 4194320 | tf_op jit(solution)/shard_map/all_gather | solution.py:86
  369.6 5.0 multiply_reduce_fusion
  374.6 2.9 fusion.15
  377.4 3.3 copy.107
  380.8 3.4 multiply_convert_fusion.2
  384.2 4.4 convolution_bitcast_fusion
  390.3 2.6 copy.108
  394.1 76.0 %all-reduce.2 = f32[2048]{0:T(1024)S(1)} all-reduce(f32[2048]{0:T(1024)S(1)} %get-tuple-element.485), channel_id=7, replica_groups=mesh['shower'=8,'seq'=32] {'shower','seq'}, use_global_device_ids=true, to_apply=%region_18.19.clone | all-reduce | flops 2048 | bytes 16384
  472.5 3.0 convert_reduce_fusion
  476.3 2.8 fusion.8
  479.1 184.7 %all-reduce.5.cloned.1.call-done = f32[1024,2048]{0,1:T(8,128)} async-done(((f32[1024,2048]{0,1:T(8,128)}), f32[1024,2048]{0,1:T(8,128)}) %all-reduce.5.cloned.1.call-update) | async-done | bytes 8388624
  666.3 233.6 %all-gather.12.cloned.1.call-done = f32[512,128,128]{2,1,0:T(8,128)} async-done(((f32[16,128,128]{2,1,0:T(8,128)}), f32[512,128,128]{2,1,0:T(8,128)}) %all-gather.12.cloned.1.call-update) | async-done | bytes 33554448 | tf_op jit(solution)/shard_map/all_gather | solution.py:11
  899.9 48.5 %while.57 = (s32[]{:T(128)}, f32[16,128,128]{2,1,0:T(8,128)S(1)}, s32[]{:T(128)}, f32[32,16]{1,0:T(8,128)S(1)}, f32[32,16,128,128]{3,2,1,0:T(8,128)}, /*index=5*/s32[]{:T(128)}, s32[]{:T(128)}, s32[]{:T(128)}, s32[]{:T(128)}) while((s32[]{:T(128)}, f32[16,128,128]{2,1,0:T(8,128)S(1)}, s32[]{:T(128)}, f32[32,16]{1,0:T(8,128)S(1)}, ...), condition=%wide.region_7.8_spmd.clone, body=%wide.region_6.7_spmd.clone.sunk | while | flops 1048584 | bytes 3146087 | solution.py:24
  950.0 2.2 multiply_reduce_fusion.1
  953.7 71.9 %all-reduce = f32[512]{0:T(512)S(1)} all-reduce(f32[512]{0:T(512)S(1)} %dynamic-update-slice), channel_id=5, replica_groups=mesh['shower'=8,'seq'=32] {'seq'}, use_global_device_ids=true, to_apply=%add | all-reduce | flops 512 | bytes 4096
  (254 shorter events, 122.3 us)
Async XLA Ops:
  7.2 362.4 %copy-start = (bf16[1,256,1024]{2,1,0:T(8,128)(2,1)S(1)}, bf16[1,256,1024]{2,1,0:T(8,128)(2,1)}, u32[]{:S(2)}) copy-start(bf16[1,256,1024]{2,1,0:T(8,128)(2,1)} %param.21) | copy-start | bytes 1572868
  7.2 245.6 %all-gather.10.cloned.1.call-start = ((), (), s32[]{:S(2)}) async-start(), calls=%async_computation.1 | async-start | bytes 34603008 | tf_op jit(solution)/shard_map/all_gather | solution.py:11
  10.9 3.0 copy-start.4
  15.8 1.2 copy-start.11
  16.0 1.0 copy-start.2
  18.5 42.5 %copy-start.13 = (bf16[1,256,128]{2,1,0:T(8,128)(2,1)S(1)}, bf16[1,256,128]{2,1,0:T(8,128)(2,1)}, u32[]{:S(2)}) copy-start(bf16[1,256,128]{2,1,0:T(8,128)(2,1)} %param.17) | copy-start | bytes 196612
  18.6 351.0 %all-gather.8.cloned.1.call-start = ((), (), s32[]{:S(2)}) async-start(), calls=%async_computation | async-start | bytes 4210688 | tf_op jit(solution)/shard_map/all_gather | solution.py:86
  19.3 644.5 %all-reduce.5.cloned.1.call-start = ((), (), s32[]{:S(2)}) async-start(), calls=%async_computation.3 | async-start | bytes 16777216
  65.3 3.0 copy-start.12
  305.8 63.7 %copy-start.9 = (bf16[1,256,2048]{2,1,0:T(8,128)(2,1)S(1)}, bf16[1,256,2048]{2,1,0:T(8,128)(2,1)}, u32[]{:S(2)}) copy-start(bf16[1,256,2048]{2,1,0:T(8,128)(2,1)} %param.15) | copy-start | bytes 3145732
  305.8 63.7 %copy-start.14 = (f32[2048]{0:T(1024)S(1)}, f32[2048]{0:T(1024)}, u32[]{:S(2)}) copy-start(f32[2048]{0:T(1024)} %param.19) | copy-start | bytes 24580
  369.5 5.0 copy-start.7
  369.5 5.0 copy-start.8
  369.5 5.0 copy-start.10
  377.4 11.3 %copy-start.1 = (bf16[32,16,8,128]{3,2,1,0:T(8,128)(2,1)}, bf16[32,16,8,128]{3,2,1,0:T(8,128)(2,1)S(1)}, u32[]{:S(2)}) copy-start(bf16[32,16,8,128]{3,2,1,0:T(8,128)(2,1)S(1)} %get-tuple-element.517) | copy-start | bytes 3145732
  388.7 511.2 %all-gather.12.cloned.1.call-start = ((), (), s32[]{:S(2)}) async-start(), calls=%async_computation.2 | async-start | bytes 34603008 | tf_op jit(solution)/shard_map/all_gather | solution.py:11
  390.2 2.7 copy-start.15
  470.1 2.4 copy-start.6
  899.9 48.5 %copy-start.3 = (bf16[32,8,16,128]{3,2,1,0:T(8,128)(2,1)S(1)}, bf16[32,8,16,128]{3,2,1,0:T(8,128)(2,1)}, u32[]{:S(2)}) copy-start(bf16[32,8,16,128]{3,2,1,0:T(8,128)(2,1)} %copy-done.2) | copy-start | bytes 3145732
  948.4 1.6 copy-start.5
Sparse Core Ops, SparseCore 0:
  18.7 234.0 all-gather.9
  256.6 112.8 all-gather.7
  388.8 274.9 all-reduce.4
  667.1 232.7 all-gather.11
where the time goes:
time: 1040 us
  waiting for transfers between devices  661 us (64%)
  blocking collectives  188 us (18%)
  other arithmetic  105 us (10%)
  matrix products  32.5 us (3%)
  local copies, waits for them, and re-layouts  32.1 us (3%)
  between operations  14.7 us (1%)
    all_gather x2, waiting for transfers between devices, carried_in(): everything = jax.tree.map(lambda part: lax.all_gather(part, axis), value)  415 us
    unnamed x5, waiting for transfers between devices  185 us
    unnamed x2, blocking collectives  148 us
    select_n x96, other arithmetic, turn(): return jax.tree.map(lambda a, b: jnp.where(reached, a, b), new, before)  94.1 us
    all_gather x1, waiting for transfers between devices, body(): lax.all_gather(out_weight, ('shower', 'seq'), axis=1, tiled=True)  60.6 us
    all_gather x1, blocking collectives, carried_in(): everything = jax.tree.map(lambda part: lax.all_gather(part, axis), value)  40.3 us
  transfers between devices with their start and end apart: 4, of which 4 were waited for; matrix products, arithmetic and copies ran while one was open for 8% of the time, Pallas kernels for 0%

commit v1 on v0

v1 whole, which is shorter than its diff:
```python
import functools

import jax
import jax.numpy as jnp
from jax import lax
from jax.experimental import pallas as pl
from jax.experimental.pallas import tpu as pltpu
from jax.sharding import Mesh
from jax.sharding import PartitionSpec as P

F32, BF16 = jnp.float32, jnp.bfloat16
T = 256
H = 16
W = 128
INNER = H * W
D = 1024
SEQ = 32
HALF = 64
EXTRA = 16
GAINROWS = 16
SEQ_AXES = ("y", "z")
FAR = -1e30
HI = lax.Precision.HIGHEST


def lane(h, width=W):
    return pl.ds(pl.multiple_of(h * width, width), width)


def dot(a, b, ca=1, cb=0, precision=None):
    return lax.dot_general(
        a, b, (((ca,), (cb,)), ((), ())), precision=precision, preferred_element_type=F32
    )


def iota(shape, axis):
    return lax.broadcasted_iota(jnp.int32, shape, axis)


def row_sum(a):
    return jnp.sum(a, axis=1, keepdims=True)


def pair_cols(ref, h):
    return jnp.concatenate([ref[2 * h], ref[2 * h + 1]], axis=1)


def pair_state(ref, h):
    blocks = ref[pl.ds(4 * h, 4)]
    first = blocks[0:2].reshape(W, W)
    second = blocks[2:4].reshape(W, W)
    return jnp.concatenate([first, second], axis=1)


def split_state(ref, h, value):
    ref[pl.ds(4 * h, 2), 0:HALF, :] = value[:, :W].reshape(2, HALF, W)
    ref[pl.ds(4 * h + 2, 2), 0:HALF, :] = value[:, W:].reshape(2, HALF, W)


def state_kernel(x_ref, b_ref, decay_ref, send_ref, state_ref, col_ref, row_ref, end_ref):
    tri = (iota((T, T), 0) >= iota((T, T), 1)).astype(F32)
    decay = decay_ref[...]
    cum = dot(tri, decay, precision=HI)
    row_ref[...] = dot(decay, tri, 0, 1, precision=HI)
    for h in range(H):
        col_ref[h] = jnp.broadcast_to(cum[:, h : h + 1], (T, W))
    b = b_ref[...]

    @pl.loop(0, H // 2)
    def _(h):
        col = pair_cols(col_ref, h)
        total = col[T - 1 : T, :]
        cols = lane(h, 2 * W)
        x_end = (x_ref[:, cols].astype(F32) * jnp.exp(total - col)).astype(BF16)
        end_ref[:, cols] = x_end
        state = dot(b, x_end, 0, 0)
        state_ref[:, cols] = state
        split_state(send_ref, h, state.astype(BF16))
        high = total.astype(BF16).astype(F32)
        middle = (total - high).astype(BF16).astype(F32)
        low = total - high - middle
        at = iota((EXTRA, 2 * W), 0)
        rows = jnp.where(at == 0, high, jnp.where(at == 1, middle, jnp.where(at == 2, low, 0.0)))
        rows = rows.astype(BF16)
        for k in range(4):
            half = rows[:, :W] if k < 2 else rows[:, W:]
            send_ref[4 * h + k, HALF : HALF + EXTRA, :] = half


def forward_scan_kernel(got_ref, out_ref, factor_ref):
    def step(j, carry):
        out_ref[j] = carry.astype(BF16)
        tail = got_ref[j, HALF : HALF + EXTRA, :].astype(F32)
        factor = jnp.exp(jnp.sum(tail, axis=0, keepdims=True))
        factor_ref[pl.ds(j, 1), :] = factor
        return factor * carry + got_ref[j, 0:HALF, :].astype(F32)

    lax.fori_loop(0, SEQ, step, jnp.zeros((HALF, W), F32))


def backward_scan_kernel(got_ref, factor_ref, out_ref):
    def step(k, carry):
        j = SEQ - 1 - k
        out_ref[j] = carry.astype(BF16)
        return factor_ref[pl.ds(j, 1), :] * carry + got_ref[j].astype(F32)

    lax.fori_loop(0, SEQ, step, jnp.zeros((HALF, W), F32))


def inner_kernel(x_ref, b_ref, c_ref, col_ref, row_ref, inner_ref):
    scores = dot(c_ref[...], b_ref[...], 1, 1)
    causal = iota((T, T), 0) >= iota((T, T), 1)

    @pl.loop(0, H)
    def _(h):
        col = col_ref[h]
        differ = jnp.concatenate([col, col], axis=1) - row_ref[pl.ds(h, 1), :]
        kernel = (scores * jnp.exp(jnp.where(causal, differ, FAR))).astype(BF16)
        inner_ref[:, lane(h)] = dot(kernel, x_ref[:, lane(h)])


def normed_grad_kernel(at_ref, grad_ref, *refs):
    *pieces, out_ref = refs
    grad = grad_ref[...]
    x, c = at_ref[0], at_ref[1]
    for core in range(2):
        for k in range(4):
            source = lax.rem(x + 4 - k, 4) * 2 + (c if core == 0 else 1 - c)
            out_ref[:, lane(source, 2 * W)] = dot(grad, pieces[core * 4 + k][...], 1, 1)


def norm_kernel(
    inner_ref, gn_ref, gate_ref, enter_ref, c_ref, col_ref, gain_ref,
    gate_out, grad_out, start_out, normed_out, send_ref, gain_out, rate_out, y_ref, u_ref,
):
    c = c_ref[...]

    def first(h, sums):
        squares, mixed = sums
        cols = lane(h, 2 * W)
        keep = jnp.exp(pair_cols(col_ref, h))
        y = inner_ref[:, cols] + keep * dot(c, pair_state(enter_ref, h))
        gate = gate_ref[:, cols].astype(F32)
        u = y * (gate * jax.nn.sigmoid(gate))
        y_ref[:, cols] = y
        u_ref[:, cols] = u
        both = gain_ref[:, cols] * gn_ref[:, cols] * u
        squared = u * u
        return (
            squares + squared[:, :W] + squared[:, W:],
            mixed + both[:, :W] + both[:, W:],
        )

    zero = jnp.zeros((T, W), F32)
    squares, mixed = lax.fori_loop(0, H // 2, first, (zero, zero))
    rstd = lax.rsqrt(row_sum(squares) / INNER + 1e-5)
    pull = rstd * rstd * rstd * (row_sum(mixed) / INNER)
    rate_out[...] = zero

    @pl.loop(0, H // 2)
    def _(h):
        cols = lane(h, 2 * W)
        y, u, gn = y_ref[:, cols], u_ref[:, cols], gn_ref[:, cols]
        gain = gain_ref[:, cols]
        gate = gate_ref[:, cols].astype(F32)
        sig = jax.nn.sigmoid(gate)
        normal = u * rstd
        grad_u = rstd * (gain * gn) - u * pull
        grad_y = grad_u * (gate * sig)
        gate_out[:, cols] = (grad_u * y * sig * (1.0 + gate * (1.0 - sig))).astype(BF16)
        normed_out[:, cols] = (normal * gain).astype(BF16)
        gain_out[:, cols] = jnp.sum(gn * normal, axis=0, keepdims=True)
        grad_out[:, cols] = grad_y.astype(BF16)
        start = (grad_y * jnp.exp(pair_cols(col_ref, h))).astype(BF16)
        start_out[:, cols] = start
        rate = grad_y * y
        at = iota((T, W), 1)
        rates = rate_out[...]
        rates = jnp.where(at == 2 * h, row_sum(rate[:, :W]), rates)
        rate_out[...] = jnp.where(at == 2 * h + 1, row_sum(rate[:, W:]), rates)
        split_state(send_ref, h, dot(c, start, 0, 0).astype(BF16))


def weight_kernel(at_ref, grad_ref, normed_ref, gain_ref, *outs):
    x, c = at_ref[0], at_ref[1]
    normed = normed_ref[...]
    for core in range(2):
        for k in range(4):
            block = lax.rem(x + k, 4) * 2 + (c if core == 0 else 1 - c)
            out = outs[core * 4 + k]
            out[0:W, :] = dot(grad_ref[:, lane(block)], normed, 0, 0).astype(BF16)
            gain = jnp.broadcast_to(gain_ref[:, lane(block, 2 * W)], (GAINROWS, 2 * W))
            out[W : W + GAINROWS, :] = jnp.zeros((GAINROWS, INNER), BF16)
            out[W : W + GAINROWS, 0 : 2 * W] = gain.astype(BF16)


def pair_kernel(
    x_ref, grad_ref, start_ref, b_ref, c_ref, col_ref, row_ref, enter_ref,
    inner_ref, grad_c_ref, grad_b_ref, sum_ref,
):
    b, c = b_ref[...], c_ref[...]
    scores = dot(b, c, 1, 1)
    causal = iota((T, T), 0) <= iota((T, T), 1)
    sum_ref[...] = jnp.zeros((T, T), F32)

    @pl.loop(0, H)
    def _(h):
        col = col_ref[h]
        differ = row_ref[pl.ds(h, 1), :] - jnp.concatenate([col, col], axis=1)
        table = jnp.exp(jnp.where(causal, differ, FAR))
        grad = grad_ref[:, lane(h)]
        inner_ref[:, lane(h)] = dot((scores * table).astype(BF16), grad)
        sum_ref[...] += dot(x_ref[:, lane(h)], grad, 1, 1) * table

    weights = sum_ref[...].astype(BF16)
    grad_b_ref[...] = dot(weights, c)

    def carried(h, total):
        return total + dot(start_ref[:, lane(h, 2 * W)], pair_state(enter_ref, h), 1, 1)

    grad_c_ref[...] = lax.fori_loop(0, H // 2, carried, dot(weights, b, 0, 0)).astype(BF16)


def last_kernel(
    inner_ref, leave_ref, b_ref, x_ref, end_ref, col_ref, grad_b_in, rate_ref, state_ref, enter_ref,
    grad_x_ref, grad_b_ref, decay_ref,
):
    b = b_ref[...]

    def step(h, carry):
        grad_b, rates, tail = carry
        cols = lane(h, 2 * W)
        leave = pair_state(leave_ref, h)
        col = pair_cols(col_ref, h)
        total = col[T - 1 : T, :]
        grad_x = inner_ref[:, cols] + jnp.exp(total - col) * dot(b, leave)
        grad_x_ref[:, cols] = grad_x.astype(BF16)
        rate = x_ref[:, cols].astype(F32) * grad_x
        at = iota((T, W), 1)
        rates = rates - jnp.where(at == 2 * h, row_sum(rate[:, :W]), 0.0)
        rates = rates - jnp.where(at == 2 * h + 1, row_sum(rate[:, W:]), 0.0)
        later = jnp.exp(total) * pair_state(enter_ref, h).astype(F32) + state_ref[:, cols]
        flow = jnp.sum(later * leave.astype(F32), axis=0, keepdims=True)
        at = iota((1, W), 1)
        tail = tail + jnp.where(at == 2 * h, row_sum(flow[:, :W]), 0.0)
        tail = tail + jnp.where(at == 2 * h + 1, row_sum(flow[:, W:]), 0.0)
        return grad_b + dot(end_ref[:, cols], leave, 1, 1), rates, tail

    start = (grad_b_in[...], rate_ref[...], jnp.zeros((1, W), F32))
    grad_b, rates, tail = lax.fori_loop(0, H // 2, step, start)
    grad_b_ref[...] = grad_b.astype(BF16)
    upper = (iota((T, T), 0) <= iota((T, T), 1)).astype(F32)
    decay_ref[...] = (dot(upper, rates, precision=HI) + tail)[:, :H]


def call(kernel, outs, args, scratch=(), smem=0, flops=0, cells=0):
    specs = [
        pl.BlockSpec(memory_space=pltpu.SMEM if i < smem else pltpu.VMEM) for i in range(len(args))
    ]
    moved = sum(a.size * a.dtype.itemsize for a in (*args, *outs))
    return pl.pallas_call(
        kernel,
        out_shape=outs,
        in_specs=specs,
        out_specs=[pl.BlockSpec(memory_space=pltpu.VMEM)] * len(outs),
        scratch_shapes=scratch,
        compiler_params=pltpu.CompilerParams(vmem_limit_bytes=48 * 2**20),
        cost_estimate=pl.CostEstimate(flops=flops, bytes_accessed=moved, transcendentals=cells),
    )(*args)


def shaped(shape, dtype=F32):
    return jax.ShapeDtypeStruct(shape, dtype)


def shift(value, axis, by):
    size = lax.axis_size(axis)
    return lax.ppermute(value, axis, [(i, (i + by) % size) for i in range(size)])


def gathered(value, axis):
    size, me = lax.axis_size(axis), lax.axis_index(axis)
    pieces = [shift(value, axis, k) if k else value for k in range(size - 1, -1, -1)]
    rows = value.shape[0]
    twice = jnp.concatenate(pieces + pieces, axis=0)
    return lax.dynamic_slice_in_dim(twice, lax.rem(2 * size - me - 1, size) * rows, size * rows, 0)


def exchange(value):
    return lax.all_to_all(value, SEQ_AXES, 0, 0, tiled=True)


def body(ssm, gate, state_in, state_out, log_decay, gain, out_weight, grad_rows):
    x, b, c = ssm[0], state_in[0], state_out[0]
    gate, grad_rows, gain_row = gate[0], grad_rows[0], gain[None]
    at = jnp.stack([lax.axis_index("x"), lax.axis_index("c")]).astype(jnp.int32)
    wide = shaped((T, INNER))
    wide_bf = shaped((T, INNER), BF16)
    states = shaped((SEQ, HALF, W), BF16)

    send, state, col, row, x_end = call(
        state_kernel,
        [shaped((SEQ, HALF + EXTRA, W), BF16), shaped((W, INNER)), shaped((H, T, W)), shaped((H, T)), wide_bf],
        [x, b, log_decay[0]],
        flops=2 * T * W * INNER,
        cells=T * INNER,
    )
    got = exchange(send)

    own = gathered(gathered(out_weight.T, "z"), "y")
    along = [own] + [shift(own, "x", k) for k in (1, 2, 3)]
    across = [shift(piece, "c", 1) for piece in along]

    [inner] = call(
        inner_kernel, [wide], [x, b, c, col, row], flops=2 * T * T * INNER, cells=T * T * H
    )
    enter_part, factor = call(forward_scan_kernel, [states, shaped((SEQ, W))], [got])
    enter = exchange(enter_part)
    [grad_normed] = call(
        normed_grad_kernel, [wide], [at, grad_rows, *along, *across], smem=1, flops=2 * T * D * INNER
    )
    grad_gate, grad_y, grad_start, normed, grad_send, gain_term, rate = call(
        norm_kernel,
        [wide_bf, wide_bf, wide_bf, wide_bf, states, shaped((1, INNER)), shaped((T, W))],
        [inner, grad_normed, gate, enter, c, col, gain_row],
        scratch=[pltpu.VMEM((T, INNER), F32), pltpu.VMEM((T, INNER), F32)],
        flops=4 * T * W * INNER,
        cells=4 * T * INNER,
    )
    grad_got = exchange(grad_send)
    terms = call(
        weight_kernel,
        [shaped((W + GAINROWS, INNER), BF16)] * 8,
        [at, grad_rows, normed, gain_term],
        smem=1,
        flops=2 * T * D * INNER,
    )
    halves = [
        terms[k].astype(F32) + shift(terms[4 + k], "c", 1).astype(F32) for k in range(4)
    ]
    quarter = halves[0] + sum(
        shift(halves[k].astype(BF16), "x", k).astype(F32) for k in (1, 2, 3)
    )
    grad_inner, grad_state_out, grad_b = call(
        pair_kernel,
        [wide, shaped((T, W), BF16), shaped((T, W))],
        [x, grad_y, grad_start, b, c, col, row, enter],
        scratch=[pltpu.VMEM((T, T), F32)],
        flops=5 * T * T * INNER,
        cells=T * T * H,
    )
    [leave_part] = call(backward_scan_kernel, [states], [grad_got, factor])
    leave = exchange(leave_part)
    rows = quarter[:W].astype(BF16).reshape(SEQ, HALF, W)
    gains = jnp.pad(quarter[W, : 2 * W].astype(BF16).reshape(SEQ, 1, 8), ((0, 0), (0, 7), (0, W - 8)))
    final = jnp.sum(exchange(jnp.concatenate([rows, gains], axis=1)).astype(F32), axis=0)
    grad_input, grad_state_in, grad_log_decay = call(
        last_kernel,
        [wide_bf, shaped((T, W), BF16), shaped((T, H))],
        [grad_inner, leave, b, x, x_end, col, grad_b, rate, state, enter],
        flops=4 * T * W * INNER,
        cells=T * INNER,
    )
    return (
        grad_input[None],
        grad_gate[None],
        grad_state_in[None],
        grad_state_out[None],
        grad_log_decay[None],
        final[:HALF].reshape(4, INNER),
        final[HALF, :8],
    )


def solution(mesh):
    split = Mesh(mesh.devices.reshape(4, 2, 4, 8), ("x", "c", "y", "z"))
    shower, seq = ("x", "c"), ("y", "z")
    rows = P(shower, seq, None)
    every = (*shower, *seq)
    return jax.shard_map(
        body,
        mesh=split,
        in_specs=(rows, rows, rows, rows, rows, P(), P(None, every), rows),
        out_specs=(rows, rows, rows, rows, rows, P(every, None), P(every)),
        check_vma=False,
    )
```

time: 1040 us -> 195 us (0.19)
  waiting for transfers between devices: 661 us -> 38.9 us
  blocking collectives: 188 us -> 0 us
  other arithmetic: 105 us -> 8.17 us
  starting transfers between devices: 0.16 us -> 79.6 us
  Pallas kernels: 0 us -> 41.3 us
  matrix products: 32.5 us -> 0 us
  between operations: 14.7 us -> 1.06 us
    all_gather x3 -> x0, waiting for transfers between devices: 476 us -> none  [the longest x2 415 us: carried_in(): everything = jax.tree.map(lambda part: lax.all_gather(part, axis), value)]
    unnamed x5 -> x0, waiting for transfers between devices: 185 us -> none
    unnamed x2 -> x0, blocking collectives: 148 us -> none
    select_n x96 -> x0, other arithmetic: 94.1 us -> none  [turn(): return jax.tree.map(lambda a, b: jnp.where(reached, a, b), new, before)]
    all_to_all x0 -> x5, starting transfers between devices: none -> 43.3 us  [exchange(): return lax.all_to_all(value, SEQ_AXES, 0, 0, tiled=True)]
    pallas_call x0 -> x9, Pallas kernels: none -> 41.3 us  [call(): pl.pallas_call(kernel, out_shape=outs, in_specs=specs, out_specs=[pl.Bloc...]
    all_gather x1 -> x0, blocking collectives: 40.3 us -> none  [carried_in(): everything = jax.tree.map(lambda part: lax.all_gather(part, axis), value)]
    ppermute x0 -> x24, starting transfers between devices: none -> 36.3 us  [shift(): lax.ppermute(value, axis, [(i, (i + by) % size) for i in range(size)])]
  transfers between devices with their start and end apart: 4 -> 29, of which waited for: 4 -> 11; matrix products, arithmetic and copies ran while one was open for 8% -> 7% of each run, Pallas kernels for 0% -> 15%
where the time goes in v1:
time: 195 us; the launch traced here: 194 us
  starting transfers between devices  79.6 us (41%)
  Pallas kernels  41.3 us (21%)
  waiting for transfers between devices  38.9 us (20%)
  local copies, waits for them, and re-layouts  25 us (13%)
  other arithmetic  8.17 us (4%)
    all_to_all x5, starting transfers between devices, exchange(): return lax.all_to_all(value, SEQ_AXES, 0, 0, tiled=True)  43.3 us
    pallas_call x9, Pallas kernels, call(): pl.pallas_call(kernel, out_shape=outs, in_specs=specs, out_specs=[pl.Bloc...  41.3 us
    ppermute x24, starting transfers between devices, shift(): lax.ppermute(value, axis, [(i, (i + by) % size) for i in range(size)])  36.3 us
    ppermute x24, waiting for transfers between devices, shift(): lax.ppermute(value, axis, [(i, (i + by) % size) for i in range(size)])  28.4 us
    unnamed x94, local copies, waits for them, and re-layouts  19.4 us
    all_to_all x5, waiting for transfers between devices, exchange(): return lax.all_to_all(value, SEQ_AXES, 0, 0, tiled=True)  10.5 us
    convert_element_type x3, other arithmetic, body(): halves[k].astype(BF16)  5.04 us
  transfers between devices with their start and end apart: 29, of which 11 were waited for; matrix products, arithmetic and copies ran while one was open for 7% of the time, Pallas kernels for 15%

profile of v1, /device:TPU:38, one launch (start us, length us, event | category | flops | bytes accessed | tf_op | source)
XLA Modules:
  0.0 194.1 jit_solution(17493746288897354745)
XLA Ops:
  2.7 4.5 %collective-permute-start.5 = (bf16[8,1024]{1,0:T(8,128)(2,1)}, bf16[8,1024]{1,0:T(8,128)(2,1)S(1)}, u32[]{:S(2)}, u32[]{:S(2)}) collective-permute-start(bf16[8,1024]{1,0:T(8,128)(2,1)} %bitcast.38), channel_id=1, source_target_pairs={{0,2},{1,3},{2,4},{3,5},{4,6},{5,7},{6,0},{7,1},{8,10},{9,11},{10,... | collective-permute-start | bytes 49160 | tf_op jit(solution)/shard_map/ppermute | solution.py:278
  7.2 2.8 %collective-permute-start.4 = (bf16[8,1024]{1,0:T(8,128)(2,1)}, bf16[8,1024]{1,0:T(8,128)(2,1)S(1)}, u32[]{:S(2)}, u32[]{:S(2)}) collective-permute-start(bf16[8,1024]{1,0:T(8,128)(2,1)} %bitcast.39), channel_id=1, source_target_pairs={{0,3},{1,4},{2,5},{3,6},{4,7},{5,0},{6,1},{7,2},{8,11},{9,12},{10,... | collective-permute-start | bytes 49160 | tf_op jit(solution)/shard_map/ppermute | solution.py:278
  11.7 3.6 %collective-permute-start.1 = (bf16[8,1024]{1,0:T(8,128)(2,1)}, bf16[8,1024]{1,0:T(8,128)(2,1)S(1)}, u32[]{:S(2)}, u32[]{:S(2)}) collective-permute-start(bf16[8,1024]{1,0:T(8,128)(2,1)} %bitcast.41), channel_id=1, source_target_pairs={{0,6},{1,7},{2,0},{3,1},{4,2},{5,3},{6,4},{7,5},{8,14},{9,15},{10,... | collective-permute-start | bytes 49160 | tf_op jit(solution)/shard_map/ppermute | solution.py:278
  17.3 5.5 %collective-permute-start.2 = (bf16[8,1024]{1,0:T(8,128)(2,1)}, bf16[8,1024]{1,0:T(8,128)(2,1)S(1)}, u32[]{:S(2)}, u32[]{:S(2)}) collective-permute-start(bf16[8,1024]{1,0:T(8,128)(2,1)} %bitcast.42), channel_id=1, source_target_pairs={{0,5},{1,6},{2,7},{3,0},{4,1},{5,2},{6,3},{7,4},{8,13},{9,14},{10,... | collective-permute-start | bytes 49160 | tf_op jit(solution)/shard_map/ppermute | solution.py:278
  26.8 3.0 %collective-permute-start.7 = (bf16[64,1024]{1,0:T(8,128)(2,1)}, bf16[64,1024]{1,0:T(8,128)(2,1)S(1)}, u32[]{:S(2)}, u32[]{:S(2)}) collective-permute-start(bf16[64,1024]{1,0:T(8,128)(2,1)} %constant_dynamic-slice_fusion.1), channel_id=1, source_target_pairs={{0,24},{8,0},{16,8},{24,16},{1,25},{9,1},{17,9},{25,17},{2,26},{10... | collective-permute-start | bytes 393224 | tf_op jit(solution)/shard_map/ppermute | solution.py:278
  32.7 3.7 %shard_map.135 = (bf16[32,80,128]{2,1,0:T(8,128)(2,1)}, f32[128,2048]{1,0:T(8,128)S(1)}, f32[16,256,128]{2,1,0:T(8,128)S(1)}, f32[16,256]{1,0:T(8,128)S(1)}, bf16[256,2048]{1,0:T(8,128)(2,1)S(1)}) custom-call(bf16[256,2048]{1,0:T(8,128)(2,1)S(1)} %bitcast.19, bf16[256,128]{1,0:T(8,128)(2,1)S(1)} %bitcast.23, f32[256,16]{1,0:T(8,128)S(1)} %bitcast.31), custom_call_target="tpu_custom_call" | custom-call | flops 134217728 | bytes 5996544 | tf_op jit(solution)/shard_map/pallas_call | solution.py:261
  38.4 7.7 %all-to-all-start = ((bf16[32,80,128]{2,1,0:T(8,128)(2,1)}), bf16[32,80,128]{2,1,0:T(8,128)(2,1)}, u32[]{:S(2)}, u32[]{:S(2)}) async-start(bf16[32,80,128]{2,1,0:T(8,128)(2,1)} %get-tuple-element.37), calls=%async_computation | async-start | bytes 1310720 | tf_op jit(solution)/shard_map/all_to_all | solution.py:290
  46.0 3.1 %collective-permute-start.8 = (bf16[64,1024]{1,0:T(8,128)(2,1)}, bf16[64,1024]{1,0:T(8,128)(2,1)S(1)}, u32[]{:S(2)}, u32[]{:S(2)}) collective-permute-start(bf16[64,1024]{1,0:T(8,128)(2,1)} %constant_dynamic-slice_fusion.1), channel_id=1, source_target_pairs={{0,16},{8,24},{16,0},{24,8},{1,17},{9,25},{17,1},{25,9},{2,18},{10... | collective-permute-start | bytes 393224 | tf_op jit(solution)/shard_map/ppermute | solution.py:278
  49.7 4.5 %collective-permute-done.8 = bf16[64,1024]{1,0:T(8,128)(2,1)S(1)} collective-permute-done((bf16[64,1024]{1,0:T(8,128)(2,1)}, bf16[64,1024]{1,0:T(8,128)(2,1)S(1)}, u32[]{:S(2)}, u32[]{:S(2)}) %collective-permute-start.8) | collective-permute-done | bytes 131104 | tf_op jit(solution)/shard_map/ppermute | solution.py:278
  54.2 2.8 %collective-permute-done.9 = bf16[64,1024]{1,0:T(8,128)(2,1)S(1)} collective-permute-done((bf16[64,1024]{1,0:T(8,128)(2,1)}, bf16[64,1024]{1,0:T(8,128)(2,1)S(1)}, u32[]{:S(2)}, u32[]{:S(2)}) %collective-permute-start.9) | collective-permute-done | bytes 131104 | tf_op jit(solution)/shard_map/ppermute | solution.py:278
  65.3 8.0 %all-to-all-start.1 = ((bf16[32,64,128]{2,1,0:T(8,128)(2,1)}), bf16[32,64,128]{2,1,0:T(8,128)(2,1)}, u32[]{:S(2)}, u32[]{:S(2)}) async-start(bf16[32,64,128]{2,1,0:T(8,128)(2,1)} %copy-done.25), calls=%async_computation.1 | async-start | bytes 1048576 | tf_op jit(solution)/shard_map/all_to_all | solution.py:290
  73.5 4.6 %collective-permute-done.12.refs_3_ = bf16[256,1024]{1,0:T(8,128)(2,1)} collective-permute-done((bf16[256,1024]{1,0:T(8,128)(2,1)}, bf16[256,1024]{1,0:T(8,128)(2,1)}, u32[]{:S(2)}, u32[]{:S(2)}) %collective-permute-start.12) | collective-permute-done | bytes 524320 | tf_op jit(solution)/shard_map/ppermute | solution.py:278
  78.9 3.3 %shard_map.136.inner_ref = f32[256,2048]{1,0:T(8,128)S(1)} custom-call(bf16[256,2048]{1,0:T(8,128)(2,1)S(1)} %bitcast.20, bf16[256,128]{1,0:T(8,128)(2,1)S(1)} %bitcast.24, bf16[256,128]{1,0:T(8,128)(2,1)S(1)} %bitcast.28, f32[16,256,128]{2,1,0:T(8,128)S(1)} %get-tuple-element.35.col_ref, f32[16,256]{1,0:T(8,128)S(1)} %get-tuple-element.36.row_ref), custom_call_target="tpu_custom_call" | custom-call | flops 268435456 | bytes 5390336 | tf_op jit(solution)/shard_map/pallas_call | solution.py:261
  83.6 4.9 %shard_map.137.gn_ref = f32[256,2048]{1,0:T(8,128)} custom-call(s32[2]{0:T(128)S(1)} %pad_add_fusion.at_ref, bf16[256,1024]{1,0:T(8,128)(2,1)S(1)} %bitcast.32, bf16[256,1024]{1,0:T(8,128)(2,1)} %constant_dynamic-slice_fusion.refs_0_, bf16[256,1024]{1,0:T(8,128)(2,1)} %collective-permute-done.10.refs_1_, bf16[256,1024]{1,0:T(8,128)(2,1)} %collective-permute-done.11.refs_2_, ...), custom_call_target="tpu_custom_call" | custom-call | flops 1073741824 | bytes 6815752 | tf_op jit(solution)/shard_map/pallas_call | solution.py:261
  88.5 9.1 %shard_map.139 = (bf16[256,2048]{1,0:T(8,128)(2,1)}, bf16[256,2048]{1,0:T(8,128)(2,1)S(1)}, bf16[256,2048]{1,0:T(8,128)(2,1)S(1)}, bf16[256,2048]{1,0:T(8,128)(2...) custom-call(f32[256,2048]{1,0:T(8,128)} %copy-done.3, ...), custom_call_target="tpu_custom_call" | custom-call | flops 268435456 | bytes 12795904 | tf_op jit(solution)/shard_map/pallas_call | solution.py:261
  99.6 3.7 %shard_map.143 = (bf16[144,2048]{1,0:T(8,128)(2,1)S(1)}, bf16[144,2048]{1,0:T(8,128)(2,1)S(1)}, bf16[144,2048]{1,0:T(8,128)(2,1)S(1)}, bf16[144,2048]{1,0:T(8,12...) custom-call(s32[2]{0:T(128)S(1)} %pad_add_fusion.at_ref, ...), custom_call_target="tpu_custom_call" | custom-call | flops 1073741824 | bytes 6299656 | tf_op jit(solution)/shard_map/pallas_call | solution.py:261
  108.8 13.1 %all-to-all-start.2 = ((bf16[32,64,128]{2,1,0:T(8,128)(2,1)}), bf16[32,64,128]{2,1,0:T(8,128)(2,1)S(1)}, u32[]{:S(2)}, u32[]{:S(2)}) async-start(bf16[32,64,128]{2,1,0:T(8,128)(2,1)} %get-tuple-element.42), calls=%async_computation.2 | async-start | bytes 1048576 | tf_op jit(solution)/shard_map/all_to_all | solution.py:290
  131.1 9.1 %all-to-all-done.2.got_ref = bf16[32,64,128]{2,1,0:T(8,128)(2,1)S(1)} async-done(((bf16[32,64,128]{2,1,0:T(8,128)(2,1)}), bf16[32,64,128]{2,1,0:T(8,128)(2,1)S(1)}, u32[]{:S(2)}, u32[]{:S(2)}) %all-to-all-start.2) | async-done | bytes 524320 | tf_op jit(solution)/shard_map/all_to_all | solution.py:290
  141.2 4.8 %all-to-all-start.3 = ((bf16[32,64,128]{2,1,0:T(8,128)(2,1)}), bf16[32,64,128]{2,1,0:T(8,128)(2,1)S(1)}, u32[]{:S(2)}, u32[]{:S(2)}) async-start(bf16[32,64,128]{2,1,0:T(8,128)(2,1)} %shard_map.141), calls=%async_computation.3 | async-start | bytes 1048576 | tf_op jit(solution)/shard_map/all_to_all | solution.py:290
  146.1 7.0 %collective-permute-done.19 = bf16[144,2048]{1,0:T(8,128)(2,1)S(1)} collective-permute-done((bf16[144,2048]{1,0:T(8,128)(2,1)}, bf16[144,2048]{1,0:T(8,128)(2,1)S(1)}, u32[]{:S(2)}, u32[]{:S(2)}) %collective-permute-start.19) | collective-permute-done | bytes 589856 | tf_op jit(solution)/shard_map/ppermute | solution.py:278
  153.0 5.7 %collective-permute-done.23 = bf16[144,2048]{1,0:T(8,128)(2,1)} collective-permute-done((bf16[144,2048]{1,0:T(8,128)(2,1)}, bf16[144,2048]{1,0:T(8,128)(2,1)}, u32[]{:S(2)}, u32[]{:S(2)}) %collective-permute-start.23) | collective-permute-done | bytes 589856 | tf_op jit(solution)/shard_map/ppermute | solution.py:278
  163.9 9.8 %all-to-all-start.4 = ((bf16[32,72,128]{2,1,0:T(8,128)(2,1)}), bf16[32,72,128]{2,1,0:T(8,128)(2,1)S(1)}, u32[]{:S(2)}, u32[]{:S(2)}) async-start(bf16[32,72,128]{2,1,0:T(8,128)(2,1)} %fusion.1), calls=%async_computation.4 | async-start | bytes 1179648 | tf_op jit(solution)/shard_map/all_to_all | solution.py:290
  176.2 8.2 %shard_map.140 = (f32[256,2048]{1,0:T(8,128)S(1)}, bf16[256,128]{1,0:T(8,128)(2,1)}, f32[256,128]{1,0:T(8,128)S(1)}) custom-call(bf16[256,2048]{1,0:T(8,128)(2,1)S(1)} %bitcast.21, bf16[256,2048]{1,0:T(8,128)(2,1)S(1)} %copy-done.13, bf16[256,2048]{1,0:T(8,128)(2,1)S(1)} %copy-done.15, bf16[256,128]{1,0:T(8,128)(2,1)S(1)} %bitcast.25, ...), custom_call_target="tpu_custom_call" | custom-call | flops 671088640 | bytes 8208384 | tf_op jit(solution)/shard_map/pallas_call | solution.py:261
  185.7 5.8 %shard_map.142 = (bf16[256,2048]{1,0:T(8,128)(2,1)}, bf16[256,128]{1,0:T(8,128)(2,1)}, f32[256,16]{1,0:T(8,128)S(1)}) custom-call(f32[256,2048]{1,0:T(8,128)} %copy-done.4, bf16[32,64,128]{2,1,0:T(8,128)(2,1)S(1)} %all-to-all-done.3.leave_ref, bf16[256,128]{1,0:T(8,128)(2,1)S(1)} %bitcast.26, bf16[256,2048]{1,0:T(8,128)(2,1)S(1)} %bitcast.22, ...), custom_call_target="tpu_custom_call" | custom-call | flops 268435456 | bytes 9846784 | tf_op jit(solution)/shard_map/pallas_call | solution.py:261
  (155 shorter events, 55.0 us)
Async XLA Ops:
  0.6 11.1 %collective-permute-start = (bf16[8,1024]{1,0:T(8,128)(2,1)}, bf16[8,1024]{1,0:T(8,128)(2,1)S(1)}, u32[]{:S(2)}, u32[]{:S(2)}) collective-permute-start(bf16[8,1024]{1,0:T(8,128)(2,1)} %bitcast.36), channel_id=1, source_target_pairs={{0,7},{1,0},{2,1},{3,2},{4,3},{5,4},{6,5},{7,6},{8,15},{9,8},{10,9... | collective-permute-start | bytes 49160 | tf_op jit(solution)/shard_map/ppermute | solution.py:278
  0.8 23.7 %collective-permute-start.6 = (bf16[8,1024]{1,0:T(8,128)(2,1)}, bf16[8,1024]{1,0:T(8,128)(2,1)S(1)}, u32[]{:S(2)}, u32[]{:S(2)}) collective-permute-start(bf16[8,1024]{1,0:T(8,128)(2,1)} %bitcast.37), channel_id=1, source_target_pairs={{0,1},{1,2},{2,3},{3,4},{4,5},{5,6},{6,7},{7,0},{8,9},{9,10},{10,1... | collective-permute-start | bytes 49160 | tf_op jit(solution)/shard_map/ppermute | solution.py:278
  2.7 21.8 %collective-permute-start.5 = (bf16[8,1024]{1,0:T(8,128)(2,1)}, bf16[8,1024]{1,0:T(8,128)(2,1)S(1)}, u32[]{:S(2)}, u32[]{:S(2)}) collective-permute-start(bf16[8,1024]{1,0:T(8,128)(2,1)} %bitcast.38), channel_id=1, source_target_pairs={{0,2},{1,3},{2,4},{3,5},{4,6},{5,7},{6,0},{7,1},{8,10},{9,11},{10,... | collective-permute-start | bytes 49160 | tf_op jit(solution)/shard_map/ppermute | solution.py:278
  7.2 17.3 %collective-permute-start.4 = (bf16[8,1024]{1,0:T(8,128)(2,1)}, bf16[8,1024]{1,0:T(8,128)(2,1)S(1)}, u32[]{:S(2)}, u32[]{:S(2)}) collective-permute-start(bf16[8,1024]{1,0:T(8,128)(2,1)} %bitcast.39), channel_id=1, source_target_pairs={{0,3},{1,4},{2,5},{3,6},{4,7},{5,0},{6,1},{7,2},{8,11},{9,12},{10,... | collective-permute-start | bytes 49160 | tf_op jit(solution)/shard_map/ppermute | solution.py:278
  10.0 14.4 %collective-permute-start.3 = (bf16[8,1024]{1,0:T(8,128)(2,1)}, bf16[8,1024]{1,0:T(8,128)(2,1)S(1)}, u32[]{:S(2)}, u32[]{:S(2)}) collective-permute-start(bf16[8,1024]{1,0:T(8,128)(2,1)} %bitcast.40), channel_id=1, source_target_pairs={{0,4},{1,5},{2,6},{3,7},{4,0},{5,1},{6,2},{7,3},{8,12},{9,13},{10,... | collective-permute-start | bytes 49160 | tf_op jit(solution)/shard_map/ppermute | solution.py:278
  26.8 22.9 %collective-permute-start.7 = (bf16[64,1024]{1,0:T(8,128)(2,1)}, bf16[64,1024]{1,0:T(8,128)(2,1)S(1)}, u32[]{:S(2)}, u32[]{:S(2)}) collective-permute-start(bf16[64,1024]{1,0:T(8,128)(2,1)} %constant_dynamic-slice_fusion.1), channel_id=1, source_target_pairs={{0,24},{8,0},{16,8},{24,16},{1,25},{9,1},{17,9},{25,17},{2,26},{10... | collective-permute-start | bytes 393224 | tf_op jit(solution)/shard_map/ppermute | solution.py:278
  38.4 24.4 %all-to-all-start = ((bf16[32,80,128]{2,1,0:T(8,128)(2,1)}), bf16[32,80,128]{2,1,0:T(8,128)(2,1)}, u32[]{:S(2)}, u32[]{:S(2)}) async-start(bf16[32,80,128]{2,1,0:T(8,128)(2,1)} %get-tuple-element.37), calls=%async_computation | async-start | bytes 1310720 | tf_op jit(solution)/shard_map/all_to_all | solution.py:290
  46.0 8.2 %collective-permute-start.8 = (bf16[64,1024]{1,0:T(8,128)(2,1)}, bf16[64,1024]{1,0:T(8,128)(2,1)S(1)}, u32[]{:S(2)}, u32[]{:S(2)}) collective-permute-start(bf16[64,1024]{1,0:T(8,128)(2,1)} %constant_dynamic-slice_fusion.1), channel_id=1, source_target_pairs={{0,16},{8,24},{16,0},{24,8},{1,17},{9,25},{17,1},{25,9},{2,18},{10... | collective-permute-start | bytes 393224 | tf_op jit(solution)/shard_map/ppermute | solution.py:278
  49.1 7.9 %collective-permute-start.9 = (bf16[64,1024]{1,0:T(8,128)(2,1)}, bf16[64,1024]{1,0:T(8,128)(2,1)S(1)}, u32[]{:S(2)}, u32[]{:S(2)}) collective-permute-start(bf16[64,1024]{1,0:T(8,128)(2,1)} %constant_dynamic-slice_fusion.1), channel_id=1, source_target_pairs={{0,8},{8,16},{16,24},{24,0},{1,9},{9,17},{17,25},{25,1},{2,10},{10... | collective-permute-start | bytes 393224 | tf_op jit(solution)/shard_map/ppermute | solution.py:278
  58.0 20.2 %collective-permute-start.12 = (bf16[256,1024]{1,0:T(8,128)(2,1)}, bf16[256,1024]{1,0:T(8,128)(2,1)}, u32[]{:S(2)}, u32[]{:S(2)}) collective-permute-start(bf16[256,1024]{1,0:T(8,128)(2,1)} %constant_dynamic-slice_fusion.refs_0_), channel_id=1, source_target_pairs={{0,192},{64,0},{128,64},{192,128},{1,193},{65,1},{129,65},{193,129... | collective-permute-start | bytes 1572872 | tf_op jit(solution)/shard_map/ppermute | solution.py:278
  58.8 19.3 %collective-permute-start.11 = (bf16[256,1024]{1,0:T(8,128)(2,1)}, bf16[256,1024]{1,0:T(8,128)(2,1)}, u32[]{:S(2)}, u32[]{:S(2)}) collective-permute-start(bf16[256,1024]{1,0:T(8,128)(2,1)} %constant_dynamic-slice_fusion.refs_0_), channel_id=1, source_target_pairs={{0,128},{64,192},{128,0},{192,64},{1,129},{65,193},{129,1},{193,65... | collective-permute-start | bytes 1572872 | tf_op jit(solution)/shard_map/ppermute | solution.py:278
  59.9 18.9 %collective-permute-start.10 = (bf16[256,1024]{1,0:T(8,128)(2,1)}, bf16[256,1024]{1,0:T(8,128)(2,1)}, u32[]{:S(2)}, u32[]{:S(2)}) collective-permute-start(bf16[256,1024]{1,0:T(8,128)(2,1)} %constant_dynamic-slice_fusion.refs_0_), channel_id=1, source_target_pairs={{0,64},{64,128},{128,192},{192,0},{1,65},{65,129},{129,193},{193,1... | collective-permute-start | bytes 1572872 | tf_op jit(solution)/shard_map/ppermute | solution.py:278
  65.3 23.2 %all-to-all-start.1 = ((bf16[32,64,128]{2,1,0:T(8,128)(2,1)}), bf16[32,64,128]{2,1,0:T(8,128)(2,1)}, u32[]{:S(2)}, u32[]{:S(2)}) async-start(bf16[32,64,128]{2,1,0:T(8,128)(2,1)} %copy-done.25), calls=%async_computation.1 | async-start | bytes 1048576 | tf_op jit(solution)/shard_map/all_to_all | solution.py:290
  73.2 10.3 %collective-permute-start.13 = (bf16[256,1024]{1,0:T(8,128)(2,1)}, bf16[256,1024]{1,0:T(8,128)(2,1)}, u32[]{:S(2)}, u32[]{:S(2)}) collective-permute-start(bf16[256,1024]{1,0:T(8,128)(2,1)} %constant_dynamic-slice_fusion.refs_0_), channel_id=1, source_target_pairs={{0,32},{32,0},{1,33},{33,1},{2,34},{34,2},{3,35},{35,3},{4,36},{36... | collective-permute-start | bytes 1572872 | tf_op jit(solution)/shard_map/ppermute | solution.py:278
  108.3 14.2 %collective-permute-start.18 = (bf16[144,2048]{1,0:T(8,128)(2,1)}, bf16[144,2048]{1,0:T(8,128)(2,1)}, u32[]{:S(2)}, u32[]{:S(2)}) collective-permute-start(bf16[144,2048]{1,0:T(8,128)(2,1)} %get-tuple-element.58), channel_id=1, source_target_pairs={{0,32},{32,0},{1,33},{33,1},{2,34},{34,2},{3,35},{35,3},{4,36},{36... | collective-permute-start | bytes 1769480 | tf_op jit(solution)/shard_map/ppermute | solution.py:278
  108.8 18.4 %collective-permute-start.20 = (bf16[144,2048]{1,0:T(8,128)(2,1)}, bf16[144,2048]{1,0:T(8,128)(2,1)}, u32[]{:S(2)}, u32[]{:S(2)}) collective-permute-start(bf16[144,2048]{1,0:T(8,128)(2,1)} %get-tuple-element.60), channel_id=1, source_target_pairs={{0,32},{32,0},{1,33},{33,1},{2,34},{34,2},{3,35},{35,3},{4,36},{36... | collective-permute-start | bytes 1769480 | tf_op jit(solution)/shard_map/ppermute | solution.py:278
  108.8 31.4 %all-to-all-start.2 = ((bf16[32,64,128]{2,1,0:T(8,128)(2,1)}), bf16[32,64,128]{2,1,0:T(8,128)(2,1)S(1)}, u32[]{:S(2)}, u32[]{:S(2)}) async-start(bf16[32,64,128]{2,1,0:T(8,128)(2,1)} %get-tuple-element.42), calls=%async_computation.2 | async-start | bytes 1048576 | tf_op jit(solution)/shard_map/all_to_all | solution.py:290
  121.9 24.2 %collective-permute-start.17 = (bf16[144,2048]{1,0:T(8,128)(2,1)}, bf16[144,2048]{1,0:T(8,128)(2,1)}, u32[]{:S(2)}, u32[]{:S(2)}) collective-permute-start(bf16[144,2048]{1,0:T(8,128)(2,1)} %copy-done.30), channel_id=1, source_target_pairs={{0,32},{32,0},{1,33},{33,1},{2,34},{34,2},{3,35},{35,3},{4,36},{36... | collective-permute-start | bytes 1769480 | tf_op jit(solution)/shard_map/ppermute | solution.py:278
  122.0 7.4 %collective-permute-start.22 = (bf16[144,2048]{1,0:T(8,128)(2,1)}, bf16[144,2048]{1,0:T(8,128)(2,1)S(1)}, u32[]{:S(2)}, u32[]{:S(2)}) collective-permute-start(bf16[144,2048]{1,0:T(8,128)(2,1)} %copy-done.31), channel_id=1, source_target_pairs={{0,32},{32,0},{1,33},{33,1},{2,34},{34,2},{3,35},{35,3},{4,36},{36... | collective-permute-start | bytes 1769480 | tf_op jit(solution)/shard_map/ppermute | solution.py:278
  124.6 28.5 %collective-permute-start.19 = (bf16[144,2048]{1,0:T(8,128)(2,1)}, bf16[144,2048]{1,0:T(8,128)(2,1)S(1)}, u32[]{:S(2)}, u32[]{:S(2)}) collective-permute-start(bf16[144,2048]{1,0:T(8,128)(2,1)} %add_convert_fusion.3), channel_id=1, source_target_pairs={{0,64},{64,128},{128,192},{192,0},{1,65},{65,129},{129,193},{193,1... | collective-permute-start | bytes 1769480 | tf_op jit(solution)/shard_map/ppermute | solution.py:278
  129.2 23.8 %collective-permute-start.21 = (bf16[144,2048]{1,0:T(8,128)(2,1)}, bf16[144,2048]{1,0:T(8,128)(2,1)}, u32[]{:S(2)}, u32[]{:S(2)}) collective-permute-start(bf16[144,2048]{1,0:T(8,128)(2,1)} %add_convert_fusion.2), channel_id=1, source_target_pairs={{0,128},{64,192},{128,0},{192,64},{1,129},{65,193},{129,1},{193,65... | collective-permute-start | bytes 1769480 | tf_op jit(solution)/shard_map/ppermute | solution.py:278
  130.4 28.3 %collective-permute-start.23 = (bf16[144,2048]{1,0:T(8,128)(2,1)}, bf16[144,2048]{1,0:T(8,128)(2,1)}, u32[]{:S(2)}, u32[]{:S(2)}) collective-permute-start(bf16[144,2048]{1,0:T(8,128)(2,1)} %add_convert_fusion.1), channel_id=1, source_target_pairs={{0,192},{64,0},{128,64},{192,128},{1,193},{65,1},{129,65},{193,129... | collective-permute-start | bytes 1769480 | tf_op jit(solution)/shard_map/ppermute | solution.py:278
  141.2 22.7 %all-to-all-start.3 = ((bf16[32,64,128]{2,1,0:T(8,128)(2,1)}), bf16[32,64,128]{2,1,0:T(8,128)(2,1)S(1)}, u32[]{:S(2)}, u32[]{:S(2)}) async-start(bf16[32,64,128]{2,1,0:T(8,128)(2,1)} %shard_map.141), calls=%async_computation.3 | async-start | bytes 1048576 | tf_op jit(solution)/shard_map/all_to_all | solution.py:290
  163.9 28.9 %all-to-all-start.4 = ((bf16[32,72,128]{2,1,0:T(8,128)(2,1)}), bf16[32,72,128]{2,1,0:T(8,128)(2,1)S(1)}, u32[]{:S(2)}, u32[]{:S(2)}) async-start(bf16[32,72,128]{2,1,0:T(8,128)(2,1)} %fusion.1), calls=%async_computation.4 | async-start | bytes 1179648 | tf_op jit(solution)/shard_map/all_to_all | solution.py:290
  (40 other events, 290.3 us)

commit v2 on v1

v2 whole, which is shorter than its diff:
```python
import math

import jax
import jax.numpy as jnp
from jax import lax
from jax.experimental import pallas as pl
from jax.experimental.pallas import tpu as pltpu
from jax.sharding import Mesh
from jax.sharding import PartitionSpec as P

F32, BF16 = jnp.float32, jnp.bfloat16
T = 256
H = 16
W = 128
INNER = H * W
D = 1024
SEQ = 32
HALF = 64
EXTRA = 16
GAINROWS = 16
SEQ_AXES = ("y", "z")
FAR = -1e30
HI = lax.Precision.HIGHEST


def lane(h, width=W):
    return pl.ds(pl.multiple_of(h * width, width), width)


def dot(a, b, ca=1, cb=0, precision=None):
    return lax.dot_general(
        a, b, (((ca,), (cb,)), ((), ())), precision=precision, preferred_element_type=F32
    )


def iota(shape, axis):
    return lax.broadcasted_iota(jnp.int32, shape, axis)


def row_sum(a):
    return jnp.sum(a, axis=1, keepdims=True)


def column(ref, h):
    return jnp.broadcast_to(ref[pl.ds(h, 1), :], (W, T)).T


def pair_cols(ref, h):
    return jnp.concatenate([column(ref, 2 * h), column(ref, 2 * h + 1)], axis=1)


def pair_state(ref, h):
    blocks = ref[pl.ds(4 * h, 4), 0:HALF, :]
    first = blocks[0:2].reshape(W, W)
    second = blocks[2:4].reshape(W, W)
    return jnp.concatenate([first, second], axis=1)


def split_state(ref, h, value):
    ref[pl.ds(4 * h, 2), 0:HALF, :] = value[:, :W].reshape(2, HALF, W)
    ref[pl.ds(4 * h + 2, 2), 0:HALF, :] = value[:, W:].reshape(2, HALF, W)


def state_kernel(flow, x_ref, b_ref, decay_ref, send_ref, row_ref):
    tri = (iota((T, T), 0) >= iota((T, T), 1)).astype(F32)
    flow.arrive()
    decay = decay_ref[...]
    row_ref[...] = dot(decay, tri, 1, 1, precision=HI)
    flow.leave()
    b = b_ref[...]

    @pl.loop(0, H // 2)
    def _(h):
        flow.arrive(h)
        col = pair_cols(row_ref, h)
        total = col[T - 1 : T, :]
        cols = lane(h, 2 * W)
        x_end = (x_ref[:, cols].astype(F32) * jnp.exp(total - col)).astype(BF16)
        split_state(send_ref, h, dot(b, x_end, 0, 0).astype(BF16))
        high = total.astype(BF16).astype(F32)
        middle = (total - high).astype(BF16).astype(F32)
        low = total - high - middle
        at = iota((EXTRA, 2 * W), 0)
        rows = jnp.where(at == 0, high, jnp.where(at == 1, middle, jnp.where(at == 2, low, 0.0)))
        rows = rows.astype(BF16)
        for k in range(4):
            half = rows[:, :W] if k < 2 else rows[:, W:]
            send_ref[4 * h + k, HALF : HALF + EXTRA, :] = half
        flow.leave(h)


def forward_scan_kernel(flow, got_ref, out_ref, factor_ref):
    group = SEQ // PAIRS

    def step(h, carry):
        flow.arrive(h)
        for k in range(group):
            j = h * group + k
            out_ref[j] = carry.astype(BF16)
            tail = got_ref[j, HALF : HALF + EXTRA, :].astype(F32)
            factor = jnp.exp(jnp.sum(tail, axis=0, keepdims=True))
            factor_ref[pl.ds(j, 1), :] = factor
            carry = factor * carry + got_ref[j, 0:HALF, :].astype(F32)
        flow.leave(h)
        return carry

    lax.fori_loop(0, PAIRS, step, jnp.zeros((HALF, W), F32))
    flow.leave()


def backward_scan_kernel(flow, got_ref, factor_ref, out_ref):
    group = SEQ // PAIRS
    flow.arrive()

    def step(i, carry):
        h = PAIRS - 1 - i
        flow.arrive(h, True)
        for k in range(group - 1, -1, -1):
            j = h * group + k
            out_ref[j] = carry.astype(BF16)
            carry = factor_ref[pl.ds(j, 1), :] * carry + got_ref[j].astype(F32)
        flow.leave(h, True)
        return carry

    lax.fori_loop(0, PAIRS, step, jnp.zeros((HALF, W), F32))


def inner_kernel(flow, x_ref, b_ref, c_ref, row_ref, inner_ref):
    flow.arrive()
    scores = dot(c_ref[...], b_ref[...], 1, 1)
    causal = iota((T, T), 0) >= iota((T, T), 1)

    @pl.loop(0, PAIRS)
    def _(pair):
        flow.arrive(pair)
        for h in (2 * pair, 2 * pair + 1):
            col = column(row_ref, h)
            differ = jnp.concatenate([col, col], axis=1) - row_ref[pl.ds(h, 1), :]
            kernel = (scores * jnp.exp(jnp.where(causal, differ, FAR))).astype(BF16)
            inner_ref[:, lane(h)] = dot(kernel, x_ref[:, lane(h)])
        flow.leave(pair)


def order_kernel(flow, at_ref, *refs):
    pieces, (_, sems) = refs[:4], refs[4:]
    target = flow.outgoing.pairs.pop()[1]
    copies = []
    for k, piece in enumerate(pieces):
        rows = pl.multiple_of(lax.rem(at_ref[2] + 4 - k, 4) * HALF, HALF)
        copies.append(pltpu.make_async_copy(piece, target.at[pl.ds(rows, HALF), :], sems.at[k, 0]))
        copies[k].start()
    for copy in copies:
        copy.wait()


def normed_grad_kernel(flow, at_ref, grad_far, *refs):
    pieces, (out_ref, grad_ref, weight_ref, sems) = refs[:8], refs[8:]
    x, c = at_ref[0], at_ref[1]
    copies = [pltpu.make_async_copy(grad_far, grad_ref, sems.at[0, 0])]
    for k, piece in enumerate(pieces):
        copies.append(pltpu.make_async_copy(piece, weight_ref.at[k], sems.at[1 + k, 0]))
    for copy in copies:
        copy.start()
    copies[0].wait()
    for core in range(2):
        for k in range(4):
            copies[1 + 4 * core + k].wait()
            block = lax.rem(x + 4 - k, 4) * 2 + (c if core == 0 else 1 - c)
            out_ref[:, lane(block, 2 * W)] = dot(grad_ref[...], weight_ref[4 * core + k], 1, 1).astype(BF16)
    for h in range(CHUNKS):
        for k in flow.outgoing.where(True):
            flow.outgoing.copy(k, h).start()


def norm_kernel(
    flow, inner_ref, gn_ref, gate_ref, enter_ref, c_ref, row_ref, gain_ref,
    gate_out, grad_out, start_out, normed_out, send_ref, gain_out, rate_out, y_ref, u_ref,
):
    flow.arrive()
    c = c_ref[...]

    def first(h, sums):
        flow.arrive(h)
        squares, mixed = sums
        cols = lane(h, 2 * W)
        keep = jnp.exp(pair_cols(row_ref, h))
        y = inner_ref[:, cols] + keep * dot(c, pair_state(enter_ref, h))
        gate = gate_ref[:, cols].astype(F32)
        u = y * (gate * jax.nn.sigmoid(gate))
        y_ref[:, cols] = y
        u_ref[:, cols] = u
        both = gain_ref[:, cols] * gn_ref[:, cols].astype(F32) * u
        squared = u * u
        return (
            squares + squared[:, :W] + squared[:, W:],
            mixed + both[:, :W] + both[:, W:],
        )

    zero = jnp.zeros((T, W), F32)
    squares, mixed = lax.fori_loop(0, H // 2, first, (zero, zero))
    rstd = lax.rsqrt(row_sum(squares) / INNER + 1e-5)
    pull = rstd * rstd * rstd * (row_sum(mixed) / INNER)
    rate_out[...] = zero

    @pl.loop(0, H // 2)
    def _(h):
        cols = lane(h, 2 * W)
        y, u, gn = y_ref[:, cols], u_ref[:, cols], gn_ref[:, cols].astype(F32)
        gain = gain_ref[:, cols]
        gate = gate_ref[:, cols].astype(F32)
        sig = jax.nn.sigmoid(gate)
        normal = u * rstd
        grad_u = rstd * (gain * gn) - u * pull
        grad_y = grad_u * (gate * sig)
        gate_out[:, cols] = (grad_u * y * sig * (1.0 + gate * (1.0 - sig))).astype(BF16)
        normed_out[:, cols] = (normal * gain).astype(BF16)
        gain_out[:, cols] = jnp.sum(gn * normal, axis=0, keepdims=True)
        grad_out[:, cols] = grad_y.astype(BF16)
        start = (grad_y * jnp.exp(pair_cols(row_ref, h))).astype(BF16)
        start_out[:, cols] = start
        rate = grad_y * y
        at = iota((T, W), 1)
        rates = rate_out[...]
        rates = jnp.where(at == 2 * h, row_sum(rate[:, :W]), rates)
        rate_out[...] = jnp.where(at == 2 * h + 1, row_sum(rate[:, W:]), rates)
        split_state(send_ref, h, dot(c, start, 0, 0).astype(BF16))
        flow.leave(h)

    flow.leave()


def weight_kernel(flow, at_ref, grad_ref, normed_ref, gain_ref, own_ref, other_ref):
    x, c = at_ref[0], at_ref[1]
    flow.arrive()
    for h in range(0, PAIRS, STEP):
        flow.arrive(h)
    normed = normed_ref[...]
    for at, out, core in ((1, other_ref, 1 - c), (0, own_ref, c)):
        for k in range(4):
            block = lax.rem(x + k, 4) * 2 + core
            out[k, 0:W, :] = dot(grad_ref[:, lane(block)], normed, 0, 0).astype(BF16)
            gain = jnp.broadcast_to(gain_ref[:, lane(block, 2 * W)], (GAINROWS, 2 * W))
            out[k, W : W + GAINROWS, :] = jnp.zeros((GAINROWS, INNER), BF16)
            out[k, W : W + GAINROWS, 0 : 2 * W] = gain.astype(BF16)
            flow.outgoing.copy(at, k).start()


def add_kernel(flow, own_term, other_term, own_ref, right_ref, left_ref, forth_ref, back_ref):
    for at, k in ((3, 2), (1, 1), (2, 3), (0, 0)):
        flow.arrive(k * STEP)
        total = (own_term[k].astype(F32) + other_term[k].astype(F32)).astype(BF16)
        if k == 2:
            forth_ref[...] = total[:, :D]
            back_ref[...] = total[:, D:]
            flow.outgoing.copy(4).start()
        else:
            (own_ref, right_ref, left_ref)[at][...] = total
        flow.outgoing.copy(at).start()


def relay_kernel(flow, right_in, left_in, forth_in, back_in, right_ref, left_ref):
    flow.arrive()
    right_ref[:, :D] = (right_in[:, :D].astype(F32) + forth_in[...].astype(F32)).astype(BF16)
    right_ref[:, D:] = right_in[:, D:]
    left_ref[:, :D] = left_in[:, :D]
    left_ref[:, D:] = (left_in[:, D:].astype(F32) + back_in[...].astype(F32)).astype(BF16)
    flow.leave()


def pair_kernel(
    flow, x_ref, grad_ref, start_ref, b_ref, c_ref, row_ref, enter_ref,
    inner_ref, grad_c_ref, grad_b_ref, sum_ref,
):
    flow.arrive()
    b, c = b_ref[...], c_ref[...]
    scores = dot(b, c, 1, 1)
    causal = iota((T, T), 0) <= iota((T, T), 1)
    sum_ref[...] = jnp.zeros((T, T), F32)

    def step(pair, total):
        flow.arrive(pair)
        weights = []
        for h in (2 * pair, 2 * pair + 1):
            col = column(row_ref, h)
            differ = row_ref[pl.ds(h, 1), :] - jnp.concatenate([col, col], axis=1)
            table = jnp.exp(jnp.where(causal, differ, FAR))
            grad = grad_ref[:, lane(h)]
            inner_ref[:, lane(h)] = dot((scores * table).astype(BF16), grad)
            weights.append(dot(x_ref[:, lane(h)], grad, 1, 1) * table)
        sum_ref[...] += weights[0] + weights[1]
        flow.leave(pair)
        return total + dot(start_ref[:, lane(pair, 2 * W)], pair_state(enter_ref, pair), 1, 1)

    carried = lax.fori_loop(0, PAIRS, step, jnp.zeros((T, W), F32))
    weights = sum_ref[...].astype(BF16)
    grad_b_ref[...] = dot(weights, c)
    grad_c_ref[...] = (carried + dot(weights, b, 0, 0)).astype(BF16)
    flow.leave()


def sum_kernel(flow, *refs):
    *terms, out_ref, gain_ref = refs
    flow.arrive()
    total = terms[0][...].astype(F32)
    for term in terms[1:]:
        total = total + term[...].astype(F32)
    out_ref[...] = total[0:W, :].astype(BF16)
    gain_ref[...] = total[W : W + 8, 0 : 2 * W]
    flow.leave()


def last_kernel(
    flow, inner_ref, leave_ref, b_ref, x_ref, row_ref, grad_b_in, rate_ref, state_ref, enter_ref,
    grad_x_ref, grad_b_ref, decay_ref,
):
    flow.arrive()
    b = b_ref[...]

    def step(h, carry):
        flow.arrive(h)
        grad_b, rates, tail = carry
        cols = lane(h, 2 * W)
        leave = pair_state(leave_ref, h)
        col = pair_cols(row_ref, h)
        total = col[T - 1 : T, :]
        keep = jnp.exp(total - col)
        grad_x = inner_ref[:, cols] + keep * dot(b, leave)
        grad_x_ref[:, cols] = grad_x.astype(BF16)
        flow.leave(h)
        x = x_ref[:, cols].astype(F32)
        rate = x * grad_x
        at = iota((T, W), 1)
        rates = rates - jnp.where(at == 2 * h, row_sum(rate[:, :W]), 0.0)
        rates = rates - jnp.where(at == 2 * h + 1, row_sum(rate[:, W:]), 0.0)
        state = pair_state(state_ref, h).astype(F32)
        later = jnp.exp(total) * pair_state(enter_ref, h).astype(F32) + state
        across = jnp.sum(later * leave.astype(F32), axis=0, keepdims=True)
        at = iota((W, 1), 0)
        tail = tail + jnp.where(at == 2 * h, row_sum(across[:, :W]), 0.0)
        tail = tail + jnp.where(at == 2 * h + 1, row_sum(across[:, W:]), 0.0)
        return grad_b + dot((x * keep).astype(BF16), leave, 1, 1), rates, tail

    start = (grad_b_in[...], rate_ref[...], jnp.zeros((W, 1), F32))
    grad_b, rates, tail = lax.fori_loop(0, H // 2, step, start)
    grad_b_ref[...] = grad_b.astype(BF16)
    lower = (iota((T, T), 0) >= iota((T, T), 1)).astype(F32)
    decay_ref[...] = (dot(rates, lower, 0, 0, precision=HI) + tail)[:H, :]
    flow.leave()


PAIRS = H // 2
CHUNKS = 4
STEP = PAIRS // CHUNKS


def chunked(array):
    return array.shape == (T, INNER) or len(array.shape) == 3 and array.shape[0] in (4, SEQ)


def part(ref, h):
    if len(ref.shape) == 2:
        return ref.at[:, lane(h, 2 * W * STEP)]
    count = ref.shape[0] // CHUNKS
    return ref.at[pl.ds(h * count, count)]


class Traffic:
    def __init__(self, sources, targets, sems):
        self.pairs = list(zip(sources, targets, range(len(sources))))
        self.sems = sems

    def copy(self, k, h=None):
        source, target, at = self.pairs[k]
        if h is None:
            return pltpu.make_async_copy(source, target, self.sems.at[at, 0])
        return pltpu.make_async_copy(part(source, h), part(target, h), self.sems.at[at, h])

    def where(self, pieces):
        return [k for k, (source, _, _) in enumerate(self.pairs) if chunked(source) == pieces]


class Flow:
    def __init__(self, incoming, outgoing):
        self.incoming, self.outgoing = incoming, outgoing

    def begin(self):
        for k in self.incoming.where(False):
            self.incoming.copy(k).start()
        for h in range(CHUNKS):
            for k in self.incoming.where(True):
                self.incoming.copy(k, h).start()

    def arrive(self, pair=None, last_first=False):
        if pair is None:
            for k in self.incoming.where(False):
                self.incoming.copy(k).wait()
            return

        @pl.when(lax.rem(pair, STEP) == (STEP - 1 if last_first else 0))
        def _():
            for k in self.incoming.where(True):
                self.incoming.copy(k, lax.div(pair, STEP)).wait()

    def leave(self, pair=None, last_first=False):
        if pair is None:
            for k in self.outgoing.where(False):
                self.outgoing.copy(k).start()
            return

        @pl.when(lax.rem(pair, STEP) == (0 if last_first else STEP - 1))
        def _():
            for k in self.outgoing.where(True):
                self.outgoing.copy(k, lax.div(pair, STEP)).start()

    def end(self):
        for k in self.outgoing.where(False):
            self.outgoing.copy(k).wait()
        for h in range(CHUNKS):
            for k in self.outgoing.where(True):
                self.outgoing.copy(k, h).wait()


def call(kernel, outs, args, scratch=(), smem=0, us=1.0, loose=(), after=(), own=False):
    scalars, arrays = args[:smem], args[smem:]
    far = pl.BlockSpec(memory_space=pltpu.HBM)
    moved = sum(a.size * a.dtype.itemsize for a in (*args, *outs))
    held = moved + sum(math.prod(s.shape) * 4 for s in scratch)
    kept = [] if own else arrays
    counts = (smem, len(arrays), len(after), len(outs), len(kept), len(outs), len(scratch))

    def run(*refs):
        groups = []
        for count in counts:
            groups.append(refs[:count])
            refs = refs[count:]
        numbers, sources, _, targets, near_in, near_out, rest = groups
        flow = Flow(Traffic(sources, near_in, refs[0]), Traffic(near_out, targets, refs[1]))
        if own:
            kernel(flow, *numbers, *sources, *near_out, *rest, refs[0])
        else:
            flow.begin()
            kernel(flow, *numbers, *near_in, *near_out, *rest)
        flow.end()

    tied = [a if any(a is b for b in loose) else pltpu.with_memory_space_constraint(a, pltpu.HBM) for a in arrays]
    return pl.pallas_call(
        run,
        out_shape=[pltpu.HBM(out.shape, out.dtype) for out in outs],
        in_specs=[pl.BlockSpec(memory_space=pltpu.SMEM)] * smem
        + [pl.BlockSpec(memory_space=pl.ANY) if any(a is b for b in loose) else far for a in arrays]
        + [pl.BlockSpec(memory_space=pl.ANY)] * len(after),
        out_specs=[far] * len(outs),
        scratch_shapes=[
            *(pltpu.VMEM(a.shape, a.dtype) for a in (*kept, *outs)),
            *scratch,
            pltpu.SemaphoreType.DMA((len(arrays), CHUNKS)),
            pltpu.SemaphoreType.DMA((len(outs), CHUNKS)),
        ],
        compiler_params=pltpu.CompilerParams(vmem_limit_bytes=held + 6 * 2**20),
        cost_estimate=pl.CostEstimate(flops=int(us * 1.1e9), bytes_accessed=moved, transcendentals=0),
    )(*scalars, *tied, *after)


def shaped(shape, dtype=F32):
    return jax.ShapeDtypeStruct(shape, dtype)


def shift(value, axis, by):
    size = lax.axis_size(axis)
    return lax.ppermute(value, axis, [(i, (i + by) % size) for i in range(size)])


def shifts(values, axis):
    return [value if k == 0 else shift(value, axis, k) for k, value in enumerate(values)]


def exchange(value, axes=SEQ_AXES):
    return lax.all_to_all(value, axes, 0, 0, tiled=True)


def body(ssm, gate, state_in, state_out, log_decay, gain, out_weight, grad_rows):
    x, b, c = ssm[0], state_in[0], state_out[0]
    gate, grad_rows, gain_row = gate[0], grad_rows[0], gain[None]
    at = jnp.stack([lax.axis_index(name) for name in ("x", "c", "y")]).astype(jnp.int32)
    wide = shaped((T, INNER))
    wide_bf = shaped((T, INNER), BF16)
    states = shaped((SEQ, HALF, W), BF16)

    send, row = call(
        state_kernel,
        [shaped((SEQ, HALF + EXTRA, W), BF16), shaped((H, T))],
        [x, b, log_decay[0].T],
        us=0.1,
    )
    got = exchange(send)

    own = exchange(jnp.broadcast_to(out_weight.T, (8, 8, D)), "z").reshape(HALF, D)
    [inner] = call(inner_kernel, [wide], [x, b, c, row], us=0.3)
    slices = shifts([own] * 4, "y")
    [ordered] = call(
        order_kernel, [shaped((T, D), BF16)], [at, *slices], smem=1, us=0.1, loose=slices, own=True, after=[inner]
    )
    pieces = shifts([ordered] * 4, "x")
    pieces += [shift(piece, "c", 1) for piece in pieces]

    enter_part, factor = call(
        forward_scan_kernel, [states, shaped((SEQ, W))], [got], us=0.1, loose=[got]
    )
    enter = exchange(enter_part)
    [grad_normed] = call(
        normed_grad_kernel,
        [wide_bf],
        [at, grad_rows, *pieces],
        scratch=[pltpu.VMEM((T, D), BF16), pltpu.VMEM((8, T, D), BF16)],
        own=True,
        smem=1,
        us=1.0,
        loose=pieces,
    )
    grad_gate, grad_y, grad_start, normed, grad_send, gain_term, rate = call(
        norm_kernel,
        [wide_bf, wide_bf, wide_bf, wide_bf, states, shaped((1, INNER)), shaped((T, W))],
        [inner, grad_normed, gate, enter, c, row, gain_row],
        scratch=[pltpu.VMEM((T, INNER), F32), pltpu.VMEM((T, INNER), F32)],
        us=0.3,
        loose=[enter],
    )
    grad_got = exchange(grad_send)
    own_term, other_term = call(
        weight_kernel,
        [shaped((4, W + GAINROWS, INNER), BF16)] * 2,
        [at, grad_rows, normed, gain_term],
        smem=1,
        us=4.6,
    )
    other_term = shift(other_term, "c", 1)
    block = shaped((W + GAINROWS, INNER), BF16)
    half = shaped((W + GAINROWS, D), BF16)
    kept, right, left, forth, back = call(
        add_kernel, [block, block, block, half, half], [own_term, other_term], us=3.7, loose=[other_term]
    )
    forth, back = shift(forth, "x", 1), shift(back, "x", -1)
    right, left = call(
        relay_kernel, [block, block], [right, left, forth, back], us=2.8, loose=[forth, back]
    )
    [leave_part] = call(
        backward_scan_kernel, [states], [grad_got, factor], us=2.0, loose=[grad_got], after=[right]
    )
    leave = exchange(leave_part)
    right, left = shift(right, "x", 1), shift(left, "x", -1)
    quarter, gains = call(
        sum_kernel,
        [shaped((W, INNER), BF16), shaped((8, 2 * W))],
        [kept, right, left],
        us=2.6,
        loose=[right, left],
    )
    grad_inner, grad_state_out, grad_b = call(
        pair_kernel,
        [wide, shaped((T, W), BF16), shaped((T, W))],
        [x, grad_y, grad_start, b, c, row, enter],
        scratch=[pltpu.VMEM((T, T), F32)],
        us=5.8,
        loose=[enter],
        after=[leave_part],
    )
    rows = quarter.reshape(SEQ, HALF, W)
    gains = jnp.pad(gains[0].astype(BF16).reshape(SEQ, 1, 8), ((0, 0), (0, 7), (0, W - 8)))
    final = jnp.sum(exchange(jnp.concatenate([rows, gains], axis=1)).astype(F32), axis=0)
    grad_input, grad_state_in, grad_log_decay = call(
        last_kernel,
        [wide_bf, shaped((T, W), BF16), shaped((H, T))],
        [grad_inner, leave, b, x, row, grad_b, rate, send, enter],
        us=5.5,
        loose=[leave, enter],
    )
    return (
        grad_input[None],
        grad_gate[None],
        grad_state_in[None],
        grad_state_out[None],
        grad_log_decay.T[None],
        final[:HALF].reshape(4, INNER),
        final[HALF, :8],
    )


def solution(mesh):
    split = Mesh(mesh.devices.reshape(4, 2, 4, 8), ("x", "c", "y", "z"))
    shower, seq = ("x", "c"), ("y", "z")
    rows = P(shower, seq, None)
    every = (*shower, *seq)
    return jax.shard_map(
        body,
        mesh=split,
        in_specs=(rows, rows, rows, rows, rows, P(), P(None, every), rows),
        out_specs=(rows, rows, rows, rows, rows, P(every, None), P(every)),
        check_vma=False,
    )
```

time: 195 us -> 174 us (0.89)
  starting transfers between devices: 79.6 us -> 61.6 us
  local copies, waits for them, and re-layouts: 25 us -> 7.38 us
  Pallas kernels: 41.3 us -> 52.5 us
  waiting for transfers between devices: 38.9 us -> 49.6 us
  other arithmetic: 8.17 us -> 1.03 us
    ppermute x24 -> x15, starting transfers between devices: 36.3 us -> 15 us  [shift(): lax.ppermute(value, axis, [(i, (i + by) % size) for i in range(size)])]
    unnamed x94 -> x8, local copies, waits for them, and re-layouts: 19.4 us -> 2.7 us
    pallas_call x9 -> x13, Pallas kernels: 41.3 us -> 52.5 us  [call(): pl.pallas_call(run, out_shape=[pltpu.HBM(out.shape, out.dtype) for out in...]
    all_to_all x5 -> x6, waiting for transfers between devices: 10.5 us -> 18.8 us  [exchange(): return lax.all_to_all(value, axes, 0, 0, tiled=True)]
    convert_element_type x3 -> x0, other arithmetic: 5.04 us -> none  [body(): halves[k].astype(BF16)]
    all_to_all x5 -> x6, starting transfers between devices: 43.3 us -> 46.6 us  [exchange(): return lax.all_to_all(value, axes, 0, 0, tiled=True)]
    ppermute x24 -> x15, waiting for transfers between devices: 28.4 us -> 30.7 us  [shift(): lax.ppermute(value, axis, [(i, (i + by) % size) for i in range(size)])]
    another operation x2 -> x1, other arithmetic: 2.17 us -> 0.08 us  [body(): jnp.stack([lax.axis_index(name) for name in ('x', 'c', 'y')])]
  transfers between devices with their start and end apart: 29 -> 21, of which waited for: 11 -> 13; matrix products, arithmetic and copies ran while one was open for 7% -> 2% of each run, Pallas kernels for 15% -> 23%
where the time goes in v2:
time: 174 us; the launch traced here: 173 us
  starting transfers between devices  61.6 us (35%)
  Pallas kernels  52.5 us (30%)
  waiting for transfers between devices  49.6 us (29%)
  local copies, waits for them, and re-layouts  7.38 us (4%)
    pallas_call x13, Pallas kernels, call(): pl.pallas_call(run, out_shape=[pltpu.HBM(out.shape, out.dtype) for out in...  52.5 us
    all_to_all x6, starting transfers between devices, exchange(): return lax.all_to_all(value, axes, 0, 0, tiled=True)  46.6 us
    ppermute x15, waiting for transfers between devices, shift(): lax.ppermute(value, axis, [(i, (i + by) % size) for i in range(size)])  30.7 us
    all_to_all x6, waiting for transfers between devices, exchange(): return lax.all_to_all(value, axes, 0, 0, tiled=True)  18.8 us
    ppermute x15, starting transfers between devices, shift(): lax.ppermute(value, axis, [(i, (i + by) % size) for i in range(size)])  15 us
  transfers between devices with their start and end apart: 21, of which 13 were waited for; matrix products, arithmetic and copies ran while one was open for 2% of the time, Pallas kernels for 23%

profile of v2, /device:TPU:38, one launch (start us, length us, event | category | flops | bytes accessed | tf_op | source)
XLA Modules:
  0.0 173.1 jit_solution(6162886102519367617)
XLA Ops:
  2.0 8.6 %all-to-all-start = ((bf16[8,8,1024]{2,1,0:T(8,128)(2,1)}), bf16[8,8,1024]{2,1,0:T(8,128)(2,1)S(1)}, u32[]{:S(2)}, u32[]{:S(2)}) async-start(bf16[8,8,1024]{2,1,0:T(8,128)(2,1)} %broadcast_in_dim.21), calls=%async_computation | async-start | bytes 262144 | tf_op jit(solution)/shard_map/all_to_all | solution.py:478
  10.6 4.4 %shard_map.135 = (bf16[32,80,128]{2,1,0:T(8,128)(2,1)}, f32[16,256]{1,0:T(8,128)}) custom-call(bf16[256,2048]{1,0:T(8,128)(2,1)} %bitcast.27, bf16[256,128]{1,0:T(8,128)(2,1)} %bitcast.37, f32[16,256]{1,0:T(8,128)} %bitcast.41), custom_call_target="tpu_custom_call" | custom-call | flops 110000000 | bytes 1802240 | tf_op jit(solution)/shard_map/pallas_call | solution.py:446
  15.0 3.0 %all-to-all-done = bf16[8,8,1024]{2,1,0:T(8,128)(2,1)S(1)} async-done(((bf16[8,8,1024]{2,1,0:T(8,128)(2,1)}), bf16[8,8,1024]{2,1,0:T(8,128)(2,1)S(1)}, u32[]{:S(2)}, u32[]{:S(2)}) %all-to-all-start) | async-done | bytes 131104 | tf_op jit(solution)/shard_map/all_to_all | solution.py:478
  18.0 7.0 %all-to-all-start.1 = ((bf16[32,80,128]{2,1,0:T(8,128)(2,1)}), bf16[32,80,128]{2,1,0:T(8,128)(2,1)S(1)}, u32[]{:S(2)}, u32[]{:S(2)}) async-start(bf16[32,80,128]{2,1,0:T(8,128)(2,1)} %get-tuple-element.36.refs_7_), calls=%async_computation.1 | async-start | bytes 1310720 | tf_op jit(solution)/shard_map/all_to_all | solution.py:478
  25.1 2.8 %collective-permute-start.2 = (bf16[64,1024]{1,0:T(8,128)(2,1)S(1)}, bf16[64,1024]{1,0:T(8,128)(2,1)S(1)}, u32[]{:S(2)}, u32[]{:S(2)}) collective-permute-start(bf16[64,1024]{1,0:T(8,128)(2,1)S(1)} %bitcast.23), channel_id=1, source_target_pairs={{0,24},{8,0},{16,8},{24,16},{1,25},{9,1},{17,9},{25,17},{2,26},{10... | collective-permute-start | bytes 393224 | tf_op jit(solution)/shard_map/ppermute | solution.py:470
  29.5 4.6 %shard_map.136.refs_5_.refs_0_ = f32[256,2048]{1,0:T(8,128)} custom-call(bf16[256,2048]{1,0:T(8,128)(2,1)} %bitcast.28, bf16[256,128]{1,0:T(8,128)(2,1)} %bitcast.38, bf16[256,128]{1,0:T(8,128)(2,1)} %bitcast.34, f32[16,256]{1,0:T(8,128)} %get-tuple-element.35.refs_3_.refs_5_.refs_4_), custom_call_target="tpu_custom_call" | custom-call | flops 330000000 | bytes 3293184 | tf_op jit(solution)/shard_map/pallas_call | solution.py:446
  34.2 3.2 %collective-permute-done.2.refs_4_ = bf16[64,1024]{1,0:T(8,128)(2,1)S(1)} collective-permute-done((bf16[64,1024]{1,0:T(8,128)(2,1)S(1)}, bf16[64,1024]{1,0:T(8,128)(2,1)S(1)}, u32[]{:S(2)}, u32[]{:S(2)}) %collective-permute-start.2) | collective-permute-done | bytes 131104 | tf_op jit(solution)/shard_map/ppermute | solution.py:470
  49.5 8.2 %all-to-all-start.2 = ((bf16[32,64,128]{2,1,0:T(8,128)(2,1)}), bf16[32,64,128]{2,1,0:T(8,128)(2,1)S(1)}, u32[]{:S(2)}, u32[]{:S(2)}) async-start(bf16[32,64,128]{2,1,0:T(8,128)(2,1)} %get-tuple-element.37), calls=%async_computation.2 | async-start | bytes 1048576 | tf_op jit(solution)/shard_map/all_to_all | solution.py:478
  57.8 12.2 %collective-permute-done.5.refs_5_ = bf16[256,1024]{1,0:T(8,128)(2,1)S(1)} collective-permute-done((bf16[256,1024]{1,0:T(8,128)(2,1)}, bf16[256,1024]{1,0:T(8,128)(2,1)S(1)}, u32[]{:S(2)}, u32[]{:S(2)}) %collective-permute-start.5) | collective-permute-done | bytes 524320 | tf_op jit(solution)/shard_map/ppermute | solution.py:470
  73.4 6.5 %shard_map.138.refs_1_ = bf16[256,2048]{1,0:T(8,128)(2,1)} custom-call(s32[3]{0:T(128)S(1)} %pad_add_fusion.refs_0_, bf16[256,1024]{1,0:T(8,128)(2,1)} %bitcast.32, bf16[256,1024]{1,0:T(8,128)(2,1)S(1)} %copy-done.1, bf16[256,1024]{1,0:T(8,128)(2,1)S(1)} %collective-permute-done.3.refs_3_, bf16[256,1024]{1,0:T(8,128)(2,1)S(1)} %collective-permute-done.4.refs_4_, ...), custom_call_target="tpu_custom_call" | custom-call | flops 1100000000 | bytes 5767180 | tf_op jit(solution)/shard_map/pallas_call | solution.py:446
  80.0 8.0 %shard_map.140 = (bf16[256,2048]{1,0:T(8,128)(2,1)}, bf16[256,2048]{1,0:T(8,128)(2,1)}, bf16[256,2048]{1,0:T(8,128)(2,1)}, bf16[256,2048]{1,0:T(8,128)(2,1)}, bf...) custom-call(f32[256,2048]{1,0:T(8,128)} %shard_map.136.refs_5_.refs_0_, ...), custom_call_target="tpu_custom_call" | custom-call | flops 330000000 | bytes 9666560 | tf_op jit(solution)/shard_map/pallas_call | solution.py:446
  88.0 4.6 %shard_map.141 = (bf16[4,144,2048]{2,1,0:T(8,128)(2,1)}, bf16[4,144,2048]{2,1,0:T(8,128)(2,1)}) custom-call(s32[3]{0:T(128)S(1)} %pad_add_fusion.refs_0_, bf16[256,1024]{1,0:T(8,128)(2,1)} %bitcast.33, bf16[256,2048]{1,0:T(8,128)(2,1)} %get-tuple-element.42.refs_2_, f32[1,2048]{1,0:T(1,128)} %get-tuple-element.43.refs_3_), custom_call_target="tpu_custom_call" | custom-call | flops 5059999744 | bytes 6299660 | tf_op jit(solution)/shard_map/pallas_call | solution.py:446
  92.8 8.2 %all-to-all-start.3 = ((bf16[32,64,128]{2,1,0:T(8,128)(2,1)}), bf16[32,64,128]{2,1,0:T(8,128)(2,1)S(1)}, u32[]{:S(2)}, u32[]{:S(2)}) async-start(bf16[32,64,128]{2,1,0:T(8,128)(2,1)} %get-tuple-element.40), calls=%async_computation.3 | async-start | bytes 1048576 | tf_op jit(solution)/shard_map/all_to_all | solution.py:478
  101.1 3.2 %shard_map.142 = (bf16[144,2048]{1,0:T(8,128)(2,1)}, bf16[144,2048]{1,0:T(8,128)(2,1)}, bf16[144,2048]{1,0:T(8,128)(2,1)}, bf16[144,1024]{1,0:T(8,128)(2,1)}, bf16[144,1024]{1,0:T(8,128)(2,1)}) custom-call(bf16[4,144,2048]{2,1,0:T(8,128)(2,1)} %get-tuple-element.44.refs_0_, bf16[4,144,2048]{2,1,0:T(8,128)(2,1)S(1)} %collective-permute-done.10.refs_1_), custom_call_target="tpu_custom_call" | custom-call | flops 4070000128 | bytes 7077888 | tf_op jit(solution)/shard_map/pallas_call | solution.py:446
  106.4 6.9 %collective-permute-done.11.refs_2_ = bf16[144,1024]{1,0:T(8,128)(2,1)S(1)} collective-permute-done((bf16[144,1024]{1,0:T(8,128)(2,1)}, bf16[144,1024]{1,0:T(8,128)(2,1)S(1)}, u32[]{:S(2)}, u32[]{:S(2)}) %collective-permute-start.11) | collective-permute-done | bytes 294944 | tf_op jit(solution)/shard_map/ppermute | solution.py:470
  113.3 2.7 %collective-permute-done.12.refs_3_ = bf16[144,1024]{1,0:T(8,128)(2,1)S(1)} collective-permute-done((bf16[144,1024]{1,0:T(8,128)(2,1)}, bf16[144,1024]{1,0:T(8,128)(2,1)S(1)}, u32[]{:S(2)}, u32[]{:S(2)}) %collective-permute-start.12) | collective-permute-done | bytes 294944 | tf_op jit(solution)/shard_map/ppermute | solution.py:470
  116.0 2.6 %shard_map.143 = (bf16[144,2048]{1,0:T(8,128)(2,1)}, bf16[144,2048]{1,0:T(8,128)(2,1)}) custom-call(bf16[144,2048]{1,0:T(8,128)(2,1)} %get-tuple-element.46.refs_0_, bf16[144,2048]{1,0:T(8,128)(2,1)} %get-tuple-element.47.refs_1_, bf16[144,1024]{1,0:T(8,128)(2,1)S(1)} %collective-permute-done.11.refs_2_, bf16[144,1024]{1,0:T(8,128)(2,1)S(1)} %collective-permute-done.12.refs_3_), custom_call_target="tpu_custom_call" | custom-call | flops 3080000000 | bytes 2949120 | tf_op jit(solution)/shard_map/pallas_call | solution.py:446
  118.6 3.2 %collective-permute-start.13 = (bf16[144,2048]{1,0:T(8,128)(2,1)}, bf16[144,2048]{1,0:T(8,128)(2,1)S(1)}, u32[]{:S(2)}, u32[]{:S(2)}) collective-permute-start(bf16[144,2048]{1,0:T(8,128)(2,1)} %get-tuple-element.50.refs_2_), channel_id=1, source_target_pairs={{0,64},{64,128},{128,192},{192,0},{1,65},{65,129},{129,193},{193,1... | collective-permute-start | bytes 1769480 | tf_op jit(solution)/shard_map/ppermute | solution.py:470
  124.7 9.8 %all-to-all-start.4 = ((bf16[32,64,128]{2,1,0:T(8,128)(2,1)}), bf16[32,64,128]{2,1,0:T(8,128)(2,1)S(1)}, u32[]{:S(2)}, u32[]{:S(2)}) async-start(bf16[32,64,128]{2,1,0:T(8,128)(2,1)} %shard_map.144.refs_7_), calls=%async_computation.4 | async-start | bytes 1048576 | tf_op jit(solution)/shard_map/all_to_all | solution.py:478
  139.7 10.6 %all-to-all-done.4.refs_1_ = bf16[32,64,128]{2,1,0:T(8,128)(2,1)S(1)} async-done(((bf16[32,64,128]{2,1,0:T(8,128)(2,1)}), bf16[32,64,128]{2,1,0:T(8,128)(2,1)S(1)}, u32[]{:S(2)}, u32[]{:S(2)}) %all-to-all-start.4) | async-done | bytes 524320 | tf_op jit(solution)/shard_map/all_to_all | solution.py:478
  150.3 4.8 %all-to-all-start.5 = ((bf16[32,72,128]{2,1,0:T(8,128)(2,1)}), bf16[32,72,128]{2,1,0:T(8,128)(2,1)S(1)}, u32[]{:S(2)}, u32[]{:S(2)}) async-start(bf16[32,72,128]{2,1,0:T(8,128)(2,1)} %fusion.1), calls=%async_computation.5 | async-start | bytes 1179648 | tf_op jit(solution)/shard_map/all_to_all | solution.py:478
  155.2 5.8 %shard_map.145 = (f32[256,2048]{1,0:T(8,128)}, bf16[256,128]{1,0:T(8,128)(2,1)}, f32[256,128]{1,0:T(8,128)}) custom-call(bf16[256,2048]{1,0:T(8,128)(2,1)} %bitcast.29, bf16[256,2048]{1,0:T(8,128)(2,1)} %get-tuple-element.38.refs_1_, bf16[256,2048]{1,0:T(8,128)(2,1)} %get-tuple-element.39.refs_2_, bf16[256,128]{1,0:T(8,128)(2,1)} %bitcast.39, ...), custom_call_target="tpu_custom_call" | custom-call | flops 6380000256 | bytes 6111232 | tf_op jit(solution)/shard_map/pallas_call | solution.py:446
  161.0 5.6 %shard_map.146 = (bf16[256,2048]{1,0:T(8,128)(2,1)}, bf16[256,128]{1,0:T(8,128)(2,1)}, f32[16,256]{1,0:T(8,128)}) custom-call(f32[256,2048]{1,0:T(8,128)} %get-tuple-element.51.refs_0_, bf16[32,64,128]{2,1,0:T(8,128)(2,1)S(1)} %all-to-all-done.4.refs_1_, bf16[256,128]{1,0:T(8,128)(2,1)} %bitcast.40, bf16[256,2048]{1,0:T(8,128)(2,1)} %bitcast.30, ...), custom_call_target="tpu_custom_call" | custom-call | flops 6049999872 | bytes 6324224 | tf_op jit(solution)/shard_map/pallas_call | solution.py:446
  166.5 5.3 %all-to-all-done.5 = bf16[32,72,128]{2,1,0:T(8,128)(2,1)S(1)} async-done(((bf16[32,72,128]{2,1,0:T(8,128)(2,1)}), bf16[32,72,128]{2,1,0:T(8,128)(2,1)S(1)}, u32[]{:S(2)}, u32[]{:S(2)}) %all-to-all-start.5) | async-done | bytes 589856 | tf_op jit(solution)/shard_map/all_to_all | solution.py:478
  (49 shorter events, 30.4 us)
Async XLA Ops:
  2.0 16.0 %all-to-all-start = ((bf16[8,8,1024]{2,1,0:T(8,128)(2,1)}), bf16[8,8,1024]{2,1,0:T(8,128)(2,1)S(1)}, u32[]{:S(2)}, u32[]{:S(2)}) async-start(bf16[8,8,1024]{2,1,0:T(8,128)(2,1)} %broadcast_in_dim.21), calls=%async_computation | async-start | bytes 262144 | tf_op jit(solution)/shard_map/all_to_all | solution.py:478
  18.0 29.6 %all-to-all-start.1 = ((bf16[32,80,128]{2,1,0:T(8,128)(2,1)}), bf16[32,80,128]{2,1,0:T(8,128)(2,1)S(1)}, u32[]{:S(2)}, u32[]{:S(2)}) async-start(bf16[32,80,128]{2,1,0:T(8,128)(2,1)} %get-tuple-element.36.refs_7_), calls=%async_computation.1 | async-start | bytes 1310720 | tf_op jit(solution)/shard_map/all_to_all | solution.py:478
  25.1 12.4 %collective-permute-start.2 = (bf16[64,1024]{1,0:T(8,128)(2,1)S(1)}, bf16[64,1024]{1,0:T(8,128)(2,1)S(1)}, u32[]{:S(2)}, u32[]{:S(2)}) collective-permute-start(bf16[64,1024]{1,0:T(8,128)(2,1)S(1)} %bitcast.23), channel_id=1, source_target_pairs={{0,24},{8,0},{16,8},{24,16},{1,25},{9,1},{17,9},{25,17},{2,26},{10... | collective-permute-start | bytes 393224 | tf_op jit(solution)/shard_map/ppermute | solution.py:470
  27.9 10.0 %collective-permute-start.1 = (bf16[64,1024]{1,0:T(8,128)(2,1)S(1)}, bf16[64,1024]{1,0:T(8,128)(2,1)S(1)}, u32[]{:S(2)}, u32[]{:S(2)}) collective-permute-start(bf16[64,1024]{1,0:T(8,128)(2,1)S(1)} %bitcast.24), channel_id=1, source_target_pairs={{0,16},{8,24},{16,0},{24,8},{1,17},{9,25},{17,1},{25,9},{2,18},{10... | collective-permute-start | bytes 393224 | tf_op jit(solution)/shard_map/ppermute | solution.py:470
  28.7 11.7 %collective-permute-start = (bf16[64,1024]{1,0:T(8,128)(2,1)S(1)}, bf16[64,1024]{1,0:T(8,128)(2,1)S(1)}, u32[]{:S(2)}, u32[]{:S(2)}) collective-permute-start(bf16[64,1024]{1,0:T(8,128)(2,1)S(1)} %bitcast.25), channel_id=1, source_target_pairs={{0,8},{8,16},{16,24},{24,0},{1,9},{9,17},{17,25},{25,1},{2,10},{10... | collective-permute-start | bytes 393224 | tf_op jit(solution)/shard_map/ppermute | solution.py:470
  40.4 1.6 copy-start
  43.5 14.1 %copy-start.1 = (bf16[256,1024]{1,0:T(8,128)(2,1)S(1)}, bf16[256,1024]{1,0:T(8,128)(2,1)}, u32[]{:S(2)}) copy-start(bf16[256,1024]{1,0:T(8,128)(2,1)} %shard_map.137.refs_2_) | copy-start | bytes 1572868
  43.5 26.5 %collective-permute-start.5 = (bf16[256,1024]{1,0:T(8,128)(2,1)}, bf16[256,1024]{1,0:T(8,128)(2,1)S(1)}, u32[]{:S(2)}, u32[]{:S(2)}) collective-permute-start(bf16[256,1024]{1,0:T(8,128)(2,1)} %shard_map.137.refs_2_), channel_id=1, source_target_pairs={{0,192},{64,0},{128,64},{192,128},{1,193},{65,1},{129,65},{193,129... | collective-permute-start | bytes 1572872 | tf_op jit(solution)/shard_map/ppermute | solution.py:470
  44.4 25.6 %collective-permute-start.4 = (bf16[256,1024]{1,0:T(8,128)(2,1)}, bf16[256,1024]{1,0:T(8,128)(2,1)S(1)}, u32[]{:S(2)}, u32[]{:S(2)}) collective-permute-start(bf16[256,1024]{1,0:T(8,128)(2,1)} %shard_map.137.refs_2_), channel_id=1, source_target_pairs={{0,128},{64,192},{128,0},{192,64},{1,129},{65,193},{129,1},{193,65... | collective-permute-start | bytes 1572872 | tf_op jit(solution)/shard_map/ppermute | solution.py:470
  45.6 25.1 %collective-permute-start.3 = (bf16[256,1024]{1,0:T(8,128)(2,1)}, bf16[256,1024]{1,0:T(8,128)(2,1)S(1)}, u32[]{:S(2)}, u32[]{:S(2)}) collective-permute-start(bf16[256,1024]{1,0:T(8,128)(2,1)} %shard_map.137.refs_2_), channel_id=1, source_target_pairs={{0,64},{64,128},{128,192},{192,0},{1,65},{65,129},{129,193},{193,1... | collective-permute-start | bytes 1572872 | tf_op jit(solution)/shard_map/ppermute | solution.py:470
  49.5 30.5 %all-to-all-start.2 = ((bf16[32,64,128]{2,1,0:T(8,128)(2,1)}), bf16[32,64,128]{2,1,0:T(8,128)(2,1)S(1)}, u32[]{:S(2)}, u32[]{:S(2)}) async-start(bf16[32,64,128]{2,1,0:T(8,128)(2,1)} %get-tuple-element.37), calls=%async_computation.2 | async-start | bytes 1048576 | tf_op jit(solution)/shard_map/all_to_all | solution.py:478
  57.7 13.1 %collective-permute-start.6 = (bf16[256,1024]{1,0:T(8,128)(2,1)S(1)}, bf16[256,1024]{1,0:T(8,128)(2,1)S(1)}, u32[]{:S(2)}, u32[]{:S(2)}) collective-permute-start(bf16[256,1024]{1,0:T(8,128)(2,1)S(1)} %copy-done.1), channel_id=1, source_target_pairs={{0,32},{32,0},{1,33},{33,1},{2,34},{34,2},{3,35},{35,3},{4,36},{36... | collective-permute-start | bytes 1572872 | tf_op jit(solution)/shard_map/ppermute | solution.py:470
  70.0 1.9 %collective-permute-start.9 = (bf16[256,1024]{1,0:T(8,128)(2,1)S(1)}, bf16[256,1024]{1,0:T(8,128)(2,1)S(1)}, u32[]{:S(2)}, u32[]{:S(2)}) collective-permute-start(bf16[256,1024]{1,0:T(8,128)(2,1)S(1)} %collective-permute-done.5.refs_5_), channel_id=1, source_target_pairs={{0,32},{32,0},{1,33},{33,1},{2,34},{34,2},{3,35},{35,3},{4,36},{36... | collective-permute-start | bytes 1572872 | tf_op jit(solution)/shard_map/ppermute | solution.py:470
  70.0 2.7 %collective-permute-start.8 = (bf16[256,1024]{1,0:T(8,128)(2,1)S(1)}, bf16[256,1024]{1,0:T(8,128)(2,1)S(1)}, u32[]{:S(2)}, u32[]{:S(2)}) collective-permute-start(bf16[256,1024]{1,0:T(8,128)(2,1)S(1)} %collective-permute-done.4.refs_4_), channel_id=1, source_target_pairs={{0,32},{32,0},{1,33},{33,1},{2,34},{34,2},{3,35},{35,3},{4,36},{36... | collective-permute-start | bytes 1572872 | tf_op jit(solution)/shard_map/ppermute | solution.py:470
  70.6 2.8 %collective-permute-start.7 = (bf16[256,1024]{1,0:T(8,128)(2,1)S(1)}, bf16[256,1024]{1,0:T(8,128)(2,1)S(1)}, u32[]{:S(2)}, u32[]{:S(2)}) collective-permute-start(bf16[256,1024]{1,0:T(8,128)(2,1)S(1)} %collective-permute-done.3.refs_3_), channel_id=1, source_target_pairs={{0,32},{32,0},{1,33},{33,1},{2,34},{34,2},{3,35},{35,3},{4,36},{36... | collective-permute-start | bytes 1572872 | tf_op jit(solution)/shard_map/ppermute | solution.py:470
  92.6 8.5 %collective-permute-start.10 = (bf16[4,144,2048]{2,1,0:T(8,128)(2,1)}, bf16[4,144,2048]{2,1,0:T(8,128)(2,1)S(1)}, u32[]{:S(2)}, u32[]{:S(2)}) collective-permute-start(bf16[4,144,2048]{2,1,0:T(8,128)(2,1)} %get-tuple-element.45), channel_id=1, source_target_pairs={{0,32},{32,0},{1,33},{33,1},{2,34},{34,2},{3,35},{35,3},{4,36},{36... | collective-permute-start | bytes 7077896 | tf_op jit(solution)/shard_map/ppermute | solution.py:470
  92.8 29.0 %all-to-all-start.3 = ((bf16[32,64,128]{2,1,0:T(8,128)(2,1)}), bf16[32,64,128]{2,1,0:T(8,128)(2,1)S(1)}, u32[]{:S(2)}, u32[]{:S(2)}) async-start(bf16[32,64,128]{2,1,0:T(8,128)(2,1)} %get-tuple-element.40), calls=%async_computation.3 | async-start | bytes 1048576 | tf_op jit(solution)/shard_map/all_to_all | solution.py:478
  104.3 9.0 %collective-permute-start.11 = (bf16[144,1024]{1,0:T(8,128)(2,1)}, bf16[144,1024]{1,0:T(8,128)(2,1)S(1)}, u32[]{:S(2)}, u32[]{:S(2)}) collective-permute-start(bf16[144,1024]{1,0:T(8,128)(2,1)} %get-tuple-element.48), channel_id=1, source_target_pairs={{0,64},{64,128},{128,192},{192,0},{1,65},{65,129},{129,193},{193,1... | collective-permute-start | bytes 884744 | tf_op jit(solution)/shard_map/ppermute | solution.py:470
  106.1 9.9 %collective-permute-start.12 = (bf16[144,1024]{1,0:T(8,128)(2,1)}, bf16[144,1024]{1,0:T(8,128)(2,1)S(1)}, u32[]{:S(2)}, u32[]{:S(2)}) collective-permute-start(bf16[144,1024]{1,0:T(8,128)(2,1)} %get-tuple-element.49), channel_id=1, source_target_pairs={{0,192},{64,0},{128,64},{192,128},{1,193},{65,1},{129,65},{193,129... | collective-permute-start | bytes 884744 | tf_op jit(solution)/shard_map/ppermute | solution.py:470
  118.5 15.9 %collective-permute-start.14 = (bf16[144,2048]{1,0:T(8,128)(2,1)}, bf16[144,2048]{1,0:T(8,128)(2,1)S(1)}, u32[]{:S(2)}, u32[]{:S(2)}) collective-permute-start(bf16[144,2048]{1,0:T(8,128)(2,1)} %get-tuple-element.60), channel_id=1, source_target_pairs={{0,192},{64,0},{128,64},{192,128},{1,193},{65,1},{129,65},{193,129... | collective-permute-start | bytes 1769480 | tf_op jit(solution)/shard_map/ppermute | solution.py:470
  118.6 15.8 %collective-permute-start.13 = (bf16[144,2048]{1,0:T(8,128)(2,1)}, bf16[144,2048]{1,0:T(8,128)(2,1)S(1)}, u32[]{:S(2)}, u32[]{:S(2)}) collective-permute-start(bf16[144,2048]{1,0:T(8,128)(2,1)} %get-tuple-element.50.refs_2_), channel_id=1, source_target_pairs={{0,64},{64,128},{128,192},{192,0},{1,65},{65,129},{129,193},{193,1... | collective-permute-start | bytes 1769480 | tf_op jit(solution)/shard_map/ppermute | solution.py:470
  124.7 25.6 %all-to-all-start.4 = ((bf16[32,64,128]{2,1,0:T(8,128)(2,1)}), bf16[32,64,128]{2,1,0:T(8,128)(2,1)S(1)}, u32[]{:S(2)}, u32[]{:S(2)}) async-start(bf16[32,64,128]{2,1,0:T(8,128)(2,1)} %shard_map.144.refs_7_), calls=%async_computation.4 | async-start | bytes 1048576 | tf_op jit(solution)/shard_map/all_to_all | solution.py:478
  138.0 17.2 %copy-start.2 = (bf16[32,64,128]{2,1,0:T(8,128)(2,1)S(1)}, bf16[32,64,128]{2,1,0:T(8,128)(2,1)}, u32[]{:S(2)}) copy-start(bf16[32,64,128]{2,1,0:T(8,128)(2,1)} %shard_map.144.refs_7_) | copy-start | bytes 1572868
  150.3 21.5 %all-to-all-start.5 = ((bf16[32,72,128]{2,1,0:T(8,128)(2,1)}), bf16[32,72,128]{2,1,0:T(8,128)(2,1)S(1)}, u32[]{:S(2)}, u32[]{:S(2)}) async-start(bf16[32,72,128]{2,1,0:T(8,128)(2,1)} %fusion.1), calls=%async_computation.5 | async-start | bytes 1179648 | tf_op jit(solution)/shard_map/all_to_all | solution.py:478
  (1 other events, 1.1 us)

commit v3 on v2

--- a/solution.py
+++ b/solution.py
@@ -20,6 +20,7 @@
 GAINROWS = 16
 SEQ_AXES = ("y", "z")
 FAR = -1e30
+FAR_PIECES = (0, 4, 1, 3)
 HI = lax.Precision.HIGHEST
 
 
@@ -41,12 +42,23 @@
     return jnp.sum(a, axis=1, keepdims=True)
 
 
-def column(ref, h):
-    return jnp.broadcast_to(ref[pl.ds(h, 1), :], (W, T)).T
-
-
-def pair_cols(ref, h):
-    return jnp.concatenate([column(ref, 2 * h), column(ref, 2 * h + 1)], axis=1)
+def column(row):
+    return jnp.broadcast_to(row, (W, T)).T
+
+
+def row_of(ref, h):
+    return ref[pl.ds(h, 1), :]
+
+
+def pair_starts(ref, h):
+    return jnp.concatenate([column(jnp.exp(row_of(ref, 2 * h + k))) for k in range(2)], axis=1)
+
+
+def pair_ends(ref, h):
+    rows = [row_of(ref, 2 * h + k) for k in range(2)]
+    keep = jnp.concatenate([column(jnp.exp(row[:, T - 1 :] - row)) for row in rows], axis=1)
+    total = jnp.concatenate([jnp.broadcast_to(row[:, T - 1 :], (1, W)) for row in rows], axis=1)
+    return keep, total
 
 
 def pair_state(ref, h):
@@ -72,10 +84,9 @@
     @pl.loop(0, H // 2)
     def _(h):
         flow.arrive(h)
-        col = pair_cols(row_ref, h)
-        total = col[T - 1 : T, :]
+        keep, total = pair_ends(row_ref, h)
         cols = lane(h, 2 * W)
-        x_end = (x_ref[:, cols].astype(F32) * jnp.exp(total - col)).astype(BF16)
+        x_end = (x_ref[:, cols].astype(F32) * keep).astype(BF16)
         split_state(send_ref, h, dot(b, x_end, 0, 0).astype(BF16))
         high = total.astype(BF16).astype(F32)
         middle = (total - high).astype(BF16).astype(F32)
@@ -134,10 +145,10 @@
     def _(pair):
         flow.arrive(pair)
         for h in (2 * pair, 2 * pair + 1):
-            col = column(row_ref, h)
-            differ = jnp.concatenate([col, col], axis=1) - row_ref[pl.ds(h, 1), :]
+            col = column(row_of(row_ref, h))
+            differ = jnp.concatenate([col, col], axis=1) - row_of(row_ref, h)
             kernel = (scores * jnp.exp(jnp.where(causal, differ, FAR))).astype(BF16)
-            inner_ref[:, lane(h)] = dot(kernel, x_ref[:, lane(h)])
+            inner_ref[:, lane(h)] = dot(kernel, x_ref[:, lane(h)]).astype(BF16)
         flow.leave(pair)
 
 
@@ -156,25 +167,27 @@
 def normed_grad_kernel(flow, at_ref, grad_far, *refs):
     pieces, (out_ref, grad_ref, weight_ref, sems) = refs[:8], refs[8:]
     x, c = at_ref[0], at_ref[1]
-    copies = [pltpu.make_async_copy(grad_far, grad_ref, sems.at[0, 0])]
-    for k, piece in enumerate(pieces):
-        copies.append(pltpu.make_async_copy(piece, weight_ref.at[k], sems.at[1 + k, 0]))
-    for copy in copies:
-        copy.start()
-    copies[0].wait()
-    for core in range(2):
-        for k in range(4):
-            copies[1 + 4 * core + k].wait()
-            block = lax.rem(x + 4 - k, 4) * 2 + (c if core == 0 else 1 - c)
-            out_ref[:, lane(block, 2 * W)] = dot(grad_ref[...], weight_ref[4 * core + k], 1, 1).astype(BF16)
+    grad_copy = pltpu.make_async_copy(grad_far, grad_ref, sems.at[0, 0])
+    grad_copy.start()
+    copies = {}
+    for slot, at in enumerate(FAR_PIECES):
+        copies[at] = (pltpu.make_async_copy(pieces[at], weight_ref.at[slot], sems.at[1 + slot, 0]), slot)
+        copies[at][0].start()
+    grad_copy.wait()
+    for at in (*(k for k in range(8) if k not in FAR_PIECES), *FAR_PIECES):
+        if at in copies:
+            copies[at][0].wait()
+        weight = weight_ref[copies[at][1]] if at in copies else pieces[at][...]
+        block = lax.rem(x + 4 - at % 4, 4) * 2 + (c if at < 4 else 1 - c)
+        out_ref[:, lane(block, 2 * W)] = dot(grad_ref[...], weight, 1, 1).astype(BF16)
     for h in range(CHUNKS):
         for k in flow.outgoing.where(True):
             flow.outgoing.copy(k, h).start()
 
 
 def norm_kernel(
-    flow, inner_ref, gn_ref, gate_ref, enter_ref, c_ref, row_ref, gain_ref,
-    gate_out, grad_out, start_out, normed_out, send_ref, gain_out, rate_out, y_ref, u_ref,
+    flow, at_ref, inner_ref, gn_ref, gate_ref, enter_ref, c_ref, row_ref, gain_ref, rows_ref,
+    gate_out, grad_out, send_ref, rate_out, own_ref, other_ref, y_ref, sig_ref, normed_out, gain_out,
 ):
     flow.arrive()
     c = c_ref[...]
@@ -183,12 +196,13 @@
         flow.arrive(h)
         squares, mixed = sums
         cols = lane(h, 2 * W)
-        keep = jnp.exp(pair_cols(row_ref, h))
-        y = inner_ref[:, cols] + keep * dot(c, pair_state(enter_ref, h))
+        keep = pair_starts(row_ref, h)
+        y = inner_ref[:, cols].astype(F32) + keep * dot(c, pair_state(enter_ref, h))
         gate = gate_ref[:, cols].astype(F32)
-        u = y * (gate * jax.nn.sigmoid(gate))
+        sig = 0.5 * jnp.tanh(0.5 * gate) + 0.5
+        u = y * (gate * sig)
         y_ref[:, cols] = y
-        u_ref[:, cols] = u
+        sig_ref[:, cols] = sig
         both = gain_ref[:, cols] * gn_ref[:, cols].astype(F32) * u
         squared = u * u
         return (
@@ -205,19 +219,19 @@
     @pl.loop(0, H // 2)
     def _(h):
         cols = lane(h, 2 * W)
-        y, u, gn = y_ref[:, cols], u_ref[:, cols], gn_ref[:, cols].astype(F32)
+        y, sig, gn = y_ref[:, cols], sig_ref[:, cols], gn_ref[:, cols].astype(F32)
         gain = gain_ref[:, cols]
         gate = gate_ref[:, cols].astype(F32)
-        sig = jax.nn.sigmoid(gate)
+        active = gate * sig
+        u = y * active
         normal = u * rstd
         grad_u = rstd * (gain * gn) - u * pull
-        grad_y = grad_u * (gate * sig)
-        gate_out[:, cols] = (grad_u * y * sig * (1.0 + gate * (1.0 - sig))).astype(BF16)
+        grad_y = grad_u * active
+        gate_out[:, cols] = (grad_u * y * (sig + active * (1.0 - sig))).astype(BF16)
         normed_out[:, cols] = (normal * gain).astype(BF16)
         gain_out[:, cols] = jnp.sum(gn * normal, axis=0, keepdims=True)
         grad_out[:, cols] = grad_y.astype(BF16)
-        start = (grad_y * jnp.exp(pair_cols(row_ref, h))).astype(BF16)
-        start_out[:, cols] = start
+        start = (grad_y * pair_starts(row_ref, h)).astype(BF16)
         rate = grad_y * y
         at = iota((T, W), 1)
         rates = rate_out[...]
@@ -227,19 +241,13 @@
         flow.leave(h)
 
     flow.leave()
-
-
-def weight_kernel(flow, at_ref, grad_ref, normed_ref, gain_ref, own_ref, other_ref):
-    x, c = at_ref[0], at_ref[1]
-    flow.arrive()
-    for h in range(0, PAIRS, STEP):
-        flow.arrive(h)
-    normed = normed_ref[...]
-    for at, out, core in ((1, other_ref, 1 - c), (0, own_ref, c)):
+    x, core = at_ref[0], at_ref[1]
+    normed = normed_out[...]
+    for at, out, target in ((5, other_ref, 1 - core), (4, own_ref, core)):
         for k in range(4):
-            block = lax.rem(x + k, 4) * 2 + core
-            out[k, 0:W, :] = dot(grad_ref[:, lane(block)], normed, 0, 0).astype(BF16)
-            gain = jnp.broadcast_to(gain_ref[:, lane(block, 2 * W)], (GAINROWS, 2 * W))
+            block = lax.rem(x + k, 4) * 2 + target
+            out[k, 0:W, :] = dot(rows_ref[:, lane(block)], normed, 0, 0).astype(BF16)
+            gain = jnp.broadcast_to(gain_out[:, lane(block, 2 * W)], (GAINROWS, 2 * W))
             out[k, W : W + GAINROWS, :] = jnp.zeros((GAINROWS, INNER), BF16)
             out[k, W : W + GAINROWS, 0 : 2 * W] = gain.astype(BF16)
             flow.outgoing.copy(at, k).start()
@@ -268,7 +276,7 @@
 
 
 def pair_kernel(
-    flow, x_ref, grad_ref, start_ref, b_ref, c_ref, row_ref, enter_ref,
+    flow, x_ref, grad_ref, b_ref, c_ref, row_ref, enter_ref,
     inner_ref, grad_c_ref, grad_b_ref, sum_ref,
 ):
     flow.arrive()
@@ -281,15 +289,16 @@
         flow.arrive(pair)
         weights = []
         for h in (2 * pair, 2 * pair + 1):
-            col = column(row_ref, h)
-            differ = row_ref[pl.ds(h, 1), :] - jnp.concatenate([col, col], axis=1)
+            col = column(row_of(row_ref, h))
+            differ = row_of(row_ref, h) - jnp.concatenate([col, col], axis=1)
             table = jnp.exp(jnp.where(causal, differ, FAR))
             grad = grad_ref[:, lane(h)]
             inner_ref[:, lane(h)] = dot((scores * table).astype(BF16), grad)
             weights.append(dot(x_ref[:, lane(h)], grad, 1, 1) * table)
         sum_ref[...] += weights[0] + weights[1]
         flow.leave(pair)
-        return total + dot(start_ref[:, lane(pair, 2 * W)], pair_state(enter_ref, pair), 1, 1)
+        start = (grad_ref[:, lane(pair, 2 * W)].astype(F32) * pair_starts(row_ref, pair)).astype(BF16)
+        return total + dot(start, pair_state(enter_ref, pair), 1, 1)
 
     carried = lax.fori_loop(0, PAIRS, step, jnp.zeros((T, W), F32))
     weights = sum_ref[...].astype(BF16)
@@ -321,9 +330,7 @@
         grad_b, rates, tail = carry
         cols = lane(h, 2 * W)
         leave = pair_state(leave_ref, h)
-        col = pair_cols(row_ref, h)
-        total = col[T - 1 : T, :]
-        keep = jnp.exp(total - col)
+        keep, total = pair_ends(row_ref, h)
         grad_x = inner_ref[:, cols] + keep * dot(b, leave)
         grad_x_ref[:, cols] = grad_x.astype(BF16)
         flow.leave(h)
@@ -410,7 +417,8 @@
         @pl.when(lax.rem(pair, STEP) == (0 if last_first else STEP - 1))
         def _():
             for k in self.outgoing.where(True):
-                self.outgoing.copy(k, lax.div(pair, STEP)).start()
+                if self.outgoing.pairs[k][0].shape[0] != 4:
+                    self.outgoing.copy(k, lax.div(pair, STEP)).start()
 
     def end(self):
         for k in self.outgoing.where(False):
@@ -420,12 +428,12 @@
                 self.outgoing.copy(k, h).wait()
 
 
-def call(kernel, outs, args, scratch=(), smem=0, us=1.0, loose=(), after=(), own=False):
+def call(kernel, outs, args, scratch=(), smem=0, us=1.0, loose=(), after=(), own=False, near=()):
     scalars, arrays = args[:smem], args[smem:]
-    far = pl.BlockSpec(memory_space=pltpu.HBM)
-    moved = sum(a.size * a.dtype.itemsize for a in (*args, *outs))
-    held = moved + sum(math.prod(s.shape) * 4 for s in scratch)
-    kept = [] if own else arrays
+    held = sum(a.size * a.dtype.itemsize for a in (*arrays, *outs))
+    room = held + sum(math.prod(s.shape) * 4 for s in scratch)
+    spaces = [next((space for group, space in ((near, pltpu.VMEM), (loose, pl.ANY)) if any(a is b for b in group)), pltpu.HBM) for a in arrays]
+    kept = [] if own else [a for a, space in zip(arrays, spaces) if space is not pltpu.VMEM]
     counts = (smem, len(arrays), len(after), len(outs), len(kept), len(outs), len(scratch))
 
     def run(*refs):
@@ -433,32 +441,38 @@
         for count in counts:
             groups.append(refs[:count])
             refs = refs[count:]
-        numbers, sources, _, targets, near_in, near_out, rest = groups
-        flow = Flow(Traffic(sources, near_in, refs[0]), Traffic(near_out, targets, refs[1]))
+        numbers, sources, _, targets, copies, near_out, rest = groups
+        far = [source for source, space in zip(sources, spaces) if space is not pltpu.VMEM]
+        flow = Flow(Traffic(far, copies, refs[0]), Traffic(near_out, targets, refs[1]))
         if own:
             kernel(flow, *numbers, *sources, *near_out, *rest, refs[0])
         else:
             flow.begin()
+            copies = list(copies)
+            near_in = [s if space is pltpu.VMEM else copies.pop(0) for s, space in zip(sources, spaces)]
             kernel(flow, *numbers, *near_in, *near_out, *rest)
         flow.end()
 
-    tied = [a if any(a is b for b in loose) else pltpu.with_memory_space_constraint(a, pltpu.HBM) for a in arrays]
+    def tie(array, space):
+        return array if space is pl.ANY else pltpu.with_memory_space_constraint(array, space)
+
+    tied = [tie(a, space) for a, space in zip(arrays, spaces)]
     return pl.pallas_call(
         run,
         out_shape=[pltpu.HBM(out.shape, out.dtype) for out in outs],
         in_specs=[pl.BlockSpec(memory_space=pltpu.SMEM)] * smem
-        + [pl.BlockSpec(memory_space=pl.ANY) if any(a is b for b in loose) else far for a in arrays]
+        + [pl.BlockSpec(memory_space=space) for space in spaces]
         + [pl.BlockSpec(memory_space=pl.ANY)] * len(after),
-        out_specs=[far] * len(outs),
+        out_specs=[pl.BlockSpec(memory_space=pltpu.HBM)] * len(outs),
         scratch_shapes=[
             *(pltpu.VMEM(a.shape, a.dtype) for a in (*kept, *outs)),
             *scratch,
             pltpu.SemaphoreType.DMA((len(arrays), CHUNKS)),
             pltpu.SemaphoreType.DMA((len(outs), CHUNKS)),
         ],
-        compiler_params=pltpu.CompilerParams(vmem_limit_bytes=held + 6 * 2**20),
-        cost_estimate=pl.CostEstimate(flops=int(us * 1.1e9), bytes_accessed=moved, transcendentals=0),
-    )(*scalars, *tied, *after)
+        compiler_params=pltpu.CompilerParams(vmem_limit_bytes=room + 6 * 2**20),
+        cost_estimate=pl.CostEstimate(flops=int(us * 1.1e9), bytes_accessed=held, transcendentals=0),
+    )(*scalars, *tied, *(pltpu.with_memory_space_constraint(a, pltpu.HBM) for a in after))
 
 
 def shaped(shape, dtype=F32):
@@ -495,7 +509,7 @@
     got = exchange(send)
 
     own = exchange(jnp.broadcast_to(out_weight.T, (8, 8, D)), "z").reshape(HALF, D)
-    [inner] = call(inner_kernel, [wide], [x, b, c, row], us=0.3)
+    [inner] = call(inner_kernel, [wide_bf], [x, b, c, row], us=0.3)
     slices = shifts([own] * 4, "y")
     [ordered] = call(
         order_kernel, [shaped((T, D), BF16)], [at, *slices], smem=1, us=0.1, loose=slices, own=True, after=[inner]
@@ -511,28 +525,28 @@
         normed_grad_kernel,
         [wide_bf],
         [at, grad_rows, *pieces],
-        scratch=[pltpu.VMEM((T, D), BF16), pltpu.VMEM((8, T, D), BF16)],
+        scratch=[pltpu.VMEM((T, D), BF16), pltpu.VMEM((4, T, D), BF16)],
         own=True,
         smem=1,
         us=1.0,
-        loose=pieces,
-    )
-    grad_gate, grad_y, grad_start, normed, grad_send, gain_term, rate = call(
+        loose=[pieces[1], pieces[3], pieces[4]],
+        near=[pieces[k] for k in range(8) if k not in FAR_PIECES],
+    )
+    grad_gate, grad_y, grad_send, rate, own_term, other_term = call(
         norm_kernel,
-        [wide_bf, wide_bf, wide_bf, wide_bf, states, shaped((1, INNER)), shaped((T, W))],
-        [inner, grad_normed, gate, enter, c, row, gain_row],
-        scratch=[pltpu.VMEM((T, INNER), F32), pltpu.VMEM((T, INNER), F32)],
+        [wide_bf, wide_bf, states, shaped((T, W)), *[shaped((4, W + GAINROWS, INNER), BF16)] * 2],
+        [at, inner, grad_normed, gate, enter, c, row, gain_row, grad_rows],
+        scratch=[
+            pltpu.VMEM((T, INNER), F32),
+            pltpu.VMEM((T, INNER), F32),
+            pltpu.VMEM((T, INNER), BF16),
+            pltpu.VMEM((1, INNER), F32),
+        ],
+        smem=1,
         us=0.3,
         loose=[enter],
     )
     grad_got = exchange(grad_send)
-    own_term, other_term = call(
-        weight_kernel,
-        [shaped((4, W + GAINROWS, INNER), BF16)] * 2,
-        [at, grad_rows, normed, gain_term],
-        smem=1,
-        us=4.6,
-    )
     other_term = shift(other_term, "c", 1)
     block = shaped((W + GAINROWS, INNER), BF16)
     half = shaped((W + GAINROWS, D), BF16)
@@ -541,7 +555,7 @@
     )
     forth, back = shift(forth, "x", 1), shift(back, "x", -1)
     right, left = call(
-        relay_kernel, [block, block], [right, left, forth, back], us=2.8, loose=[forth, back]
+        relay_kernel, [block, block], [right, left, forth, back], us=2.8, near=[forth, back]
     )
     [leave_part] = call(
         backward_scan_kernel, [states], [grad_got, factor], us=2.0, loose=[grad_got], after=[right]
@@ -553,12 +567,12 @@
         [shaped((W, INNER), BF16), shaped((8, 2 * W))],
         [kept, right, left],
         us=2.6,
-        loose=[right, left],
+        near=[right, left],
     )
     grad_inner, grad_state_out, grad_b = call(
         pair_kernel,
         [wide, shaped((T, W), BF16), shaped((T, W))],
-        [x, grad_y, grad_start, b, c, row, enter],
+        [x, grad_y, b, c, row, enter],
         scratch=[pltpu.VMEM((T, T), F32)],
         us=5.8,
         loose=[enter],

time: 174 us -> 168 us (0.966)
  Pallas kernels: 52.5 us -> 49.2 us
  local copies, waits for them, and re-layouts: 7.38 us -> 4.63 us
    pallas_call x13 -> x12, Pallas kernels: 52.5 us -> 49.2 us  [call(): pl.pallas_call(run, out_shape=[pltpu.HBM(out.shape, out.dtype) for out in...]
    unnamed x8 -> x2, local copies, waits for them, and re-layouts: 2.7 us -> 0.01 us
  transfers between devices with their start and end apart: 21 -> 21, of which waited for: 13 -> 14; matrix products, arithmetic and copies ran while one was open for 2% -> 2% of each run, Pallas kernels for 23% -> 24%
where the time goes in v3:
time: 168 us; the launch traced here: 167 us
  starting transfers between devices  62.1 us (37%)
  waiting for transfers between devices  49.3 us (29%)
  Pallas kernels  49.2 us (29%)
  local copies, waits for them, and re-layouts  4.63 us (3%)
    pallas_call x12, Pallas kernels, call(): pl.pallas_call(run, out_shape=[pltpu.HBM(out.shape, out.dtype) for out in...  49.2 us
    all_to_all x6, starting transfers between devices, exchange(): return lax.all_to_all(value, axes, 0, 0, tiled=True)  47.1 us
    ppermute x15, waiting for transfers between devices, shift(): lax.ppermute(value, axis, [(i, (i + by) % size) for i in range(size)])  31.4 us
    all_to_all x6, waiting for transfers between devices, exchange(): return lax.all_to_all(value, axes, 0, 0, tiled=True)  17.8 us
    ppermute x15, starting transfers between devices, shift(): lax.ppermute(value, axis, [(i, (i + by) % size) for i in range(size)])  15 us
  transfers between devices with their start and end apart: 21, of which 14 were waited for; matrix products, arithmetic and copies ran while one was open for 2% of the time, Pallas kernels for 24%

profile of v3, /device:TPU:38, one launch (start us, length us, event | category | flops | bytes accessed | tf_op | source)
XLA Modules:
  0.0 167.1 jit_solution(5035652281792542104)
XLA Ops:
  2.0 8.6 %all-to-all-start = ((bf16[8,8,1024]{2,1,0:T(8,128)(2,1)}), bf16[8,8,1024]{2,1,0:T(8,128)(2,1)S(1)}, u32[]{:S(2)}, u32[]{:S(2)}) async-start(bf16[8,8,1024]{2,1,0:T(8,128)(2,1)} %broadcast_in_dim.21), calls=%async_computation | async-start | bytes 262144 | tf_op jit(solution)/shard_map/all_to_all | solution.py:492
  10.6 4.9 %shard_map.135 = (bf16[32,80,128]{2,1,0:T(8,128)(2,1)}, f32[16,256]{1,0:T(8,128)}) custom-call(bf16[256,2048]{1,0:T(8,128)(2,1)} %bitcast.27, bf16[256,128]{1,0:T(8,128)(2,1)} %bitcast.37, f32[16,256]{1,0:T(8,128)} %bitcast.41), custom_call_target="tpu_custom_call" | custom-call | flops 110000000 | bytes 1802240 | tf_op jit(solution)/shard_map/pallas_call | solution.py:460
  15.5 2.5 %all-to-all-done = bf16[8,8,1024]{2,1,0:T(8,128)(2,1)S(1)} async-done(((bf16[8,8,1024]{2,1,0:T(8,128)(2,1)}), bf16[8,8,1024]{2,1,0:T(8,128)(2,1)S(1)}, u32[]{:S(2)}, u32[]{:S(2)}) %all-to-all-start) | async-done | bytes 131104 | tf_op jit(solution)/shard_map/all_to_all | solution.py:492
  18.0 7.5 %all-to-all-start.1 = ((bf16[32,80,128]{2,1,0:T(8,128)(2,1)}), bf16[32,80,128]{2,1,0:T(8,128)(2,1)S(1)}, u32[]{:S(2)}, u32[]{:S(2)}) async-start(bf16[32,80,128]{2,1,0:T(8,128)(2,1)} %get-tuple-element.33.refs_7_), calls=%async_computation.1 | async-start | bytes 1310720 | tf_op jit(solution)/shard_map/all_to_all | solution.py:492
  25.6 2.8 %collective-permute-start.2 = (bf16[64,1024]{1,0:T(8,128)(2,1)S(1)}, bf16[64,1024]{1,0:T(8,128)(2,1)S(1)}, u32[]{:S(2)}, u32[]{:S(2)}) collective-permute-start(bf16[64,1024]{1,0:T(8,128)(2,1)S(1)} %bitcast.23), channel_id=1, source_target_pairs={{0,24},{8,0},{16,8},{24,16},{1,25},{9,1},{17,9},{25,17},{2,26},{10... | collective-permute-start | bytes 393224 | tf_op jit(solution)/shard_map/ppermute | solution.py:484
  30.0 4.5 %shard_map.136.refs_5_.refs_1_ = bf16[256,2048]{1,0:T(8,128)(2,1)} custom-call(bf16[256,2048]{1,0:T(8,128)(2,1)} %bitcast.28, bf16[256,128]{1,0:T(8,128)(2,1)} %bitcast.38, bf16[256,128]{1,0:T(8,128)(2,1)} %bitcast.34, f32[16,256]{1,0:T(8,128)} %get-tuple-element.32.refs_3_.refs_6_.refs_4_), custom_call_target="tpu_custom_call" | custom-call | flops 330000000 | bytes 2244608 | tf_op jit(solution)/shard_map/pallas_call | solution.py:460
  34.6 3.3 %collective-permute-done.2.refs_4_ = bf16[64,1024]{1,0:T(8,128)(2,1)S(1)} collective-permute-done((bf16[64,1024]{1,0:T(8,128)(2,1)S(1)}, bf16[64,1024]{1,0:T(8,128)(2,1)S(1)}, u32[]{:S(2)}, u32[]{:S(2)}) %collective-permute-start.2) | collective-permute-done | bytes 131104 | tf_op jit(solution)/shard_map/ppermute | solution.py:484
  38.4 2.5 %collective-permute-done.refs_2_ = bf16[64,1024]{1,0:T(8,128)(2,1)S(1)} collective-permute-done((bf16[64,1024]{1,0:T(8,128)(2,1)S(1)}, bf16[64,1024]{1,0:T(8,128)(2,1)S(1)}, u32[]{:S(2)}, u32[]{:S(2)}) %collective-permute-start) | collective-permute-done | bytes 131104 | tf_op jit(solution)/shard_map/ppermute | solution.py:484
  48.4 8.2 %all-to-all-start.2 = ((bf16[32,64,128]{2,1,0:T(8,128)(2,1)}), bf16[32,64,128]{2,1,0:T(8,128)(2,1)S(1)}, u32[]{:S(2)}, u32[]{:S(2)}) async-start(bf16[32,64,128]{2,1,0:T(8,128)(2,1)} %get-tuple-element.34), calls=%async_computation.2 | async-start | bytes 1048576 | tf_op jit(solution)/shard_map/all_to_all | solution.py:492
  56.7 12.2 %collective-permute-done.5.refs_5_ = bf16[256,1024]{1,0:T(8,128)(2,1)S(1)} collective-permute-done((bf16[256,1024]{1,0:T(8,128)(2,1)}, bf16[256,1024]{1,0:T(8,128)(2,1)S(1)}, u32[]{:S(2)}, u32[]{:S(2)}) %collective-permute-start.5) | collective-permute-done | bytes 524320 | tf_op jit(solution)/shard_map/ppermute | solution.py:484
  72.3 5.6 %shard_map.138.refs_2_ = bf16[256,2048]{1,0:T(8,128)(2,1)} custom-call(s32[3]{0:T(128)S(1)} %pad_add_fusion.refs_0_, bf16[256,1024]{1,0:T(8,128)(2,1)} %bitcast.31, bf16[256,1024]{1,0:T(8,128)(2,1)} %shard_map.137.refs_2_, bf16[256,1024]{1,0:T(8,128)(2,1)S(1)} %collective-permute-done.3.refs_3_, bf16[256,1024]{1,0:T(8,128)(2,1)S(1)} %collective-permute-done.4.refs_4_, ...), custom_call_target="tpu_custom_call" | custom-call | flops 1100000000 | bytes 5767168 | tf_op jit(solution)/shard_map/pallas_call | solution.py:460
  77.9 9.8 %shard_map.140 = (bf16[256,2048]{1,0:T(8,128)(2,1)}, bf16[256,2048]{1,0:T(8,128)(2,1)}, bf16[32,64,128]{2,1,0:T(8,128)(2,1)}, f32[256,128]{1,0:T(8,128)}, bf16[4...) custom-call(s32[3]{0:T(128)S(1)} %pad_add_fusion.refs_0_, bf16[256,2048]{1,0:T(8,128)(2,1)} %shard_map.136.refs_5_.refs_1_, ...), custom_call_target="tpu_custom_call" | custom-call | flops 330000000 | bytes 11755520 | tf_op jit(solution)/shard_map/pallas_call | solution.py:460
  87.9 8.3 %all-to-all-start.3 = ((bf16[32,64,128]{2,1,0:T(8,128)(2,1)}), bf16[32,64,128]{2,1,0:T(8,128)(2,1)S(1)}, u32[]{:S(2)}, u32[]{:S(2)}) async-start(bf16[32,64,128]{2,1,0:T(8,128)(2,1)} %get-tuple-element.36), calls=%async_computation.3 | async-start | bytes 1048576 | tf_op jit(solution)/shard_map/all_to_all | solution.py:492
  96.2 3.2 %shard_map.141 = (bf16[144,2048]{1,0:T(8,128)(2,1)}, bf16[144,2048]{1,0:T(8,128)(2,1)}, bf16[144,2048]{1,0:T(8,128)(2,1)}, bf16[144,1024]{1,0:T(8,128)(2,1)}, bf16[144,1024]{1,0:T(8,128)(2,1)}) custom-call(bf16[4,144,2048]{2,1,0:T(8,128)(2,1)} %get-tuple-element.38.refs_0_, bf16[4,144,2048]{2,1,0:T(8,128)(2,1)S(1)} %collective-permute-done.10.refs_1_), custom_call_target="tpu_custom_call" | custom-call | flops 4070000128 | bytes 7077888 | tf_op jit(solution)/shard_map/pallas_call | solution.py:460
  101.5 6.9 %collective-permute-done.11.refs_2_ = bf16[144,1024]{1,0:T(8,128)(2,1)S(1)} collective-permute-done((bf16[144,1024]{1,0:T(8,128)(2,1)}, bf16[144,1024]{1,0:T(8,128)(2,1)S(1)}, u32[]{:S(2)}, u32[]{:S(2)}) %collective-permute-start.11) | collective-permute-done | bytes 294944 | tf_op jit(solution)/shard_map/ppermute | solution.py:484
  108.4 2.7 %collective-permute-done.12.refs_3_ = bf16[144,1024]{1,0:T(8,128)(2,1)S(1)} collective-permute-done((bf16[144,1024]{1,0:T(8,128)(2,1)}, bf16[144,1024]{1,0:T(8,128)(2,1)S(1)}, u32[]{:S(2)}, u32[]{:S(2)}) %collective-permute-start.12) | collective-permute-done | bytes 294944 | tf_op jit(solution)/shard_map/ppermute | solution.py:484
  111.1 2.6 %shard_map.142 = (bf16[144,2048]{1,0:T(8,128)(2,1)}, bf16[144,2048]{1,0:T(8,128)(2,1)}) custom-call(bf16[144,2048]{1,0:T(8,128)(2,1)} %get-tuple-element.40.refs_0_, bf16[144,2048]{1,0:T(8,128)(2,1)} %get-tuple-element.41.refs_1_, bf16[144,1024]{1,0:T(8,128)(2,1)S(1)} %collective-permute-done.11.refs_2_, bf16[144,1024]{1,0:T(8,128)(2,1)S(1)} %collective-permute-done.12.refs_3_), custom_call_target="tpu_custom_call" | custom-call | flops 3080000000 | bytes 2949120 | tf_op jit(solution)/shard_map/pallas_call | solution.py:460
  113.8 3.2 %collective-permute-start.13 = (bf16[144,2048]{1,0:T(8,128)(2,1)}, bf16[144,2048]{1,0:T(8,128)(2,1)S(1)}, u32[]{:S(2)}, u32[]{:S(2)}) collective-permute-start(bf16[144,2048]{1,0:T(8,128)(2,1)} %get-tuple-element.44.refs_2_), channel_id=1, source_target_pairs={{0,64},{64,128},{128,192},{192,0},{1,65},{65,129},{129,193},{193,1... | collective-permute-start | bytes 1769480 | tf_op jit(solution)/shard_map/ppermute | solution.py:484
  118.7 9.8 %all-to-all-start.4 = ((bf16[32,64,128]{2,1,0:T(8,128)(2,1)}), bf16[32,64,128]{2,1,0:T(8,128)(2,1)S(1)}, u32[]{:S(2)}, u32[]{:S(2)}) async-start(bf16[32,64,128]{2,1,0:T(8,128)(2,1)} %shard_map.143.refs_6_), calls=%async_computation.4 | async-start | bytes 1048576 | tf_op jit(solution)/shard_map/all_to_all | solution.py:492
  134.3 10.1 %all-to-all-done.4.refs_1_ = bf16[32,64,128]{2,1,0:T(8,128)(2,1)S(1)} async-done(((bf16[32,64,128]{2,1,0:T(8,128)(2,1)}), bf16[32,64,128]{2,1,0:T(8,128)(2,1)S(1)}, u32[]{:S(2)}, u32[]{:S(2)}) %all-to-all-start.4) | async-done | bytes 524320 | tf_op jit(solution)/shard_map/all_to_all | solution.py:492
  144.3 4.8 %all-to-all-start.5 = ((bf16[32,72,128]{2,1,0:T(8,128)(2,1)}), bf16[32,72,128]{2,1,0:T(8,128)(2,1)S(1)}, u32[]{:S(2)}, u32[]{:S(2)}) async-start(bf16[32,72,128]{2,1,0:T(8,128)(2,1)} %fusion.1), calls=%async_computation.5 | async-start | bytes 1179648 | tf_op jit(solution)/shard_map/all_to_all | solution.py:492
  149.2 5.7 %shard_map.144 = (f32[256,2048]{1,0:T(8,128)}, bf16[256,128]{1,0:T(8,128)(2,1)}, f32[256,128]{1,0:T(8,128)}) custom-call(bf16[256,2048]{1,0:T(8,128)(2,1)} %bitcast.29, bf16[256,2048]{1,0:T(8,128)(2,1)} %get-tuple-element.35.refs_1_, bf16[256,128]{1,0:T(8,128)(2,1)} %bitcast.39, bf16[256,128]{1,0:T(8,128)(2,1)} %bitcast.36, ...), custom_call_target="tpu_custom_call" | custom-call | flops 6380000256 | bytes 5062656 | tf_op jit(solution)/shard_map/pallas_call | solution.py:460
  154.9 5.7 %shard_map.145 = (bf16[256,2048]{1,0:T(8,128)(2,1)}, bf16[256,128]{1,0:T(8,128)(2,1)}, f32[16,256]{1,0:T(8,128)}) custom-call(f32[256,2048]{1,0:T(8,128)} %get-tuple-element.45.refs_0_, bf16[32,64,128]{2,1,0:T(8,128)(2,1)S(1)} %all-to-all-done.4.refs_1_, bf16[256,128]{1,0:T(8,128)(2,1)} %bitcast.40, bf16[256,2048]{1,0:T(8,128)(2,1)} %bitcast.30, ...), custom_call_target="tpu_custom_call" | custom-call | flops 6049999872 | bytes 6324224 | tf_op jit(solution)/shard_map/pallas_call | solution.py:460
  160.6 5.3 %all-to-all-done.5 = bf16[32,72,128]{2,1,0:T(8,128)(2,1)S(1)} async-done(((bf16[32,72,128]{2,1,0:T(8,128)(2,1)}), bf16[32,72,128]{2,1,0:T(8,128)(2,1)S(1)}, u32[]{:S(2)}, u32[]{:S(2)}) %all-to-all-start.5) | async-done | bytes 589856 | tf_op jit(solution)/shard_map/all_to_all | solution.py:492
  (42 shorter events, 25.6 us)
Async XLA Ops:
  2.0 16.0 %all-to-all-start = ((bf16[8,8,1024]{2,1,0:T(8,128)(2,1)}), bf16[8,8,1024]{2,1,0:T(8,128)(2,1)S(1)}, u32[]{:S(2)}, u32[]{:S(2)}) async-start(bf16[8,8,1024]{2,1,0:T(8,128)(2,1)} %broadcast_in_dim.21), calls=%async_computation | async-start | bytes 262144 | tf_op jit(solution)/shard_map/all_to_all | solution.py:492
  18.0 28.5 %all-to-all-start.1 = ((bf16[32,80,128]{2,1,0:T(8,128)(2,1)}), bf16[32,80,128]{2,1,0:T(8,128)(2,1)S(1)}, u32[]{:S(2)}, u32[]{:S(2)}) async-start(bf16[32,80,128]{2,1,0:T(8,128)(2,1)} %get-tuple-element.33.refs_7_), calls=%async_computation.1 | async-start | bytes 1310720 | tf_op jit(solution)/shard_map/all_to_all | solution.py:492
  25.6 12.4 %collective-permute-start.2 = (bf16[64,1024]{1,0:T(8,128)(2,1)S(1)}, bf16[64,1024]{1,0:T(8,128)(2,1)S(1)}, u32[]{:S(2)}, u32[]{:S(2)}) collective-permute-start(bf16[64,1024]{1,0:T(8,128)(2,1)S(1)} %bitcast.23), channel_id=1, source_target_pairs={{0,24},{8,0},{16,8},{24,16},{1,25},{9,1},{17,9},{25,17},{2,26},{10... | collective-permute-start | bytes 393224 | tf_op jit(solution)/shard_map/ppermute | solution.py:484
  28.4 10.0 %collective-permute-start.1 = (bf16[64,1024]{1,0:T(8,128)(2,1)S(1)}, bf16[64,1024]{1,0:T(8,128)(2,1)S(1)}, u32[]{:S(2)}, u32[]{:S(2)}) collective-permute-start(bf16[64,1024]{1,0:T(8,128)(2,1)S(1)} %bitcast.24), channel_id=1, source_target_pairs={{0,16},{8,24},{16,0},{24,8},{1,17},{9,25},{17,1},{25,9},{2,18},{10... | collective-permute-start | bytes 393224 | tf_op jit(solution)/shard_map/ppermute | solution.py:484
  29.2 11.7 %collective-permute-start = (bf16[64,1024]{1,0:T(8,128)(2,1)S(1)}, bf16[64,1024]{1,0:T(8,128)(2,1)S(1)}, u32[]{:S(2)}, u32[]{:S(2)}) collective-permute-start(bf16[64,1024]{1,0:T(8,128)(2,1)S(1)} %bitcast.25), channel_id=1, source_target_pairs={{0,8},{8,16},{16,24},{24,0},{1,9},{9,17},{17,25},{25,1},{2,10},{10... | collective-permute-start | bytes 393224 | tf_op jit(solution)/shard_map/ppermute | solution.py:484
  42.4 14.1 %copy-start = (bf16[256,1024]{1,0:T(8,128)(2,1)S(1)}, bf16[256,1024]{1,0:T(8,128)(2,1)}, u32[]{:S(2)}) copy-start(bf16[256,1024]{1,0:T(8,128)(2,1)} %shard_map.137.refs_2_) | copy-start | bytes 1572868
  42.4 26.5 %collective-permute-start.5 = (bf16[256,1024]{1,0:T(8,128)(2,1)}, bf16[256,1024]{1,0:T(8,128)(2,1)S(1)}, u32[]{:S(2)}, u32[]{:S(2)}) collective-permute-start(bf16[256,1024]{1,0:T(8,128)(2,1)} %shard_map.137.refs_2_), channel_id=1, source_target_pairs={{0,192},{64,0},{128,64},{192,128},{1,193},{65,1},{129,65},{193,129... | collective-permute-start | bytes 1572872 | tf_op jit(solution)/shard_map/ppermute | solution.py:484
  43.3 25.6 %collective-permute-start.4 = (bf16[256,1024]{1,0:T(8,128)(2,1)}, bf16[256,1024]{1,0:T(8,128)(2,1)S(1)}, u32[]{:S(2)}, u32[]{:S(2)}) collective-permute-start(bf16[256,1024]{1,0:T(8,128)(2,1)} %shard_map.137.refs_2_), channel_id=1, source_target_pairs={{0,128},{64,192},{128,0},{192,64},{1,129},{65,193},{129,1},{193,65... | collective-permute-start | bytes 1572872 | tf_op jit(solution)/shard_map/ppermute | solution.py:484
  44.5 25.1 %collective-permute-start.3 = (bf16[256,1024]{1,0:T(8,128)(2,1)}, bf16[256,1024]{1,0:T(8,128)(2,1)S(1)}, u32[]{:S(2)}, u32[]{:S(2)}) collective-permute-start(bf16[256,1024]{1,0:T(8,128)(2,1)} %shard_map.137.refs_2_), channel_id=1, source_target_pairs={{0,64},{64,128},{128,192},{192,0},{1,65},{65,129},{129,193},{193,1... | collective-permute-start | bytes 1572872 | tf_op jit(solution)/shard_map/ppermute | solution.py:484
  48.4 29.5 %all-to-all-start.2 = ((bf16[32,64,128]{2,1,0:T(8,128)(2,1)}), bf16[32,64,128]{2,1,0:T(8,128)(2,1)S(1)}, u32[]{:S(2)}, u32[]{:S(2)}) async-start(bf16[32,64,128]{2,1,0:T(8,128)(2,1)} %get-tuple-element.34), calls=%async_computation.2 | async-start | bytes 1048576 | tf_op jit(solution)/shard_map/all_to_all | solution.py:492
  56.6 13.1 %collective-permute-start.6 = (bf16[256,1024]{1,0:T(8,128)(2,1)S(1)}, bf16[256,1024]{1,0:T(8,128)(2,1)S(1)}, u32[]{:S(2)}, u32[]{:S(2)}) collective-permute-start(bf16[256,1024]{1,0:T(8,128)(2,1)S(1)} %copy-done), channel_id=1, source_target_pairs={{0,32},{32,0},{1,33},{33,1},{2,34},{34,2},{3,35},{35,3},{4,36},{36... | collective-permute-start | bytes 1572872 | tf_op jit(solution)/shard_map/ppermute | solution.py:484
  68.9 1.9 %collective-permute-start.9 = (bf16[256,1024]{1,0:T(8,128)(2,1)S(1)}, bf16[256,1024]{1,0:T(8,128)(2,1)S(1)}, u32[]{:S(2)}, u32[]{:S(2)}) collective-permute-start(bf16[256,1024]{1,0:T(8,128)(2,1)S(1)} %collective-permute-done.5.refs_5_), channel_id=1, source_target_pairs={{0,32},{32,0},{1,33},{33,1},{2,34},{34,2},{3,35},{35,3},{4,36},{36... | collective-permute-start | bytes 1572872 | tf_op jit(solution)/shard_map/ppermute | solution.py:484
  68.9 2.7 %collective-permute-start.8 = (bf16[256,1024]{1,0:T(8,128)(2,1)S(1)}, bf16[256,1024]{1,0:T(8,128)(2,1)S(1)}, u32[]{:S(2)}, u32[]{:S(2)}) collective-permute-start(bf16[256,1024]{1,0:T(8,128)(2,1)S(1)} %collective-permute-done.4.refs_4_), channel_id=1, source_target_pairs={{0,32},{32,0},{1,33},{33,1},{2,34},{34,2},{3,35},{35,3},{4,36},{36... | collective-permute-start | bytes 1572872 | tf_op jit(solution)/shard_map/ppermute | solution.py:484
  69.5 2.8 %collective-permute-start.7 = (bf16[256,1024]{1,0:T(8,128)(2,1)S(1)}, bf16[256,1024]{1,0:T(8,128)(2,1)S(1)}, u32[]{:S(2)}, u32[]{:S(2)}) collective-permute-start(bf16[256,1024]{1,0:T(8,128)(2,1)S(1)} %collective-permute-done.3.refs_3_), channel_id=1, source_target_pairs={{0,32},{32,0},{1,33},{33,1},{2,34},{34,2},{3,35},{35,3},{4,36},{36... | collective-permute-start | bytes 1572872 | tf_op jit(solution)/shard_map/ppermute | solution.py:484
  87.7 8.5 %collective-permute-start.10 = (bf16[4,144,2048]{2,1,0:T(8,128)(2,1)}, bf16[4,144,2048]{2,1,0:T(8,128)(2,1)S(1)}, u32[]{:S(2)}, u32[]{:S(2)}) collective-permute-start(bf16[4,144,2048]{2,1,0:T(8,128)(2,1)} %get-tuple-element.39), channel_id=1, source_target_pairs={{0,32},{32,0},{1,33},{33,1},{2,34},{34,2},{3,35},{35,3},{4,36},{36... | collective-permute-start | bytes 7077896 | tf_op jit(solution)/shard_map/ppermute | solution.py:484
  87.9 29.1 %all-to-all-start.3 = ((bf16[32,64,128]{2,1,0:T(8,128)(2,1)}), bf16[32,64,128]{2,1,0:T(8,128)(2,1)S(1)}, u32[]{:S(2)}, u32[]{:S(2)}) async-start(bf16[32,64,128]{2,1,0:T(8,128)(2,1)} %get-tuple-element.36), calls=%async_computation.3 | async-start | bytes 1048576 | tf_op jit(solution)/shard_map/all_to_all | solution.py:492
  99.4 9.0 %collective-permute-start.11 = (bf16[144,1024]{1,0:T(8,128)(2,1)}, bf16[144,1024]{1,0:T(8,128)(2,1)S(1)}, u32[]{:S(2)}, u32[]{:S(2)}) collective-permute-start(bf16[144,1024]{1,0:T(8,128)(2,1)} %get-tuple-element.42), channel_id=1, source_target_pairs={{0,64},{64,128},{128,192},{192,0},{1,65},{65,129},{129,193},{193,1... | collective-permute-start | bytes 884744 | tf_op jit(solution)/shard_map/ppermute | solution.py:484
  101.3 9.9 %collective-permute-start.12 = (bf16[144,1024]{1,0:T(8,128)(2,1)}, bf16[144,1024]{1,0:T(8,128)(2,1)S(1)}, u32[]{:S(2)}, u32[]{:S(2)}) collective-permute-start(bf16[144,1024]{1,0:T(8,128)(2,1)} %get-tuple-element.43), channel_id=1, source_target_pairs={{0,192},{64,0},{128,64},{192,128},{1,193},{65,1},{129,65},{193,129... | collective-permute-start | bytes 884744 | tf_op jit(solution)/shard_map/ppermute | solution.py:484
  113.7 15.3 %collective-permute-start.14 = (bf16[144,2048]{1,0:T(8,128)(2,1)}, bf16[144,2048]{1,0:T(8,128)(2,1)S(1)}, u32[]{:S(2)}, u32[]{:S(2)}) collective-permute-start(bf16[144,2048]{1,0:T(8,128)(2,1)} %get-tuple-element.54), channel_id=1, source_target_pairs={{0,192},{64,0},{128,64},{192,128},{1,193},{65,1},{129,65},{193,129... | collective-permute-start | bytes 1769480 | tf_op jit(solution)/shard_map/ppermute | solution.py:484
  113.8 15.2 %collective-permute-start.13 = (bf16[144,2048]{1,0:T(8,128)(2,1)}, bf16[144,2048]{1,0:T(8,128)(2,1)S(1)}, u32[]{:S(2)}, u32[]{:S(2)}) collective-permute-start(bf16[144,2048]{1,0:T(8,128)(2,1)} %get-tuple-element.44.refs_2_), channel_id=1, source_target_pairs={{0,64},{64,128},{128,192},{192,0},{1,65},{65,129},{129,193},{193,1... | collective-permute-start | bytes 1769480 | tf_op jit(solution)/shard_map/ppermute | solution.py:484
  118.7 25.6 %all-to-all-start.4 = ((bf16[32,64,128]{2,1,0:T(8,128)(2,1)}), bf16[32,64,128]{2,1,0:T(8,128)(2,1)S(1)}, u32[]{:S(2)}, u32[]{:S(2)}) async-start(bf16[32,64,128]{2,1,0:T(8,128)(2,1)} %shard_map.143.refs_6_), calls=%async_computation.4 | async-start | bytes 1048576 | tf_op jit(solution)/shard_map/all_to_all | solution.py:492
  144.3 21.5 %all-to-all-start.5 = ((bf16[32,72,128]{2,1,0:T(8,128)(2,1)}), bf16[32,72,128]{2,1,0:T(8,128)(2,1)S(1)}, u32[]{:S(2)}, u32[]{:S(2)}) async-start(bf16[32,72,128]{2,1,0:T(8,128)(2,1)} %fusion.1), calls=%async_computation.5 | async-start | bytes 1179648 | tf_op jit(solution)/shard_map/all_to_all | solution.py:492

commit v4 on v3

--- a/solution.py
+++ b/solution.py
@@ -20,7 +20,6 @@
 GAINROWS = 16
 SEQ_AXES = ("y", "z")
 FAR = -1e30
-FAR_PIECES = (0, 4, 1, 3)
 HI = lax.Precision.HIGHEST
 
 
@@ -164,37 +163,19 @@
         copy.wait()
 
 
-def normed_grad_kernel(flow, at_ref, grad_far, *refs):
-    pieces, (out_ref, grad_ref, weight_ref, sems) = refs[:8], refs[8:]
-    x, c = at_ref[0], at_ref[1]
-    grad_copy = pltpu.make_async_copy(grad_far, grad_ref, sems.at[0, 0])
-    grad_copy.start()
-    copies = {}
-    for slot, at in enumerate(FAR_PIECES):
-        copies[at] = (pltpu.make_async_copy(pieces[at], weight_ref.at[slot], sems.at[1 + slot, 0]), slot)
-        copies[at][0].start()
-    grad_copy.wait()
-    for at in (*(k for k in range(8) if k not in FAR_PIECES), *FAR_PIECES):
-        if at in copies:
-            copies[at][0].wait()
-        weight = weight_ref[copies[at][1]] if at in copies else pieces[at][...]
-        block = lax.rem(x + 4 - at % 4, 4) * 2 + (c if at < 4 else 1 - c)
-        out_ref[:, lane(block, 2 * W)] = dot(grad_ref[...], weight, 1, 1).astype(BF16)
-    for h in range(CHUNKS):
-        for k in flow.outgoing.where(True):
-            flow.outgoing.copy(k, h).start()
-
-
-def norm_kernel(
-    flow, at_ref, inner_ref, gn_ref, gate_ref, enter_ref, c_ref, row_ref, gain_ref, rows_ref,
-    gate_out, grad_out, send_ref, rate_out, own_ref, other_ref, y_ref, sig_ref, normed_out, gain_out,
-):
+def norm_kernel(flow, at_ref, inner_ref, gate_ref, enter_ref, c_ref, row_ref, gain_ref, rows_ref, *refs):
+    pieces, refs = refs[:8], refs[8:]
+    gate_out, grad_out, send_ref, rate_out, own_ref, other_ref = refs[:6]
+    y_ref, sig_ref, normed_out, gain_out, gn_ref, weight_ref, sems = refs[6:]
+    x, core = at_ref[0], at_ref[1]
+    copies = [pltpu.make_async_copy(pieces[k], weight_ref.at[k], sems.at[k]) for k in range(8)]
+    for copy in copies:
+        copy.start()
     flow.arrive()
     c = c_ref[...]
 
-    def first(h, sums):
+    def first(h, squares):
         flow.arrive(h)
-        squares, mixed = sums
         cols = lane(h, 2 * W)
         keep = pair_starts(row_ref, h)
         y = inner_ref[:, cols].astype(F32) + keep * dot(c, pair_state(enter_ref, h))
@@ -203,15 +184,24 @@
         u = y * (gate * sig)
         y_ref[:, cols] = y
         sig_ref[:, cols] = sig
-        both = gain_ref[:, cols] * gn_ref[:, cols].astype(F32) * u
         squared = u * u
-        return (
-            squares + squared[:, :W] + squared[:, W:],
-            mixed + both[:, :W] + both[:, W:],
-        )
+        return squares + squared[:, :W] + squared[:, W:]
+
+    def second(h, mixed):
+        cols = lane(h, 2 * W)
+        other = jnp.abs(lax.rem(h, 2) - core)
+        slot = 4 * other + lax.rem(x + 4 - lax.div(h, 2), 4)
+        gn = dot(rows_ref[...], weight_ref[slot], 1, 1)
+        gn_ref[:, cols] = gn
+        u = y_ref[:, cols] * (gate_ref[:, cols].astype(F32) * sig_ref[:, cols])
+        both = gain_ref[:, cols] * gn * u
+        return mixed + both[:, :W] + both[:, W:]
 
     zero = jnp.zeros((T, W), F32)
-    squares, mixed = lax.fori_loop(0, H // 2, first, (zero, zero))
+    squares = lax.fori_loop(0, H // 2, first, zero)
+    for copy in copies:
+        copy.wait()
+    mixed = lax.fori_loop(0, H // 2, second, zero)
     rstd = lax.rsqrt(row_sum(squares) / INNER + 1e-5)
     pull = rstd * rstd * rstd * (row_sum(mixed) / INNER)
     rate_out[...] = zero
@@ -219,7 +209,7 @@
     @pl.loop(0, H // 2)
     def _(h):
         cols = lane(h, 2 * W)
-        y, sig, gn = y_ref[:, cols], sig_ref[:, cols], gn_ref[:, cols].astype(F32)
+        y, sig, gn = y_ref[:, cols], sig_ref[:, cols], gn_ref[:, cols]
         gain = gain_ref[:, cols]
         gate = gate_ref[:, cols].astype(F32)
         active = gate * sig
@@ -241,7 +231,6 @@
         flow.leave(h)
 
     flow.leave()
-    x, core = at_ref[0], at_ref[1]
     normed = normed_out[...]
     for at, out, target in ((5, other_ref, 1 - core), (4, own_ref, core)):
         for k in range(4):
@@ -428,12 +417,13 @@
                 self.outgoing.copy(k, h).wait()
 
 
-def call(kernel, outs, args, scratch=(), smem=0, us=1.0, loose=(), after=(), own=False, near=()):
+def call(kernel, outs, args, scratch=(), smem=0, us=1.0, loose=(), after=(), own=False, near=(), raw=()):
     scalars, arrays = args[:smem], args[smem:]
     held = sum(a.size * a.dtype.itemsize for a in (*arrays, *outs))
     room = held + sum(math.prod(s.shape) * 4 for s in scratch)
     spaces = [next((space for group, space in ((near, pltpu.VMEM), (loose, pl.ANY)) if any(a is b for b in group)), pltpu.HBM) for a in arrays]
-    kept = [] if own else [a for a, space in zip(arrays, spaces) if space is not pltpu.VMEM]
+    direct = [space is pltpu.VMEM or any(a is b for b in raw) for a, space in zip(arrays, spaces)]
+    kept = [] if own else [a for a, skip in zip(arrays, direct) if not skip]
     counts = (smem, len(arrays), len(after), len(outs), len(kept), len(outs), len(scratch))
 
     def run(*refs):
@@ -442,14 +432,14 @@
             groups.append(refs[:count])
             refs = refs[count:]
         numbers, sources, _, targets, copies, near_out, rest = groups
-        far = [source for source, space in zip(sources, spaces) if space is not pltpu.VMEM]
+        far = [source for source, skip in zip(sources, direct) if not skip]
         flow = Flow(Traffic(far, copies, refs[0]), Traffic(near_out, targets, refs[1]))
         if own:
             kernel(flow, *numbers, *sources, *near_out, *rest, refs[0])
         else:
             flow.begin()
             copies = list(copies)
-            near_in = [s if space is pltpu.VMEM else copies.pop(0) for s, space in zip(sources, spaces)]
+            near_in = [source if skip else copies.pop(0) for source, skip in zip(sources, direct)]
             kernel(flow, *numbers, *near_in, *near_out, *rest)
         flow.end()
 
@@ -521,30 +511,23 @@
         forward_scan_kernel, [states, shaped((SEQ, W))], [got], us=0.1, loose=[got]
     )
     enter = exchange(enter_part)
-    [grad_normed] = call(
-        normed_grad_kernel,
-        [wide_bf],
-        [at, grad_rows, *pieces],
-        scratch=[pltpu.VMEM((T, D), BF16), pltpu.VMEM((4, T, D), BF16)],
-        own=True,
-        smem=1,
-        us=1.0,
-        loose=[pieces[1], pieces[3], pieces[4]],
-        near=[pieces[k] for k in range(8) if k not in FAR_PIECES],
-    )
     grad_gate, grad_y, grad_send, rate, own_term, other_term = call(
         norm_kernel,
         [wide_bf, wide_bf, states, shaped((T, W)), *[shaped((4, W + GAINROWS, INNER), BF16)] * 2],
-        [at, inner, grad_normed, gate, enter, c, row, gain_row, grad_rows],
+        [at, inner, gate, enter, c, row, gain_row, grad_rows, *pieces],
         scratch=[
             pltpu.VMEM((T, INNER), F32),
             pltpu.VMEM((T, INNER), F32),
             pltpu.VMEM((T, INNER), BF16),
             pltpu.VMEM((1, INNER), F32),
+            pltpu.VMEM((T, INNER), F32),
+            pltpu.VMEM((8, T, D), BF16),
+            pltpu.SemaphoreType.DMA((8,)),
         ],
         smem=1,
-        us=0.3,
-        loose=[enter],
+        us=1.3,
+        loose=[enter, *pieces[1:5], pieces[7]],
+        raw=pieces,
     )
     grad_got = exchange(grad_send)
     other_term = shift(other_term, "c", 1)

time: 168 us -> 166 us (0.988)
  Pallas kernels: 49.2 us -> 46.2 us
    pallas_call x12 -> x11, Pallas kernels: 49.2 us -> 46.2 us  [call(): pl.pallas_call(run, out_shape=[pltpu.HBM(out.shape, out.dtype) for out in...]
  transfers between devices with their start and end apart: 21 -> 21, of which waited for: 14 -> 14; matrix products, arithmetic and copies ran while one was open for 2% -> 2% of each run, Pallas kernels for 24% -> 21%
where the time goes in v4:
time: 166 us; the launch traced here: 165 us
  starting transfers between devices  61.6 us (37%)
  waiting for transfers between devices  49.3 us (30%)
  Pallas kernels  46.2 us (28%)
  local copies, waits for them, and re-layouts  5.46 us (3%)
    all_to_all x6, starting transfers between devices, exchange(): return lax.all_to_all(value, axes, 0, 0, tiled=True)  46.9 us
    pallas_call x11, Pallas kernels, call(): pl.pallas_call(run, out_shape=[pltpu.HBM(out.shape, out.dtype) for out in...  46.2 us
    ppermute x15, waiting for transfers between devices, shift(): lax.ppermute(value, axis, [(i, (i + by) % size) for i in range(size)])  31 us
    all_to_all x6, waiting for transfers between devices, exchange(): return lax.all_to_all(value, axes, 0, 0, tiled=True)  18.3 us
    ppermute x15, starting transfers between devices, shift(): lax.ppermute(value, axis, [(i, (i + by) % size) for i in range(size)])  14.7 us
  transfers between devices with their start and end apart: 21, of which 14 were waited for; matrix products, arithmetic and copies ran while one was open for 2% of the time, Pallas kernels for 21%

profile of v4, /device:TPU:38, one launch (start us, length us, event | category | flops | bytes accessed | tf_op | source)
XLA Modules:
  0.0 164.5 jit_solution(11257815611290168426)
XLA Ops:
  2.0 8.6 %all-to-all-start.2 = ((bf16[8,8,1024]{2,1,0:T(8,128)(2,1)}), bf16[8,8,1024]{2,1,0:T(8,128)(2,1)S(1)}, u32[]{:S(2)}, u32[]{:S(2)}) async-start(bf16[8,8,1024]{2,1,0:T(8,128)(2,1)} %broadcast_in_dim.22), calls=%async_computation.2 | async-start | bytes 262144 | tf_op jit(solution)/shard_map/all_to_all | solution.py:482
  10.6 4.9 %shard_map.135 = (bf16[32,80,128]{2,1,0:T(8,128)(2,1)}, f32[16,256]{1,0:T(8,128)}) custom-call(bf16[256,2048]{1,0:T(8,128)(2,1)} %bitcast.27, bf16[256,128]{1,0:T(8,128)(2,1)} %bitcast.36, f32[16,256]{1,0:T(8,128)} %bitcast.40), custom_call_target="tpu_custom_call" | custom-call | flops 110000000 | bytes 1802240 | tf_op jit(solution)/shard_map/pallas_call | solution.py:450
  15.5 2.5 %all-to-all-done.2 = bf16[8,8,1024]{2,1,0:T(8,128)(2,1)S(1)} async-done(((bf16[8,8,1024]{2,1,0:T(8,128)(2,1)}), bf16[8,8,1024]{2,1,0:T(8,128)(2,1)S(1)}, u32[]{:S(2)}, u32[]{:S(2)}) %all-to-all-start.2) | async-done | bytes 131104 | tf_op jit(solution)/shard_map/all_to_all | solution.py:482
  18.0 7.5 %all-to-all-start = ((bf16[32,80,128]{2,1,0:T(8,128)(2,1)}), bf16[32,80,128]{2,1,0:T(8,128)(2,1)S(1)}, u32[]{:S(2)}, u32[]{:S(2)}) async-start(bf16[32,80,128]{2,1,0:T(8,128)(2,1)} %get-tuple-element.33.refs_7_), calls=%async_computation | async-start | bytes 1310720 | tf_op jit(solution)/shard_map/all_to_all | solution.py:482
  25.5 2.8 %collective-permute-start.2 = (bf16[64,1024]{1,0:T(8,128)(2,1)S(1)}, bf16[64,1024]{1,0:T(8,128)(2,1)S(1)}, u32[]{:S(2)}, u32[]{:S(2)}) collective-permute-start(bf16[64,1024]{1,0:T(8,128)(2,1)S(1)} %bitcast.23), channel_id=1, source_target_pairs={{0,24},{8,0},{16,8},{24,16},{1,25},{9,1},{17,9},{25,17},{2,26},{10... | collective-permute-start | bytes 393224 | tf_op jit(solution)/shard_map/ppermute | solution.py:474
  30.0 4.5 %shard_map.136.refs_5_.refs_1_ = bf16[256,2048]{1,0:T(8,128)(2,1)} custom-call(bf16[256,2048]{1,0:T(8,128)(2,1)} %bitcast.28, bf16[256,128]{1,0:T(8,128)(2,1)} %bitcast.37, bf16[256,128]{1,0:T(8,128)(2,1)} %bitcast.33, f32[16,256]{1,0:T(8,128)} %get-tuple-element.32.refs_3_.refs_5_.refs_4_), custom_call_target="tpu_custom_call" | custom-call | flops 330000000 | bytes 2244608 | tf_op jit(solution)/shard_map/pallas_call | solution.py:450
  34.6 3.4 %collective-permute-done.2.refs_4_ = bf16[64,1024]{1,0:T(8,128)(2,1)S(1)} collective-permute-done((bf16[64,1024]{1,0:T(8,128)(2,1)S(1)}, bf16[64,1024]{1,0:T(8,128)(2,1)S(1)}, u32[]{:S(2)}, u32[]{:S(2)}) %collective-permute-start.2) | collective-permute-done | bytes 131104 | tf_op jit(solution)/shard_map/ppermute | solution.py:474
  38.4 2.5 %collective-permute-done.refs_2_ = bf16[64,1024]{1,0:T(8,128)(2,1)S(1)} collective-permute-done((bf16[64,1024]{1,0:T(8,128)(2,1)S(1)}, bf16[64,1024]{1,0:T(8,128)(2,1)S(1)}, u32[]{:S(2)}, u32[]{:S(2)}) %collective-permute-start) | collective-permute-done | bytes 131104 | tf_op jit(solution)/shard_map/ppermute | solution.py:474
  44.4 2.1 %collective-permute-start.3 = (bf16[256,1024]{1,0:T(8,128)(2,1)}, bf16[256,1024]{1,0:T(8,128)(2,1)S(1)}, u32[]{:S(2)}, u32[]{:S(2)}) collective-permute-start(bf16[256,1024]{1,0:T(8,128)(2,1)} %shard_map.138.refs_8_), channel_id=1, source_target_pairs={{0,64},{64,128},{128,192},{192,0},{1,65},{65,129},{129,193},{193,1... | collective-permute-start | bytes 1572872 | tf_op jit(solution)/shard_map/ppermute | solution.py:474
  48.4 8.1 %all-to-all-start.1 = ((bf16[32,64,128]{2,1,0:T(8,128)(2,1)}), bf16[32,64,128]{2,1,0:T(8,128)(2,1)S(1)}, u32[]{:S(2)}, u32[]{:S(2)}) async-start(bf16[32,64,128]{2,1,0:T(8,128)(2,1)} %get-tuple-element.34), calls=%async_computation.1 | async-start | bytes 1048576 | tf_op jit(solution)/shard_map/all_to_all | solution.py:482
  56.6 12.3 %collective-permute-done.5.refs_11_ = bf16[256,1024]{1,0:T(8,128)(2,1)S(1)} collective-permute-done((bf16[256,1024]{1,0:T(8,128)(2,1)}, bf16[256,1024]{1,0:T(8,128)(2,1)S(1)}, u32[]{:S(2)}, u32[]{:S(2)}) %collective-permute-start.5) | collective-permute-done | bytes 524320 | tf_op jit(solution)/shard_map/ppermute | solution.py:474
  73.5 12.4 %shard_map.139 = (bf16[256,2048]{1,0:T(8,128)(2,1)}, bf16[256,2048]{1,0:T(8,128)(2,1)}, bf16[32,64,128]{2,1,0:T(8,128)(2,1)}, f32[256,128]{1,0:T(8,128)}, bf16[4...) custom-call(s32[3]{0:T(128)S(1)} %pad_add_fusion.refs_0_, bf16[256,2048]{1,0:T(8,128)(2,1)} %shard_map.136.refs_5_.refs_1_, ...), custom_call_target="tpu_custom_call" | custom-call | flops 1430000000 | bytes 14901248 | tf_op jit(solution)/shard_map/pallas_call | solution.py:450
  86.0 8.1 %all-to-all-start.3 = ((bf16[32,64,128]{2,1,0:T(8,128)(2,1)}), bf16[32,64,128]{2,1,0:T(8,128)(2,1)S(1)}, u32[]{:S(2)}, u32[]{:S(2)}) async-start(bf16[32,64,128]{2,1,0:T(8,128)(2,1)} %get-tuple-element.36), calls=%async_computation.3 | async-start | bytes 1048576 | tf_op jit(solution)/shard_map/all_to_all | solution.py:482
  94.1 3.2 %shard_map.140 = (bf16[144,2048]{1,0:T(8,128)(2,1)}, bf16[144,2048]{1,0:T(8,128)(2,1)}, bf16[144,2048]{1,0:T(8,128)(2,1)}, bf16[144,1024]{1,0:T(8,128)(2,1)}, bf16[144,1024]{1,0:T(8,128)(2,1)}) custom-call(bf16[4,144,2048]{2,1,0:T(8,128)(2,1)} %get-tuple-element.38.refs_0_, bf16[4,144,2048]{2,1,0:T(8,128)(2,1)S(1)} %collective-permute-done.10.refs_1_), custom_call_target="tpu_custom_call" | custom-call | flops 4070000128 | bytes 7077888 | tf_op jit(solution)/shard_map/pallas_call | solution.py:450
  99.4 6.9 %collective-permute-done.11.refs_2_ = bf16[144,1024]{1,0:T(8,128)(2,1)S(1)} collective-permute-done((bf16[144,1024]{1,0:T(8,128)(2,1)}, bf16[144,1024]{1,0:T(8,128)(2,1)S(1)}, u32[]{:S(2)}, u32[]{:S(2)}) %collective-permute-start.11) | collective-permute-done | bytes 294944 | tf_op jit(solution)/shard_map/ppermute | solution.py:474
  108.4 2.6 %shard_map.141 = (bf16[144,2048]{1,0:T(8,128)(2,1)}, bf16[144,2048]{1,0:T(8,128)(2,1)}) custom-call(bf16[144,2048]{1,0:T(8,128)(2,1)} %get-tuple-element.40.refs_0_, bf16[144,2048]{1,0:T(8,128)(2,1)} %get-tuple-element.41.refs_1_, bf16[144,1024]{1,0:T(8,128)(2,1)S(1)} %collective-permute-done.11.refs_2_, bf16[144,1024]{1,0:T(8,128)(2,1)S(1)} %collective-permute-done.12.refs_3_), custom_call_target="tpu_custom_call" | custom-call | flops 3080000000 | bytes 2949120 | tf_op jit(solution)/shard_map/pallas_call | solution.py:450
  111.0 3.2 %collective-permute-start.13 = (bf16[144,2048]{1,0:T(8,128)(2,1)}, bf16[144,2048]{1,0:T(8,128)(2,1)S(1)}, u32[]{:S(2)}, u32[]{:S(2)}) collective-permute-start(bf16[144,2048]{1,0:T(8,128)(2,1)} %get-tuple-element.44.refs_2_), channel_id=1, source_target_pairs={{0,64},{64,128},{128,192},{192,0},{1,65},{65,129},{129,193},{193,1... | collective-permute-start | bytes 1769480 | tf_op jit(solution)/shard_map/ppermute | solution.py:474
  115.9 9.8 %all-to-all-start.4 = ((bf16[32,64,128]{2,1,0:T(8,128)(2,1)}), bf16[32,64,128]{2,1,0:T(8,128)(2,1)S(1)}, u32[]{:S(2)}, u32[]{:S(2)}) async-start(bf16[32,64,128]{2,1,0:T(8,128)(2,1)} %shard_map.142.refs_6_), calls=%async_computation.4 | async-start | bytes 1048576 | tf_op jit(solution)/shard_map/all_to_all | solution.py:482
  126.4 2.2 %shard_map.145 = (bf16[128,2048]{1,0:T(8,128)(2,1)}, f32[8,256]{1,0:T(8,128)}) custom-call(bf16[144,2048]{1,0:T(8,128)(2,1)} %get-tuple-element.53.refs_0_, bf16[144,2048]{1,0:T(8,128)(2,1)S(1)} %collective-permute-done.13.refs_1_, bf16[144,2048]{1,0:T(8,128)(2,1)S(1)} %collective-permute-done.14.refs_2_), custom_call_target="tpu_custom_call" | custom-call | flops 2860000000 | bytes 2301952 | tf_op jit(solution)/shard_map/pallas_call | solution.py:450
  131.6 10.1 %all-to-all-done.4.refs_1_ = bf16[32,64,128]{2,1,0:T(8,128)(2,1)S(1)} async-done(((bf16[32,64,128]{2,1,0:T(8,128)(2,1)}), bf16[32,64,128]{2,1,0:T(8,128)(2,1)S(1)}, u32[]{:S(2)}, u32[]{:S(2)}) %all-to-all-start.4) | async-done | bytes 524320 | tf_op jit(solution)/shard_map/all_to_all | solution.py:482
  141.7 4.8 %all-to-all-start.5 = ((bf16[32,72,128]{2,1,0:T(8,128)(2,1)}), bf16[32,72,128]{2,1,0:T(8,128)(2,1)S(1)}, u32[]{:S(2)}, u32[]{:S(2)}) async-start(bf16[32,72,128]{2,1,0:T(8,128)(2,1)} %fusion.1), calls=%async_computation.5 | async-start | bytes 1179648 | tf_op jit(solution)/shard_map/all_to_all | solution.py:482
  146.5 5.7 %shard_map.143 = (f32[256,2048]{1,0:T(8,128)}, bf16[256,128]{1,0:T(8,128)(2,1)}, f32[256,128]{1,0:T(8,128)}) custom-call(bf16[256,2048]{1,0:T(8,128)(2,1)} %bitcast.29, bf16[256,2048]{1,0:T(8,128)(2,1)} %get-tuple-element.35.refs_1_, bf16[256,128]{1,0:T(8,128)(2,1)} %bitcast.38, bf16[256,128]{1,0:T(8,128)(2,1)} %bitcast.35, ...), custom_call_target="tpu_custom_call" | custom-call | flops 6380000256 | bytes 5062656 | tf_op jit(solution)/shard_map/pallas_call | solution.py:450
  152.2 5.7 %shard_map.144 = (bf16[256,2048]{1,0:T(8,128)(2,1)}, bf16[256,128]{1,0:T(8,128)(2,1)}, f32[16,256]{1,0:T(8,128)}) custom-call(f32[256,2048]{1,0:T(8,128)} %get-tuple-element.45.refs_0_, bf16[32,64,128]{2,1,0:T(8,128)(2,1)S(1)} %all-to-all-done.4.refs_1_, bf16[256,128]{1,0:T(8,128)(2,1)} %bitcast.39, bf16[256,2048]{1,0:T(8,128)(2,1)} %bitcast.30, ...), custom_call_target="tpu_custom_call" | custom-call | flops 6049999872 | bytes 6324224 | tf_op jit(solution)/shard_map/pallas_call | solution.py:450
  157.9 5.3 %all-to-all-done.5 = bf16[32,72,128]{2,1,0:T(8,128)(2,1)S(1)} async-done(((bf16[32,72,128]{2,1,0:T(8,128)(2,1)}), bf16[32,72,128]{2,1,0:T(8,128)(2,1)S(1)}, u32[]{:S(2)}, u32[]{:S(2)}) %all-to-all-start.5) | async-done | bytes 589856 | tf_op jit(solution)/shard_map/all_to_all | solution.py:482
  (41 shorter events, 24.5 us)
Async XLA Ops:
  2.0 16.0 %all-to-all-start.2 = ((bf16[8,8,1024]{2,1,0:T(8,128)(2,1)}), bf16[8,8,1024]{2,1,0:T(8,128)(2,1)S(1)}, u32[]{:S(2)}, u32[]{:S(2)}) async-start(bf16[8,8,1024]{2,1,0:T(8,128)(2,1)} %broadcast_in_dim.22), calls=%async_computation.2 | async-start | bytes 262144 | tf_op jit(solution)/shard_map/all_to_all | solution.py:482
  18.0 28.5 %all-to-all-start = ((bf16[32,80,128]{2,1,0:T(8,128)(2,1)}), bf16[32,80,128]{2,1,0:T(8,128)(2,1)S(1)}, u32[]{:S(2)}, u32[]{:S(2)}) async-start(bf16[32,80,128]{2,1,0:T(8,128)(2,1)} %get-tuple-element.33.refs_7_), calls=%async_computation | async-start | bytes 1310720 | tf_op jit(solution)/shard_map/all_to_all | solution.py:482
  25.5 12.4 %collective-permute-start.2 = (bf16[64,1024]{1,0:T(8,128)(2,1)S(1)}, bf16[64,1024]{1,0:T(8,128)(2,1)S(1)}, u32[]{:S(2)}, u32[]{:S(2)}) collective-permute-start(bf16[64,1024]{1,0:T(8,128)(2,1)S(1)} %bitcast.23), channel_id=1, source_target_pairs={{0,24},{8,0},{16,8},{24,16},{1,25},{9,1},{17,9},{25,17},{2,26},{10... | collective-permute-start | bytes 393224 | tf_op jit(solution)/shard_map/ppermute | solution.py:474
  28.3 10.0 %collective-permute-start.1 = (bf16[64,1024]{1,0:T(8,128)(2,1)S(1)}, bf16[64,1024]{1,0:T(8,128)(2,1)S(1)}, u32[]{:S(2)}, u32[]{:S(2)}) collective-permute-start(bf16[64,1024]{1,0:T(8,128)(2,1)S(1)} %bitcast.24), channel_id=1, source_target_pairs={{0,16},{8,24},{16,0},{24,8},{1,17},{9,25},{17,1},{25,9},{2,18},{10... | collective-permute-start | bytes 393224 | tf_op jit(solution)/shard_map/ppermute | solution.py:474
  29.2 11.7 %collective-permute-start = (bf16[64,1024]{1,0:T(8,128)(2,1)S(1)}, bf16[64,1024]{1,0:T(8,128)(2,1)S(1)}, u32[]{:S(2)}, u32[]{:S(2)}) collective-permute-start(bf16[64,1024]{1,0:T(8,128)(2,1)S(1)} %bitcast.25), channel_id=1, source_target_pairs={{0,8},{8,16},{16,24},{24,0},{1,9},{9,17},{17,25},{25,1},{2,10},{10... | collective-permute-start | bytes 393224 | tf_op jit(solution)/shard_map/ppermute | solution.py:474
  42.4 26.5 %collective-permute-start.5 = (bf16[256,1024]{1,0:T(8,128)(2,1)}, bf16[256,1024]{1,0:T(8,128)(2,1)S(1)}, u32[]{:S(2)}, u32[]{:S(2)}) collective-permute-start(bf16[256,1024]{1,0:T(8,128)(2,1)} %shard_map.138.refs_8_), channel_id=1, source_target_pairs={{0,192},{64,0},{128,64},{192,128},{1,193},{65,1},{129,65},{193,129... | collective-permute-start | bytes 1572872 | tf_op jit(solution)/shard_map/ppermute | solution.py:474
  43.3 25.6 %collective-permute-start.4 = (bf16[256,1024]{1,0:T(8,128)(2,1)}, bf16[256,1024]{1,0:T(8,128)(2,1)S(1)}, u32[]{:S(2)}, u32[]{:S(2)}) collective-permute-start(bf16[256,1024]{1,0:T(8,128)(2,1)} %shard_map.138.refs_8_), channel_id=1, source_target_pairs={{0,128},{64,192},{128,0},{192,64},{1,129},{65,193},{129,1},{193,65... | collective-permute-start | bytes 1572872 | tf_op jit(solution)/shard_map/ppermute | solution.py:474
  44.4 25.1 %collective-permute-start.3 = (bf16[256,1024]{1,0:T(8,128)(2,1)}, bf16[256,1024]{1,0:T(8,128)(2,1)S(1)}, u32[]{:S(2)}, u32[]{:S(2)}) collective-permute-start(bf16[256,1024]{1,0:T(8,128)(2,1)} %shard_map.138.refs_8_), channel_id=1, source_target_pairs={{0,64},{64,128},{128,192},{192,0},{1,65},{65,129},{129,193},{193,1... | collective-permute-start | bytes 1572872 | tf_op jit(solution)/shard_map/ppermute | solution.py:474
  48.4 25.1 %all-to-all-start.1 = ((bf16[32,64,128]{2,1,0:T(8,128)(2,1)}), bf16[32,64,128]{2,1,0:T(8,128)(2,1)S(1)}, u32[]{:S(2)}, u32[]{:S(2)}) async-start(bf16[32,64,128]{2,1,0:T(8,128)(2,1)} %get-tuple-element.34), calls=%async_computation.1 | async-start | bytes 1048576 | tf_op jit(solution)/shard_map/all_to_all | solution.py:482
  56.5 13.0 %collective-permute-start.6 = (bf16[256,1024]{1,0:T(8,128)(2,1)}, bf16[256,1024]{1,0:T(8,128)(2,1)S(1)}, u32[]{:S(2)}, u32[]{:S(2)}) collective-permute-start(bf16[256,1024]{1,0:T(8,128)(2,1)} %shard_map.138.refs_8_), channel_id=1, source_target_pairs={{0,32},{32,0},{1,33},{33,1},{2,34},{34,2},{3,35},{35,3},{4,36},{36... | collective-permute-start | bytes 1572872 | tf_op jit(solution)/shard_map/ppermute | solution.py:474
  68.9 1.9 %collective-permute-start.9 = (bf16[256,1024]{1,0:T(8,128)(2,1)S(1)}, bf16[256,1024]{1,0:T(8,128)(2,1)S(1)}, u32[]{:S(2)}, u32[]{:S(2)}) collective-permute-start(bf16[256,1024]{1,0:T(8,128)(2,1)S(1)} %collective-permute-done.5.refs_11_), channel_id=1, source_target_pairs={{0,32},{32,0},{1,33},{33,1},{2,34},{34,2},{3,35},{35,3},{4,36},{36... | collective-permute-start | bytes 1572872 | tf_op jit(solution)/shard_map/ppermute | solution.py:474
  68.9 3.4 %collective-permute-start.8 = (bf16[256,1024]{1,0:T(8,128)(2,1)S(1)}, bf16[256,1024]{1,0:T(8,128)(2,1)S(1)}, u32[]{:S(2)}, u32[]{:S(2)}) collective-permute-start(bf16[256,1024]{1,0:T(8,128)(2,1)S(1)} %collective-permute-done.4.refs_10_), channel_id=1, source_target_pairs={{0,32},{32,0},{1,33},{33,1},{2,34},{34,2},{3,35},{35,3},{4,36},{36... | collective-permute-start | bytes 1572872 | tf_op jit(solution)/shard_map/ppermute | solution.py:474
  69.5 3.6 %collective-permute-start.7 = (bf16[256,1024]{1,0:T(8,128)(2,1)S(1)}, bf16[256,1024]{1,0:T(8,128)(2,1)}, u32[]{:S(2)}, u32[]{:S(2)}) collective-permute-start(bf16[256,1024]{1,0:T(8,128)(2,1)S(1)} %collective-permute-done.3.refs_9_), channel_id=1, source_target_pairs={{0,32},{32,0},{1,33},{33,1},{2,34},{34,2},{3,35},{35,3},{4,36},{36... | collective-permute-start | bytes 1572872 | tf_op jit(solution)/shard_map/ppermute | solution.py:474
  72.3 0.8 copy-start
  85.9 8.2 %collective-permute-start.10 = (bf16[4,144,2048]{2,1,0:T(8,128)(2,1)}, bf16[4,144,2048]{2,1,0:T(8,128)(2,1)S(1)}, u32[]{:S(2)}, u32[]{:S(2)}) collective-permute-start(bf16[4,144,2048]{2,1,0:T(8,128)(2,1)} %get-tuple-element.39), channel_id=1, source_target_pairs={{0,32},{32,0},{1,33},{33,1},{2,34},{34,2},{3,35},{35,3},{4,36},{36... | collective-permute-start | bytes 7077896 | tf_op jit(solution)/shard_map/ppermute | solution.py:474
  86.0 28.2 %all-to-all-start.3 = ((bf16[32,64,128]{2,1,0:T(8,128)(2,1)}), bf16[32,64,128]{2,1,0:T(8,128)(2,1)S(1)}, u32[]{:S(2)}, u32[]{:S(2)}) async-start(bf16[32,64,128]{2,1,0:T(8,128)(2,1)} %get-tuple-element.36), calls=%async_computation.3 | async-start | bytes 1048576 | tf_op jit(solution)/shard_map/all_to_all | solution.py:482
  97.3 9.0 %collective-permute-start.11 = (bf16[144,1024]{1,0:T(8,128)(2,1)}, bf16[144,1024]{1,0:T(8,128)(2,1)S(1)}, u32[]{:S(2)}, u32[]{:S(2)}) collective-permute-start(bf16[144,1024]{1,0:T(8,128)(2,1)} %get-tuple-element.42), channel_id=1, source_target_pairs={{0,64},{64,128},{128,192},{192,0},{1,65},{65,129},{129,193},{193,1... | collective-permute-start | bytes 884744 | tf_op jit(solution)/shard_map/ppermute | solution.py:474
  98.4 9.9 %collective-permute-start.12 = (bf16[144,1024]{1,0:T(8,128)(2,1)}, bf16[144,1024]{1,0:T(8,128)(2,1)S(1)}, u32[]{:S(2)}, u32[]{:S(2)}) collective-permute-start(bf16[144,1024]{1,0:T(8,128)(2,1)} %get-tuple-element.43), channel_id=1, source_target_pairs={{0,192},{64,0},{128,64},{192,128},{1,193},{65,1},{129,65},{193,129... | collective-permute-start | bytes 884744 | tf_op jit(solution)/shard_map/ppermute | solution.py:474
  110.9 15.4 %collective-permute-start.14 = (bf16[144,2048]{1,0:T(8,128)(2,1)}, bf16[144,2048]{1,0:T(8,128)(2,1)S(1)}, u32[]{:S(2)}, u32[]{:S(2)}) collective-permute-start(bf16[144,2048]{1,0:T(8,128)(2,1)} %get-tuple-element.54), channel_id=1, source_target_pairs={{0,192},{64,0},{128,64},{192,128},{1,193},{65,1},{129,65},{193,129... | collective-permute-start | bytes 1769480 | tf_op jit(solution)/shard_map/ppermute | solution.py:474
  111.0 15.3 %collective-permute-start.13 = (bf16[144,2048]{1,0:T(8,128)(2,1)}, bf16[144,2048]{1,0:T(8,128)(2,1)S(1)}, u32[]{:S(2)}, u32[]{:S(2)}) collective-permute-start(bf16[144,2048]{1,0:T(8,128)(2,1)} %get-tuple-element.44.refs_2_), channel_id=1, source_target_pairs={{0,64},{64,128},{128,192},{192,0},{1,65},{65,129},{129,193},{193,1... | collective-permute-start | bytes 1769480 | tf_op jit(solution)/shard_map/ppermute | solution.py:474
  115.9 25.7 %all-to-all-start.4 = ((bf16[32,64,128]{2,1,0:T(8,128)(2,1)}), bf16[32,64,128]{2,1,0:T(8,128)(2,1)S(1)}, u32[]{:S(2)}, u32[]{:S(2)}) async-start(bf16[32,64,128]{2,1,0:T(8,128)(2,1)} %shard_map.142.refs_6_), calls=%async_computation.4 | async-start | bytes 1048576 | tf_op jit(solution)/shard_map/all_to_all | solution.py:482
  141.7 21.6 %all-to-all-start.5 = ((bf16[32,72,128]{2,1,0:T(8,128)(2,1)}), bf16[32,72,128]{2,1,0:T(8,128)(2,1)S(1)}, u32[]{:S(2)}, u32[]{:S(2)}) async-start(bf16[32,72,128]{2,1,0:T(8,128)(2,1)} %fusion.1), calls=%async_computation.5 | async-start | bytes 1179648 | tf_op jit(solution)/shard_map/all_to_all | solution.py:482

commit v5 on v4

--- a/solution.py
+++ b/solution.py
@@ -242,17 +242,25 @@
             flow.outgoing.copy(at, k).start()
 
 
-def add_kernel(flow, own_term, other_term, own_ref, right_ref, left_ref, forth_ref, back_ref):
-    for at, k in ((3, 2), (1, 1), (2, 3), (0, 0)):
+def opposite_kernel(flow, own_far, other_far, forth_ref, back_ref, own_term, other_term, sems):
+    pairs = ((own_far, own_term), (other_far, other_term))
+    copies = [pltpu.make_async_copy(far.at[2], near, sems.at[k]) for k, (far, near) in enumerate(pairs)]
+    for copy in copies:
+        copy.start()
+    for copy in copies:
+        copy.wait()
+    total = (own_term[...].astype(F32) + other_term[...].astype(F32)).astype(BF16)
+    forth_ref[...] = total[:, :D]
+    back_ref[...] = total[:, D:]
+    flow.leave()
+
+
+def add_kernel(flow, own_term, other_term, *outs):
+    for at, k in enumerate((0, 1, 3)):
         flow.arrive(k * STEP)
-        total = (own_term[k].astype(F32) + other_term[k].astype(F32)).astype(BF16)
-        if k == 2:
-            forth_ref[...] = total[:, :D]
-            back_ref[...] = total[:, D:]
-            flow.outgoing.copy(4).start()
-        else:
-            (own_ref, right_ref, left_ref)[at][...] = total
+        outs[at][...] = (own_term[k].astype(F32) + other_term[k].astype(F32)).astype(BF16)
         flow.outgoing.copy(at).start()
+    flow.arrive(2 * STEP)
 
 
 def relay_kernel(flow, right_in, left_in, forth_in, back_in, right_ref, left_ref):
@@ -533,8 +541,21 @@
     other_term = shift(other_term, "c", 1)
     block = shaped((W + GAINROWS, INNER), BF16)
     half = shaped((W + GAINROWS, D), BF16)
-    kept, right, left, forth, back = call(
-        add_kernel, [block, block, block, half, half], [own_term, other_term], us=3.7, loose=[other_term]
+    forth, back = call(
+        opposite_kernel,
+        [half, half],
+        [own_term, other_term],
+        scratch=[
+            pltpu.VMEM((W + GAINROWS, INNER), BF16),
+            pltpu.VMEM((W + GAINROWS, INNER), BF16),
+            pltpu.SemaphoreType.DMA((2,)),
+        ],
+        us=1.2,
+        loose=[other_term],
+        raw=[own_term, other_term],
+    )
+    kept, right, left = call(
+        add_kernel, [block] * 3, [own_term, other_term], us=2.5, loose=[other_term], after=[forth]
     )
     forth, back = shift(forth, "x", 1), shift(back, "x", -1)
     right, left = call(

time: 166 us -> 165 us (level)
  waiting for transfers between devices: 49.3 us -> 44.8 us
  Pallas kernels: 46.2 us -> 48 us
    ppermute x15, waiting for transfers between devices: 31 us -> 26.4 us  [shift(): lax.ppermute(value, axis, [(i, (i + by) % size) for i in range(size)])]
    pallas_call x11 -> x12, Pallas kernels: 46.2 us -> 48 us  [call(): pl.pallas_call(run, out_shape=[pltpu.HBM(out.shape, out.dtype) for out in...]
  transfers between devices with their start and end apart: 21 -> 21, of which waited for: 14 -> 13; matrix products, arithmetic and copies ran while one was open for 2% -> 2% of each run, Pallas kernels for 21% -> 22%
where the time goes in v5:
time: 165 us; the launch traced here: 163 us
  starting transfers between devices  62.8 us (38%)
  Pallas kernels  48 us (29%)
  waiting for transfers between devices  44.8 us (27%)
  local copies, waits for them, and re-layouts  5.46 us (3%)
    pallas_call x12, Pallas kernels, call(): pl.pallas_call(run, out_shape=[pltpu.HBM(out.shape, out.dtype) for out in...  48 us
    all_to_all x6, starting transfers between devices, exchange(): return lax.all_to_all(value, axes, 0, 0, tiled=True)  46.9 us
    ppermute x15, waiting for transfers between devices, shift(): lax.ppermute(value, axis, [(i, (i + by) % size) for i in range(size)])  26.4 us
    all_to_all x6, waiting for transfers between devices, exchange(): return lax.all_to_all(value, axes, 0, 0, tiled=True)  18.3 us
    ppermute x15, starting transfers between devices, shift(): lax.ppermute(value, axis, [(i, (i + by) % size) for i in range(size)])  15.9 us
  transfers between devices with their start and end apart: 21, of which 13 were waited for; matrix products, arithmetic and copies ran while one was open for 2% of the time, Pallas kernels for 22%

profile of v5, /device:TPU:38, one launch (start us, length us, event | category | flops | bytes accessed | tf_op | source)
XLA Modules:
  0.0 162.9 jit_solution(1086590567529118345)
XLA Ops:
  2.0 8.6 %all-to-all-start.2 = ((bf16[8,8,1024]{2,1,0:T(8,128)(2,1)}), bf16[8,8,1024]{2,1,0:T(8,128)(2,1)S(1)}, u32[]{:S(2)}, u32[]{:S(2)}) async-start(bf16[8,8,1024]{2,1,0:T(8,128)(2,1)} %broadcast_in_dim.22), calls=%async_computation.2 | async-start | bytes 262144 | tf_op jit(solution)/shard_map/all_to_all | solution.py:490
  10.6 4.9 %shard_map.135 = (bf16[32,80,128]{2,1,0:T(8,128)(2,1)}, f32[16,256]{1,0:T(8,128)}) custom-call(bf16[256,2048]{1,0:T(8,128)(2,1)} %bitcast.27, bf16[256,128]{1,0:T(8,128)(2,1)} %bitcast.36, f32[16,256]{1,0:T(8,128)} %bitcast.40), custom_call_target="tpu_custom_call" | custom-call | flops 110000000 | bytes 1802240 | tf_op jit(solution)/shard_map/pallas_call | solution.py:458
  15.5 2.5 %all-to-all-done.2 = bf16[8,8,1024]{2,1,0:T(8,128)(2,1)S(1)} async-done(((bf16[8,8,1024]{2,1,0:T(8,128)(2,1)}), bf16[8,8,1024]{2,1,0:T(8,128)(2,1)S(1)}, u32[]{:S(2)}, u32[]{:S(2)}) %all-to-all-start.2) | async-done | bytes 131104 | tf_op jit(solution)/shard_map/all_to_all | solution.py:490
  18.0 7.5 %all-to-all-start = ((bf16[32,80,128]{2,1,0:T(8,128)(2,1)}), bf16[32,80,128]{2,1,0:T(8,128)(2,1)S(1)}, u32[]{:S(2)}, u32[]{:S(2)}) async-start(bf16[32,80,128]{2,1,0:T(8,128)(2,1)} %get-tuple-element.33.refs_7_), calls=%async_computation | async-start | bytes 1310720 | tf_op jit(solution)/shard_map/all_to_all | solution.py:490
  25.5 2.8 %collective-permute-start.2 = (bf16[64,1024]{1,0:T(8,128)(2,1)S(1)}, bf16[64,1024]{1,0:T(8,128)(2,1)S(1)}, u32[]{:S(2)}, u32[]{:S(2)}) collective-permute-start(bf16[64,1024]{1,0:T(8,128)(2,1)S(1)} %bitcast.23), channel_id=1, source_target_pairs={{0,24},{8,0},{16,8},{24,16},{1,25},{9,1},{17,9},{25,17},{2,26},{10... | collective-permute-start | bytes 393224 | tf_op jit(solution)/shard_map/ppermute | solution.py:482
  30.0 4.5 %shard_map.136.refs_5_.refs_1_ = bf16[256,2048]{1,0:T(8,128)(2,1)} custom-call(bf16[256,2048]{1,0:T(8,128)(2,1)} %bitcast.28, bf16[256,128]{1,0:T(8,128)(2,1)} %bitcast.37, bf16[256,128]{1,0:T(8,128)(2,1)} %bitcast.33, f32[16,256]{1,0:T(8,128)} %get-tuple-element.32.refs_3_.refs_5_.refs_4_), custom_call_target="tpu_custom_call" | custom-call | flops 330000000 | bytes 2244608 | tf_op jit(solution)/shard_map/pallas_call | solution.py:458
  34.6 3.3 %collective-permute-done.2.refs_4_ = bf16[64,1024]{1,0:T(8,128)(2,1)S(1)} collective-permute-done((bf16[64,1024]{1,0:T(8,128)(2,1)S(1)}, bf16[64,1024]{1,0:T(8,128)(2,1)S(1)}, u32[]{:S(2)}, u32[]{:S(2)}) %collective-permute-start.2) | collective-permute-done | bytes 131104 | tf_op jit(solution)/shard_map/ppermute | solution.py:482
  38.4 2.5 %collective-permute-done.refs_2_ = bf16[64,1024]{1,0:T(8,128)(2,1)S(1)} collective-permute-done((bf16[64,1024]{1,0:T(8,128)(2,1)S(1)}, bf16[64,1024]{1,0:T(8,128)(2,1)S(1)}, u32[]{:S(2)}, u32[]{:S(2)}) %collective-permute-start) | collective-permute-done | bytes 131104 | tf_op jit(solution)/shard_map/ppermute | solution.py:482
  48.4 8.2 %all-to-all-start.1 = ((bf16[32,64,128]{2,1,0:T(8,128)(2,1)}), bf16[32,64,128]{2,1,0:T(8,128)(2,1)S(1)}, u32[]{:S(2)}, u32[]{:S(2)}) async-start(bf16[32,64,128]{2,1,0:T(8,128)(2,1)} %get-tuple-element.34), calls=%async_computation.1 | async-start | bytes 1048576 | tf_op jit(solution)/shard_map/all_to_all | solution.py:490
  56.6 12.2 %collective-permute-done.5.refs_11_ = bf16[256,1024]{1,0:T(8,128)(2,1)S(1)} collective-permute-done((bf16[256,1024]{1,0:T(8,128)(2,1)}, bf16[256,1024]{1,0:T(8,128)(2,1)S(1)}, u32[]{:S(2)}, u32[]{:S(2)}) %collective-permute-start.5) | collective-permute-done | bytes 524320 | tf_op jit(solution)/shard_map/ppermute | solution.py:482
  73.5 12.5 %shard_map.139 = (bf16[256,2048]{1,0:T(8,128)(2,1)}, bf16[256,2048]{1,0:T(8,128)(2,1)}, bf16[32,64,128]{2,1,0:T(8,128)(2,1)}, f32[256,128]{1,0:T(8,128)}, bf16[4...) custom-call(s32[3]{0:T(128)S(1)} %pad_add_fusion.refs_0_, bf16[256,2048]{1,0:T(8,128)(2,1)} %shard_map.136.refs_5_.refs_1_, ...), custom_call_target="tpu_custom_call" | custom-call | flops 1430000000 | bytes 14901248 | tf_op jit(solution)/shard_map/pallas_call | solution.py:458
  86.1 8.0 %all-to-all-start.3 = ((bf16[32,64,128]{2,1,0:T(8,128)(2,1)}), bf16[32,64,128]{2,1,0:T(8,128)(2,1)S(1)}, u32[]{:S(2)}, u32[]{:S(2)}) async-start(bf16[32,64,128]{2,1,0:T(8,128)(2,1)} %get-tuple-element.36), calls=%async_computation.3 | async-start | bytes 1048576 | tf_op jit(solution)/shard_map/all_to_all | solution.py:490
  96.3 3.2 %collective-permute-start.11 = (bf16[144,1024]{1,0:T(8,128)(2,1)}, bf16[144,1024]{1,0:T(8,128)(2,1)S(1)}, u32[]{:S(2)}, u32[]{:S(2)}) collective-permute-start(bf16[144,1024]{1,0:T(8,128)(2,1)} %get-tuple-element.40.refs_2_), channel_id=1, source_target_pairs={{0,64},{64,128},{128,192},{192,0},{1,65},{65,129},{129,193},{193,1... | collective-permute-start | bytes 884744 | tf_op jit(solution)/shard_map/ppermute | solution.py:482
  99.5 2.8 %shard_map.141 = (bf16[144,2048]{1,0:T(8,128)(2,1)}, bf16[144,2048]{1,0:T(8,128)(2,1)}, bf16[144,2048]{1,0:T(8,128)(2,1)}) custom-call(bf16[4,144,2048]{2,1,0:T(8,128)(2,1)} %get-tuple-element.38.refs_0_, bf16[4,144,2048]{2,1,0:T(8,128)(2,1)S(1)} %collective-permute-done.10.refs_1_, bf16[144,1024]{1,0:T(8,128)(2,1)} %get-tuple-element.40.refs_2_), custom_call_target="tpu_custom_call" | custom-call | flops 2750000128 | bytes 6488064 | tf_op jit(solution)/shard_map/pallas_call | solution.py:458
  102.4 4.1 %collective-permute-done.12.refs_3_ = bf16[144,1024]{1,0:T(8,128)(2,1)S(1)} collective-permute-done((bf16[144,1024]{1,0:T(8,128)(2,1)}, bf16[144,1024]{1,0:T(8,128)(2,1)S(1)}, u32[]{:S(2)}, u32[]{:S(2)}) %collective-permute-start.12) | collective-permute-done | bytes 294944 | tf_op jit(solution)/shard_map/ppermute | solution.py:482
  106.4 2.6 %shard_map.142 = (bf16[144,2048]{1,0:T(8,128)(2,1)}, bf16[144,2048]{1,0:T(8,128)(2,1)}) custom-call(bf16[144,2048]{1,0:T(8,128)(2,1)} %get-tuple-element.41.refs_0_, bf16[144,2048]{1,0:T(8,128)(2,1)} %get-tuple-element.42.refs_1_, bf16[144,1024]{1,0:T(8,128)(2,1)S(1)} %collective-permute-done.11.refs_2_, bf16[144,1024]{1,0:T(8,128)(2,1)S(1)} %collective-permute-done.12.refs_3_), custom_call_target="tpu_custom_call" | custom-call | flops 3080000000 | bytes 2949120 | tf_op jit(solution)/shard_map/pallas_call | solution.py:458
  109.1 3.2 %collective-permute-start.13 = (bf16[144,2048]{1,0:T(8,128)(2,1)}, bf16[144,2048]{1,0:T(8,128)(2,1)S(1)}, u32[]{:S(2)}, u32[]{:S(2)}) collective-permute-start(bf16[144,2048]{1,0:T(8,128)(2,1)} %get-tuple-element.44.refs_2_), channel_id=1, source_target_pairs={{0,64},{64,128},{128,192},{192,0},{1,65},{65,129},{129,193},{193,1... | collective-permute-start | bytes 1769480 | tf_op jit(solution)/shard_map/ppermute | solution.py:482
  114.0 9.8 %all-to-all-start.4 = ((bf16[32,64,128]{2,1,0:T(8,128)(2,1)}), bf16[32,64,128]{2,1,0:T(8,128)(2,1)S(1)}, u32[]{:S(2)}, u32[]{:S(2)}) async-start(bf16[32,64,128]{2,1,0:T(8,128)(2,1)} %shard_map.143.refs_6_), calls=%async_computation.4 | async-start | bytes 1048576 | tf_op jit(solution)/shard_map/all_to_all | solution.py:490
  124.7 2.2 %shard_map.146 = (bf16[128,2048]{1,0:T(8,128)(2,1)}, f32[8,256]{1,0:T(8,128)}) custom-call(bf16[144,2048]{1,0:T(8,128)(2,1)} %get-tuple-element.53.refs_0_, bf16[144,2048]{1,0:T(8,128)(2,1)S(1)} %collective-permute-done.13.refs_1_, bf16[144,2048]{1,0:T(8,128)(2,1)S(1)} %collective-permute-done.14.refs_2_), custom_call_target="tpu_custom_call" | custom-call | flops 2860000000 | bytes 2301952 | tf_op jit(solution)/shard_map/pallas_call | solution.py:458
  129.9 10.1 %all-to-all-done.4.refs_1_ = bf16[32,64,128]{2,1,0:T(8,128)(2,1)S(1)} async-done(((bf16[32,64,128]{2,1,0:T(8,128)(2,1)}), bf16[32,64,128]{2,1,0:T(8,128)(2,1)S(1)}, u32[]{:S(2)}, u32[]{:S(2)}) %all-to-all-start.4) | async-done | bytes 524320 | tf_op jit(solution)/shard_map/all_to_all | solution.py:490
  140.0 4.8 %all-to-all-start.5 = ((bf16[32,72,128]{2,1,0:T(8,128)(2,1)}), bf16[32,72,128]{2,1,0:T(8,128)(2,1)S(1)}, u32[]{:S(2)}, u32[]{:S(2)}) async-start(bf16[32,72,128]{2,1,0:T(8,128)(2,1)} %fusion.1), calls=%async_computation.5 | async-start | bytes 1179648 | tf_op jit(solution)/shard_map/all_to_all | solution.py:490
  144.8 5.7 %shard_map.144 = (f32[256,2048]{1,0:T(8,128)}, bf16[256,128]{1,0:T(8,128)(2,1)}, f32[256,128]{1,0:T(8,128)}) custom-call(bf16[256,2048]{1,0:T(8,128)(2,1)} %bitcast.29, bf16[256,2048]{1,0:T(8,128)(2,1)} %get-tuple-element.35.refs_1_, bf16[256,128]{1,0:T(8,128)(2,1)} %bitcast.38, bf16[256,128]{1,0:T(8,128)(2,1)} %bitcast.35, ...), custom_call_target="tpu_custom_call" | custom-call | flops 6380000256 | bytes 5062656 | tf_op jit(solution)/shard_map/pallas_call | solution.py:458
  150.5 5.7 %shard_map.145 = (bf16[256,2048]{1,0:T(8,128)(2,1)}, bf16[256,128]{1,0:T(8,128)(2,1)}, f32[16,256]{1,0:T(8,128)}) custom-call(f32[256,2048]{1,0:T(8,128)} %get-tuple-element.45.refs_0_, bf16[32,64,128]{2,1,0:T(8,128)(2,1)S(1)} %all-to-all-done.4.refs_1_, bf16[256,128]{1,0:T(8,128)(2,1)} %bitcast.39, bf16[256,2048]{1,0:T(8,128)(2,1)} %bitcast.30, ...), custom_call_target="tpu_custom_call" | custom-call | flops 6049999872 | bytes 6324224 | tf_op jit(solution)/shard_map/pallas_call | solution.py:458
  156.2 5.4 %all-to-all-done.5 = bf16[32,72,128]{2,1,0:T(8,128)(2,1)S(1)} async-done(((bf16[32,72,128]{2,1,0:T(8,128)(2,1)}), bf16[32,72,128]{2,1,0:T(8,128)(2,1)S(1)}, u32[]{:S(2)}, u32[]{:S(2)}) %all-to-all-start.5) | async-done | bytes 589856 | tf_op jit(solution)/shard_map/all_to_all | solution.py:490
  (42 shorter events, 24.9 us)
Async XLA Ops:
  2.0 16.0 %all-to-all-start.2 = ((bf16[8,8,1024]{2,1,0:T(8,128)(2,1)}), bf16[8,8,1024]{2,1,0:T(8,128)(2,1)S(1)}, u32[]{:S(2)}, u32[]{:S(2)}) async-start(bf16[8,8,1024]{2,1,0:T(8,128)(2,1)} %broadcast_in_dim.22), calls=%async_computation.2 | async-start | bytes 262144 | tf_op jit(solution)/shard_map/all_to_all | solution.py:490
  18.0 28.5 %all-to-all-start = ((bf16[32,80,128]{2,1,0:T(8,128)(2,1)}), bf16[32,80,128]{2,1,0:T(8,128)(2,1)S(1)}, u32[]{:S(2)}, u32[]{:S(2)}) async-start(bf16[32,80,128]{2,1,0:T(8,128)(2,1)} %get-tuple-element.33.refs_7_), calls=%async_computation | async-start | bytes 1310720 | tf_op jit(solution)/shard_map/all_to_all | solution.py:490
  25.5 12.4 %collective-permute-start.2 = (bf16[64,1024]{1,0:T(8,128)(2,1)S(1)}, bf16[64,1024]{1,0:T(8,128)(2,1)S(1)}, u32[]{:S(2)}, u32[]{:S(2)}) collective-permute-start(bf16[64,1024]{1,0:T(8,128)(2,1)S(1)} %bitcast.23), channel_id=1, source_target_pairs={{0,24},{8,0},{16,8},{24,16},{1,25},{9,1},{17,9},{25,17},{2,26},{10... | collective-permute-start | bytes 393224 | tf_op jit(solution)/shard_map/ppermute | solution.py:482
  28.3 10.0 %collective-permute-start.1 = (bf16[64,1024]{1,0:T(8,128)(2,1)S(1)}, bf16[64,1024]{1,0:T(8,128)(2,1)S(1)}, u32[]{:S(2)}, u32[]{:S(2)}) collective-permute-start(bf16[64,1024]{1,0:T(8,128)(2,1)S(1)} %bitcast.24), channel_id=1, source_target_pairs={{0,16},{8,24},{16,0},{24,8},{1,17},{9,25},{17,1},{25,9},{2,18},{10... | collective-permute-start | bytes 393224 | tf_op jit(solution)/shard_map/ppermute | solution.py:482
  29.2 11.7 %collective-permute-start = (bf16[64,1024]{1,0:T(8,128)(2,1)S(1)}, bf16[64,1024]{1,0:T(8,128)(2,1)S(1)}, u32[]{:S(2)}, u32[]{:S(2)}) collective-permute-start(bf16[64,1024]{1,0:T(8,128)(2,1)S(1)} %bitcast.25), channel_id=1, source_target_pairs={{0,8},{8,16},{16,24},{24,0},{1,9},{9,17},{17,25},{25,1},{2,10},{10... | collective-permute-start | bytes 393224 | tf_op jit(solution)/shard_map/ppermute | solution.py:482
  42.4 26.5 %collective-permute-start.5 = (bf16[256,1024]{1,0:T(8,128)(2,1)}, bf16[256,1024]{1,0:T(8,128)(2,1)S(1)}, u32[]{:S(2)}, u32[]{:S(2)}) collective-permute-start(bf16[256,1024]{1,0:T(8,128)(2,1)} %shard_map.138.refs_8_), channel_id=1, source_target_pairs={{0,192},{64,0},{128,64},{192,128},{1,193},{65,1},{129,65},{193,129... | collective-permute-start | bytes 1572872 | tf_op jit(solution)/shard_map/ppermute | solution.py:482
  43.3 25.6 %collective-permute-start.4 = (bf16[256,1024]{1,0:T(8,128)(2,1)}, bf16[256,1024]{1,0:T(8,128)(2,1)S(1)}, u32[]{:S(2)}, u32[]{:S(2)}) collective-permute-start(bf16[256,1024]{1,0:T(8,128)(2,1)} %shard_map.138.refs_8_), channel_id=1, source_target_pairs={{0,128},{64,192},{128,0},{192,64},{1,129},{65,193},{129,1},{193,65... | collective-permute-start | bytes 1572872 | tf_op jit(solution)/shard_map/ppermute | solution.py:482
  44.4 25.1 %collective-permute-start.3 = (bf16[256,1024]{1,0:T(8,128)(2,1)}, bf16[256,1024]{1,0:T(8,128)(2,1)S(1)}, u32[]{:S(2)}, u32[]{:S(2)}) collective-permute-start(bf16[256,1024]{1,0:T(8,128)(2,1)} %shard_map.138.refs_8_), channel_id=1, source_target_pairs={{0,64},{64,128},{128,192},{192,0},{1,65},{65,129},{129,193},{193,1... | collective-permute-start | bytes 1572872 | tf_op jit(solution)/shard_map/ppermute | solution.py:482
  48.4 25.1 %all-to-all-start.1 = ((bf16[32,64,128]{2,1,0:T(8,128)(2,1)}), bf16[32,64,128]{2,1,0:T(8,128)(2,1)S(1)}, u32[]{:S(2)}, u32[]{:S(2)}) async-start(bf16[32,64,128]{2,1,0:T(8,128)(2,1)} %get-tuple-element.34), calls=%async_computation.1 | async-start | bytes 1048576 | tf_op jit(solution)/shard_map/all_to_all | solution.py:490
  56.5 13.0 %collective-permute-start.6 = (bf16[256,1024]{1,0:T(8,128)(2,1)}, bf16[256,1024]{1,0:T(8,128)(2,1)S(1)}, u32[]{:S(2)}, u32[]{:S(2)}) collective-permute-start(bf16[256,1024]{1,0:T(8,128)(2,1)} %shard_map.138.refs_8_), channel_id=1, source_target_pairs={{0,32},{32,0},{1,33},{33,1},{2,34},{34,2},{3,35},{35,3},{4,36},{36... | collective-permute-start | bytes 1572872 | tf_op jit(solution)/shard_map/ppermute | solution.py:482
  68.9 1.9 %collective-permute-start.9 = (bf16[256,1024]{1,0:T(8,128)(2,1)S(1)}, bf16[256,1024]{1,0:T(8,128)(2,1)S(1)}, u32[]{:S(2)}, u32[]{:S(2)}) collective-permute-start(bf16[256,1024]{1,0:T(8,128)(2,1)S(1)} %collective-permute-done.5.refs_11_), channel_id=1, source_target_pairs={{0,32},{32,0},{1,33},{33,1},{2,34},{34,2},{3,35},{35,3},{4,36},{36... | collective-permute-start | bytes 1572872 | tf_op jit(solution)/shard_map/ppermute | solution.py:482
  68.9 3.4 %collective-permute-start.8 = (bf16[256,1024]{1,0:T(8,128)(2,1)S(1)}, bf16[256,1024]{1,0:T(8,128)(2,1)S(1)}, u32[]{:S(2)}, u32[]{:S(2)}) collective-permute-start(bf16[256,1024]{1,0:T(8,128)(2,1)S(1)} %collective-permute-done.4.refs_10_), channel_id=1, source_target_pairs={{0,32},{32,0},{1,33},{33,1},{2,34},{34,2},{3,35},{35,3},{4,36},{36... | collective-permute-start | bytes 1572872 | tf_op jit(solution)/shard_map/ppermute | solution.py:482
  69.5 3.6 %collective-permute-start.7 = (bf16[256,1024]{1,0:T(8,128)(2,1)S(1)}, bf16[256,1024]{1,0:T(8,128)(2,1)}, u32[]{:S(2)}, u32[]{:S(2)}) collective-permute-start(bf16[256,1024]{1,0:T(8,128)(2,1)S(1)} %collective-permute-done.3.refs_9_), channel_id=1, source_target_pairs={{0,32},{32,0},{1,33},{33,1},{2,34},{34,2},{3,35},{35,3},{4,36},{36... | collective-permute-start | bytes 1572872 | tf_op jit(solution)/shard_map/ppermute | solution.py:482
  72.3 0.8 copy-start
  86.0 8.1 %collective-permute-start.10 = (bf16[4,144,2048]{2,1,0:T(8,128)(2,1)}, bf16[4,144,2048]{2,1,0:T(8,128)(2,1)S(1)}, u32[]{:S(2)}, u32[]{:S(2)}) collective-permute-start(bf16[4,144,2048]{2,1,0:T(8,128)(2,1)} %get-tuple-element.39), channel_id=1, source_target_pairs={{0,32},{32,0},{1,33},{33,1},{2,34},{34,2},{3,35},{35,3},{4,36},{36... | collective-permute-start | bytes 7077896 | tf_op jit(solution)/shard_map/ppermute | solution.py:482
  86.1 26.2 %all-to-all-start.3 = ((bf16[32,64,128]{2,1,0:T(8,128)(2,1)}), bf16[32,64,128]{2,1,0:T(8,128)(2,1)S(1)}, u32[]{:S(2)}, u32[]{:S(2)}) async-start(bf16[32,64,128]{2,1,0:T(8,128)(2,1)} %get-tuple-element.36), calls=%async_computation.3 | async-start | bytes 1048576 | tf_op jit(solution)/shard_map/all_to_all | solution.py:490
  96.2 10.2 %collective-permute-start.12 = (bf16[144,1024]{1,0:T(8,128)(2,1)}, bf16[144,1024]{1,0:T(8,128)(2,1)S(1)}, u32[]{:S(2)}, u32[]{:S(2)}) collective-permute-start(bf16[144,1024]{1,0:T(8,128)(2,1)} %get-tuple-element.43), channel_id=1, source_target_pairs={{0,192},{64,0},{128,64},{192,128},{1,193},{65,1},{129,65},{193,129... | collective-permute-start | bytes 884744 | tf_op jit(solution)/shard_map/ppermute | solution.py:482
  96.3 10.1 %collective-permute-start.11 = (bf16[144,1024]{1,0:T(8,128)(2,1)}, bf16[144,1024]{1,0:T(8,128)(2,1)S(1)}, u32[]{:S(2)}, u32[]{:S(2)}) collective-permute-start(bf16[144,1024]{1,0:T(8,128)(2,1)} %get-tuple-element.40.refs_2_), channel_id=1, source_target_pairs={{0,64},{64,128},{128,192},{192,0},{1,65},{65,129},{129,193},{193,1... | collective-permute-start | bytes 884744 | tf_op jit(solution)/shard_map/ppermute | solution.py:482
  109.0 15.7 %collective-permute-start.14 = (bf16[144,2048]{1,0:T(8,128)(2,1)}, bf16[144,2048]{1,0:T(8,128)(2,1)S(1)}, u32[]{:S(2)}, u32[]{:S(2)}) collective-permute-start(bf16[144,2048]{1,0:T(8,128)(2,1)} %get-tuple-element.54), channel_id=1, source_target_pairs={{0,192},{64,0},{128,64},{192,128},{1,193},{65,1},{129,65},{193,129... | collective-permute-start | bytes 1769480 | tf_op jit(solution)/shard_map/ppermute | solution.py:482
  109.1 15.6 %collective-permute-start.13 = (bf16[144,2048]{1,0:T(8,128)(2,1)}, bf16[144,2048]{1,0:T(8,128)(2,1)S(1)}, u32[]{:S(2)}, u32[]{:S(2)}) collective-permute-start(bf16[144,2048]{1,0:T(8,128)(2,1)} %get-tuple-element.44.refs_2_), channel_id=1, source_target_pairs={{0,64},{64,128},{128,192},{192,0},{1,65},{65,129},{129,193},{193,1... | collective-permute-start | bytes 1769480 | tf_op jit(solution)/shard_map/ppermute | solution.py:482
  114.0 26.0 %all-to-all-start.4 = ((bf16[32,64,128]{2,1,0:T(8,128)(2,1)}), bf16[32,64,128]{2,1,0:T(8,128)(2,1)S(1)}, u32[]{:S(2)}, u32[]{:S(2)}) async-start(bf16[32,64,128]{2,1,0:T(8,128)(2,1)} %shard_map.143.refs_6_), calls=%async_computation.4 | async-start | bytes 1048576 | tf_op jit(solution)/shard_map/all_to_all | solution.py:490
  140.0 21.6 %all-to-all-start.5 = ((bf16[32,72,128]{2,1,0:T(8,128)(2,1)}), bf16[32,72,128]{2,1,0:T(8,128)(2,1)S(1)}, u32[]{:S(2)}, u32[]{:S(2)}) async-start(bf16[32,72,128]{2,1,0:T(8,128)(2,1)} %fusion.1), calls=%async_computation.5 | async-start | bytes 1179648 | tf_op jit(solution)/shard_map/all_to_all | solution.py:490
